TPU v7x, 128 devices: a whole 4x4x4 slice. The times are simulated.
128 devices in a mesh: face: 32 (over x, z_hi, y), sub: 4 (over z_lo, core).
Axes of the slice: x: 4, y: 4, z: 4 (z_hi: 2, z_lo: 2; z = z_hi * 2 + z_lo), core: 2. Of those that a mesh axis runs over, the one named last changes fastest.
Arguments:
- pixel_state: bfloat16 [1048576, 256], P(('face', 'sub')), may hold values from -6 to 6
- norm1_gain: float32 [256], replicated, may hold values from 0.1 to 1.9
- w_qkv: bfloat16 [256, 768], replicated, may hold values from -1 to 1
- w_out: bfloat16 [256, 256], replicated, may hold values from -0.375 to 0.375
- shift_offsets: int32 [16384], P(('face', 'sub')), may hold values from 0 to 63
- seam_table: int32 [16384, 8], P(('face', 'sub')), may hold values from 0 to 4095
Outputs:
- layer_out: bfloat16 [1048576, 256], P(('face', 'sub'))
Inputs may be any that keep to these rules, and one draw needn't show every extreme that they name: `shift_offsets`: offset within each window that splits its shifted keys between itself and its partner. `seam_table`: index t of a seam neighbour window among the 4096 windows that share the block's low index s.
All inputs are finite; a program needn't handle non-finite values.
Results may differ from a plain program's by a relative error of at most 0.0051.
Values may be sent and summed in bfloat16 or wider, within the bound.
No kernel may reach another device: no remote copies, remote signals or barrier semaphores. Data moves between devices by JAX's collectives and lax.ppermute only.
A program may use at most 128 MiB of HBM per device.

v0:
```python
import functools
import math

import jax
import jax.numpy as jnp
from jax import lax
from jax.experimental import pallas as pl
from jax.experimental.pallas import tpu as pltpu
from jax.sharding import PartitionSpec as P

HEADS = 8
HALF = HEADS // 2
DIM = 32
C = 256
WIN = 64
SEAM = 8
EPS = 1e-05
SCALE = math.log2(math.e) / math.sqrt(DIM)
BF = jnp.bfloat16
F32 = jnp.float32
LOW = 2.0 ** -60
HIGH = 2.0 ** 60
NEG = -1e30
MB = 1024 * 1024


def params(limit):
    return pltpu.CompilerParams(vmem_limit_bytes=limit * MB)


def exp2(x):
    return jnp.exp2(x)


def dot(a, b):
    return jnp.dot(a, b, preferred_element_type=F32)


def dot_nt(a, b):
    return lax.dot_general(a, b, (((1,), (1,)), ((), ())), preferred_element_type=F32)


def norm_rows(x, gain):
    centre = jnp.mean(x, axis=-1, keepdims=True)
    x = x - centre
    spread = jnp.mean(x * x, axis=-1, keepdims=True)
    return (x * lax.rsqrt(spread + EPS) * gain).astype(BF)


def first_body(x_ref, gain_ref, wq_ref, q_ref, pooled_ref):
    rows = x_ref.shape[0]
    normed = norm_rows(x_ref[...].astype(F32), gain_ref[...])
    q_ref[...] = (dot(normed, wq_ref[...]) * SCALE).astype(BF)
    count = rows // WIN
    row = lax.broadcasted_iota(jnp.int32, (count, rows), 1) // WIN
    pick = jnp.where(row == lax.broadcasted_iota(jnp.int32, (count, rows), 0), 1.0, 0.0).astype(BF)
    pooled_ref[...] = (dot(pick, normed) * (1.0 / math.sqrt(WIN))).astype(BF)


def first(x, gain, wq, rows=1024):
    pixels = x.shape[0]
    return pl.pallas_call(
        first_body,
        grid=(pixels // rows,),
        in_specs=[
            pl.BlockSpec((rows, C), lambda i: (i, 0)),
            pl.BlockSpec((1, C), lambda i: (0, 0)),
            pl.BlockSpec((C, C), lambda i: (0, 0)),
        ],
        out_specs=[
            pl.BlockSpec((rows, C), lambda i: (i, 0)),
            pl.BlockSpec((rows // WIN, C), lambda i: (i, 0)),
        ],
        out_shape=[
            jax.ShapeDtypeStruct((pixels, C), BF),
            jax.ShapeDtypeStruct((pixels // WIN, C), BF),
        ],
        compiler_params=params(48),
        cost_estimate=pl.CostEstimate(flops=2 * pixels * C * C, bytes_accessed=4 * pixels * C, transcendentals=0),
        name="norm_queries_pool",
    )(x, gain, wq)


def group_body(g_ref, wk_ref, wv_ref, kt_ref, vo_ref):
    count = g_ref.shape[0]
    g = g_ref[...]
    kt = lax.dot_general(wk_ref[...], g, (((0,), (1,)), ((), ())), preferred_element_type=F32)
    v = dot(g, wv_ref[...])
    feat = lax.broadcasted_iota(jnp.int32, (128, count), 0) // DIM
    lane = lax.broadcasted_iota(jnp.int32, (count, 128), 1) // DIM
    for h in range(HEADS):
        lo = (h // HALF) * 128
        kt_ref[h] = jnp.where(feat == h % HALF, kt[lo:lo + 128], 0.0).astype(BF)
        mine = lane == h % HALF
        vo_ref[h, :, 0:128] = jnp.where(mine, v[:, lo:lo + 128], 0.0).astype(BF)
        vo_ref[h, :, 128:256] = jnp.where(mine, 1.0, 0.0).astype(BF)


def group(g, wk, wv):
    count = g.shape[0]
    return pl.pallas_call(
        group_body,
        out_shape=[
            jax.ShapeDtypeStruct((HEADS, 128, count), BF),
            jax.ShapeDtypeStruct((HEADS, count, C), BF),
        ],
        compiler_params=params(32),
        name="group_keys_values",
    )(g, wk, wv)


def coarse_body(q_ref, kt_ref, vo_ref, acc_ref):
    for half in range(2):
        q = q_ref[:, half * 128:half * 128 + 128]
        total = None
        for k in range(HALF):
            h = half * HALF + k
            weights = exp2(dot(q, kt_ref[h])).astype(BF)
            part = dot(weights, vo_ref[h])
            total = part if total is None else total + part
        acc_ref[:, half * C:half * C + C] = total


def coarse(q, kt, vo, rows=512):
    pixels = q.shape[0]
    count = kt.shape[2]
    return pl.pallas_call(
        coarse_body,
        grid=(pixels // rows,),
        in_specs=[
            pl.BlockSpec((rows, C), lambda i: (i, 0)),
            pl.BlockSpec((HEADS, 128, count), lambda i: (0, 0, 0)),
            pl.BlockSpec((HEADS, count, C), lambda i: (0, 0, 0)),
        ],
        out_specs=pl.BlockSpec((rows, 2 * C), lambda i: (i, 0)),
        out_shape=jax.ShapeDtypeStruct((pixels, 2 * C), F32),
        compiler_params=params(56),
        cost_estimate=pl.CostEstimate(
            flops=4 * pixels * HEADS * count * C, bytes_accessed=10 * pixels * C, transcendentals=pixels * HEADS * count
        ),
        name="group_attention",
    )(q, kt, vo)


def seam_body(index_ref, pool_ref, out_ref):
    rows = index_ref.shape[0]
    step = 1024
    total = jnp.zeros((rows, C), F32)
    for lo in range(0, pool_ref.shape[0], step):
        at = lax.broadcasted_iota(jnp.int32, (rows, step), 1) + lo
        pick = jnp.where(at == index_ref[...], 1.0, 0.0).astype(BF)
        total = total + dot(pick, pool_ref[lo:lo + step])
    out_ref[...] = total.astype(BF)


def seam(index, pool, rows=256):
    count = index.shape[0]
    return pl.pallas_call(
        seam_body,
        grid=(count // rows,),
        in_specs=[
            pl.BlockSpec((rows, 1), lambda i: (i, 0)),
            pl.BlockSpec(pool.shape, lambda i: (0, 0)),
        ],
        out_specs=pl.BlockSpec((rows, C), lambda i: (i, 0)),
        out_shape=jax.ShapeDtypeStruct((count, C), BF),
        compiler_params=params(48),
        name="seam_rows",
    )(index, pool)


def window_body(
    offset_ref, x_ref, part_ref, q_ref, acc_ref, seam_ref, gain_ref, wk_ref, wv_ref, wo_ref, kt_ref, vo_ref,
    out_ref, kbd, vbd, ksm, vsm, sums,
):
    rows = x_ref.shape[0]
    count = rows // WIN
    step = pl.program_id(0)
    head_of_lane = lax.broadcasted_iota(jnp.int32, (1, 128), 1) // DIM
    position = lax.broadcasted_iota(jnp.int32, (WIN, 1), 0)

    @pl.when(step == 0)
    def _():
        for w in range(count):
            for half in range(2):
                for k in range(HALF):
                    ones = jnp.where(head_of_lane == k, 1.0, 0.0).astype(BF)
                    vbd[w, half, k * WIN:k * WIN + WIN, 128:256] = jnp.broadcast_to(ones, (WIN, 128))
        for half in range(2):
            for k in range(HALF):
                ones = jnp.where(head_of_lane == k, 1.0, 0.0).astype(BF)
                vsm[half, k * 32:k * 32 + 32, 128:256] = jnp.broadcast_to(ones, (32, 128))

    x = x_ref[...].astype(F32)
    other = part_ref[...].astype(F32)
    chosen = []
    for w in range(count):
        offset = offset_ref[step * count + w]
        at = slice(w * WIN, w * WIN + WIN)
        chosen.append(jnp.where(position >= offset, x[at], other[at]))
    normed = norm_rows(jnp.concatenate(chosen, axis=0), gain_ref[...])
    keys = dot(normed, wk_ref[...]).astype(BF)
    values = dot(normed, wv_ref[...]).astype(BF)
    seam_k = dot(seam_ref[...], wk_ref[...]).astype(BF)
    seam_v = dot(seam_ref[...], wv_ref[...]).astype(BF)
    zero = jnp.zeros((), BF)
    for half in range(2):
        lo = half * 128
        for k in range(HALF):
            mine = head_of_lane == k
            at = slice(k * 32, k * 32 + 32)
            ksm[half, at, :] = jnp.where(mine, seam_k[:, lo:lo + 128], zero)
            vsm[half, at, 0:128] = jnp.where(mine, seam_v[:, lo:lo + 128], zero)
            for w in range(count):
                rows_w = slice(w * WIN, w * WIN + WIN)
                to = slice(k * WIN, k * WIN + WIN)
                kbd[w, half, to, :] = jnp.where(mine, keys[rows_w, lo:lo + 128], zero)
                vbd[w, half, to, 0:128] = jnp.where(mine, values[rows_w, lo:lo + 128], zero)

    own = (lax.broadcasted_iota(jnp.int32, (rows, 128), 1) % 32) // SEAM == lax.broadcasted_iota(
        jnp.int32, (rows, 128), 0
    ) // WIN

    def window_scores(w, half):
        q = q_ref[w * WIN:w * WIN + WIN, half * 128:half * 128 + 128]
        return dot_nt(q, kbd[w, half])

    def seam_scores(half):
        return dot_nt(q_ref[:, half * 128:half * 128 + 128], ksm[half])

    for half in range(2):
        at = slice(half * C, half * C + C)
        seam_w = jnp.where(own, exp2(seam_scores(half)), 0.0).astype(BF)
        base = acc_ref[:, at] + dot(seam_w, vsm[half])
        for w in range(count):
            weights = exp2(window_scores(w, half)).astype(BF)
            rows_w = slice(w * WIN, w * WIN + WIN)
            sums[rows_w, at] = base[rows_w] + dot(weights, vbd[w, half])

    den = jnp.concatenate([sums[:, 128:256], sums[:, 384:512]], axis=1)
    fine = jnp.where((den >= LOW) & (den <= HIGH), 0.0, 1.0)
    bad = jnp.max(fine)

    @pl.when(bad > 0.0)
    def _():
        for half in range(2):
            at = slice(half * C, half * C + C)
            q = q_ref[:, half * 128:half * 128 + 128]
            scores_s = jnp.where(own, seam_scores(half), NEG)
            scores_w = jnp.concatenate([window_scores(w, half) for w in range(count)], axis=0)
            head_s = lax.broadcasted_iota(jnp.int32, (rows, 128), 1) // 32
            head_w = lax.broadcasted_iota(jnp.int32, (rows, C), 1) // WIN
            tops_s = jnp.zeros((rows, 128), F32)
            tops_w = jnp.zeros((rows, C), F32)
            total = jnp.zeros((rows, C), F32)
            for k in range(HALF):
                h = half * HALF + k
                scores_g = dot(q, kt_ref[h])
                top = jnp.max(scores_g, axis=1, keepdims=True)
                top = jnp.maximum(top, jnp.max(jnp.where(head_s == k, scores_s, NEG), axis=1, keepdims=True))
                top = jnp.maximum(top, jnp.max(jnp.where(head_w == k, scores_w, NEG), axis=1, keepdims=True))
                tops_s = jnp.where(head_s == k, top, tops_s)
                tops_w = jnp.where(head_w == k, top, tops_w)
                total = total + dot(exp2(scores_g - top).astype(BF), vo_ref[h])
            total = total + dot(jnp.where(own, exp2(scores_s - tops_s), 0.0).astype(BF), vsm[half])
            weights = exp2(scores_w - tops_w).astype(BF)
            for w in range(count):
                rows_w = slice(w * WIN, w * WIN + WIN)
                sums[rows_w, at] = total[rows_w] + dot(weights[rows_w], vbd[w, half])

    attended = jnp.concatenate(
        [sums[:, 0:128] / sums[:, 128:256], sums[:, 256:384] / sums[:, 384:512]], axis=1
    ).astype(BF)
    out_ref[...] = (x + dot(attended, wo_ref[...])).astype(BF)


def window(offsets, x, part, q, acc, seam_rows, gain, wk, wv, wo, kt, vo, rows=256):
    pixels = x.shape[0]
    count = rows // WIN
    row = lambda i, s: (i, 0)
    fixed = lambda i, s: (0, 0)
    fixed3 = lambda i, s: (0, 0, 0)
    return pl.pallas_call(
        window_body,
        grid_spec=pltpu.PrefetchScalarGridSpec(
            num_scalar_prefetch=1,
            grid=(pixels // rows,),
            in_specs=[
                pl.BlockSpec((rows, C), row),
                pl.BlockSpec((rows, C), row),
                pl.BlockSpec((rows, C), row),
                pl.BlockSpec((rows, 2 * C), row),
                pl.BlockSpec((count * SEAM, C), row),
                pl.BlockSpec((1, C), fixed),
                pl.BlockSpec((C, C), fixed),
                pl.BlockSpec((C, C), fixed),
                pl.BlockSpec((C, C), fixed),
                pl.BlockSpec(kt.shape, fixed3),
                pl.BlockSpec(vo.shape, fixed3),
            ],
            out_specs=pl.BlockSpec((rows, C), row),
            scratch_shapes=[
                pltpu.VMEM((count, 2, HALF * WIN, 128), BF),
                pltpu.VMEM((count, 2, HALF * WIN, C), BF),
                pltpu.VMEM((2, HALF * 32, 128), BF),
                pltpu.VMEM((2, HALF * 32, C), BF),
                pltpu.VMEM((rows, 2 * C), F32),
            ],
        ),
        out_shape=jax.ShapeDtypeStruct((pixels, C), BF),
        compiler_params=params(56),
        cost_estimate=pl.CostEstimate(flops=40 * pixels * C * C, bytes_accessed=20 * pixels * C, transcendentals=0),
        name="window_attention",
    )(offsets, x, part, q, acc, seam_rows, gain, wk, wv, wo, kt, vo)


def rotation(dx, dz, dy):
    pairs = []
    for f in range(32):
        x, z, y = f // 8, f // 4 % 2, f % 4
        pairs.append((f, (x + dx) % 4 * 8 + (z + dz) % 2 * 4 + (y + dy) % 4))
    return pairs


def gather_face(block):
    for steps in ([(0, 0, 1), (0, 0, 2), (0, 0, 3)], [(0, 1, 0)], [(1, 0, 0), (2, 0, 0), (3, 0, 0)]):
        block = jnp.concatenate([block] + [lax.ppermute(block, "face", rotation(*s)) for s in steps])
    return block


def place_in_pool(index, windows):
    face, local = index // windows, index % windows
    me = lax.axis_index("face")
    dx = (me // 8 - face // 8) % 4
    dz = (me // 4 - face // 4) % 2
    dy = (me - face) % 4
    return ((dx * 2 + dz) * 4 + dy) * windows + local


def local(pixel_state, norm1_gain, w_qkv, w_out, shift_offsets, seam_table):
    gain = norm1_gain.reshape(1, C)
    wq, wk, wv = w_qkv[:, :C], w_qkv[:, C:2 * C], w_qkv[:, 2 * C:]
    q, pooled = first(pixel_state, gain, wq)
    group_rows = lax.all_gather(pooled, "sub", axis=0, tiled=True)
    pool = gather_face(pooled)
    part = lax.ppermute(pixel_state, "face", [(i, i ^ 1) for i in range(32)])
    kt, vo = group(group_rows, wk, wv)
    acc = coarse(q, kt, vo)
    index = place_in_pool(seam_table, pooled.shape[0]).reshape(-1, 1)
    seam_rows = seam(index, pool)
    return window(shift_offsets, pixel_state, part, q, acc, seam_rows, gain, wk, wv, w_out, kt, vo)


def solution(mesh):
    return jax.shard_map(
        local,
        mesh=mesh,
        in_specs=(
            P(("face", "sub"), None),
            P(),
            P(),
            P(),
            P(("face", "sub")),
            P(("face", "sub"), None),
        ),
        out_specs=P(("face", "sub"), None),
        check_vma=False,
    )
```

profile of v0, /device:TPU:102, one launch (start us, length us, event | category | flops | bytes accessed | tf_op | source)
XLA Modules:
  0.0 238.3 jit_solution(1303907878348985924)
XLA Ops:
  0.0 1.1 fusion.16
  1.1 0.0 copy-start.1
  1.1 0.0 copy-start.2
  1.1 0.0 copy-start.3
  1.1 0.7 copy-done.3
  1.8 7.4 %norm_queries_pool.1 = (bf16[8192,256]{1,0:T(8,128)(2,1)S(1)}, bf16[128,256]{1,0:T(8,128)(2,1)S(1)}) custom-call(bf16[8192,256]{1,0:T(8,128)(2,1)} %x_ref.3, f32[1,256]{1,0:T(1,128)S(1)} %bitcast.2, bf16[256,256]{1,0:T(8,128)(2,1)S(1)} %get-tuple-element.14.wq_ref), custom_call_target="tpu_custom_call" | custom-call | flops 1073741824 | bytes 8388608 | tf_op jit(solution)/shard_map/norm_queries_pool/pallas_call | solution.py:62
  9.2 0.0 copy-start.4
  9.2 2.0 copy-done.4
  11.2 3.0 %collective-permute-start.3 = (bf16[128,256]{1,0:T(8,128)(2,1)S(1)}, bf16[128,256]{1,0:T(8,128)(2,1)S(1)}, u32[]{:S(2)}, u32[]{:S(2)}) collective-permute-start(bf16[128,256]{1,0:T(8,128)(2,1)S(1)} %get-tuple-element.10), channel_id=1, source_target_pairs={{0,12},{4,0},{8,4},{12,8},{16,28},{20,16},{24,20},{28,24},{32,44},... | collective-permute-start | bytes 196616 | tf_op jit(solution)/shard_map/ppermute | solution.py:327
  14.2 0.6 collective-permute-start.2
  14.8 1.0 collective-permute-start.1
  15.8 1.9 collective-permute-start
  17.7 5.8 %all_gather.3.g_ref = bf16[512,256]{1,0:T(8,128)(2,1)S(1)} all-gather(bf16[128,256]{1,0:T(8,128)(2,1)S(1)} %get-tuple-element.10), channel_id=1, replica_groups=mesh['face'=32,'sub'=4] {'sub'}, dimensions={0}, use_global_device_ids=true | all-gather | bytes 327680 | tf_op jit(solution)/shard_map/all_gather | solution.py:344
  23.5 0.0 copy-done.1
  23.5 0.0 copy-done.2
  23.5 0.5 group_keys_values.1
  24.0 0.0 copy-start.6
  24.0 1.0 copy-done.6
  25.0 0.0 copy-start.5
  25.0 0.7 constant_dynamic-update-slice_fusion.4
  25.7 0.0 collective-permute-done.3
  25.7 0.0 collective-permute-done.2
  25.7 0.0 collective-permute-done.1
  25.7 0.6 collective-permute-start.4
  26.3 0.6 constant_dynamic-update-slice_fusion.3
  27.0 0.6 constant_dynamic-update-slice_fusion.2
  27.6 0.6 constant_dynamic-update-slice_fusion.1
  28.3 7.6 %collective-permute-done.4 = bf16[512,256]{1,0:T(8,128)(2,1)S(1)} collective-permute-done((bf16[512,256]{1,0:T(8,128)(2,1)S(1)}, bf16[512,256]{1,0:T(8,128)(2,1)S(1)}, u32[]{:S(2)}, u32[]{:S(2)}) %collective-permute-start.4) | collective-permute-done | bytes 262176 | tf_op jit(solution)/shard_map/ppermute | solution.py:327
  35.9 0.7 constant_dynamic-update-slice_fusion
  36.6 0.0 copy-done.5
  36.6 0.8 collective-permute-start.7
  37.4 1.1 collective-permute-start.6
  38.5 2.1 collective-permute-start.5
  40.6 0.0 copy-start.7
  40.6 46.7 %group_attention.1.acc_ref = f32[8192,512]{1,0:T(8,128)} custom-call(bf16[8192,256]{1,0:T(8,128)(2,1)} %copy-done.4, bf16[8,128,512]{2,1,0:T(8,128)(2,1)} %copy-done.6, bf16[8,512,256]{2,1,0:T(8,128)(2,1)} %copy-done.5), custom_call_target="tpu_custom_call" | custom-call | flops 34359738368 | bytes 20971520 | tf_op jit(solution)/shard_map/group_attention/pallas_call | solution.py:127
  87.3 0.0 copy-done.7
  87.3 0.1 copy.8
  87.5 0.2 reshape.8.index_ref
  87.6 0.0 collective-permute-done.5
  87.7 1.1 constant_dynamic-update-slice_fusion.7
  88.7 0.0 collective-permute-done.6
  88.7 1.1 constant_dynamic-update-slice_fusion.6
  89.8 0.0 collective-permute-done.7
  89.9 3.0 %seam_rows.1.seam_ref = bf16[1024,256]{1,0:T(8,128)(2,1)S(1)} custom-call(s32[1024,1]{1,0:T(8,128)S(1)} %reshape.8.index_ref, bf16[4096,256]{1,0:T(8,128)(2,1)S(1)} %constant_dynamic-update-slice_fusion.5.pool_ref), custom_call_target="tpu_custom_call" | custom-call | tf_op jit(solution)/shard_map/seam_rows/pallas_call | solution.py:158
  92.9 0.0 copy-start
  92.9 0.8 copy-done
  93.7 14.3 %collective-permute-done.part_ref = bf16[8192,256]{1,0:T(8,128)(2,1)} collective-permute-done((bf16[8192,256]{1,0:T(8,128)(2,1)}, bf16[8192,256]{1,0:T(8,128)(2,1)}, u32[]{:S(2)}, u32[]{:S(2)}) %collective-permute-start) | collective-permute-done | bytes 4194336 | tf_op jit(solution)/shard_map/ppermute | solution.py:346
  108.0 130.3 %window_attention.1 = bf16[8192,256]{1,0:T(8,128)(2,1)} custom-call(s32[128]{0:T(128)} %offset_ref.1, bf16[8192,256]{1,0:T(8,128)(2,1)} %x_ref.3, bf16[8192,256]{1,0:T(8,128)(2,1)} %collective-permute-done.part_ref, bf16[8192,256]{1,0:T(8,128)(2,1)} %copy-done.4, f32[8192,512]{1,0:T(8,128)} %group_attention.1.acc_ref, bf16[1024,256]{1,0:T(8,128)(2,1)} %copy-done, ...), custom_call_target="tpu_custom_call" | custom-call | flops 21474836480 | bytes 41943040 | tf_op jit(solution)/shard_map/window_attention/pallas_call | solution.py:283
  (3 shorter events, 0.1 us)
Async XLA Ops:
  1.1 22.4 %copy-start.1 = (bf16[256,256]{1,0:T(8,128)(2,1)}, bf16[256,256]{1,0:T(8,128)(2,1)S(1)}, u32[]{:S(2)}) copy-start(bf16[256,256]{1,0:T(8,128)(2,1)S(1)} %get-tuple-element.13.wv_ref) | copy-start | bytes 393220
  1.1 22.4 %copy-start.2 = (bf16[256,256]{1,0:T(8,128)(2,1)}, bf16[256,256]{1,0:T(8,128)(2,1)S(1)}, u32[]{:S(2)}) copy-start(bf16[256,256]{1,0:T(8,128)(2,1)S(1)} %get-tuple-element.15.wk_ref) | copy-start | bytes 393220
  1.1 0.7 copy-start.3
  9.2 2.0 copy-start.4
  11.2 14.5 %collective-permute-start.3 = (bf16[128,256]{1,0:T(8,128)(2,1)S(1)}, bf16[128,256]{1,0:T(8,128)(2,1)S(1)}, u32[]{:S(2)}, u32[]{:S(2)}) collective-permute-start(bf16[128,256]{1,0:T(8,128)(2,1)S(1)} %get-tuple-element.10), channel_id=1, source_target_pairs={{0,12},{4,0},{8,4},{12,8},{16,28},{20,16},{24,20},{28,24},{32,44},... | collective-permute-start | bytes 196616 | tf_op jit(solution)/shard_map/ppermute | solution.py:327
  14.2 11.5 %collective-permute-start.2 = (bf16[128,256]{1,0:T(8,128)(2,1)S(1)}, bf16[128,256]{1,0:T(8,128)(2,1)S(1)}, u32[]{:S(2)}, u32[]{:S(2)}) collective-permute-start(bf16[128,256]{1,0:T(8,128)(2,1)S(1)} %get-tuple-element.10), channel_id=1, source_target_pairs={{0,8},{4,12},{8,0},{12,4},{16,24},{20,28},{24,16},{28,20},{32,40},... | collective-permute-start | bytes 196616 | tf_op jit(solution)/shard_map/ppermute | solution.py:327
  14.8 10.9 %collective-permute-start.1 = (bf16[128,256]{1,0:T(8,128)(2,1)S(1)}, bf16[128,256]{1,0:T(8,128)(2,1)S(1)}, u32[]{:S(2)}, u32[]{:S(2)}) collective-permute-start(bf16[128,256]{1,0:T(8,128)(2,1)S(1)} %get-tuple-element.10), channel_id=1, source_target_pairs={{0,4},{4,8},{8,12},{12,0},{16,20},{20,24},{24,28},{28,16},{32,36},... | collective-permute-start | bytes 196616 | tf_op jit(solution)/shard_map/ppermute | solution.py:327
  15.8 92.2 %collective-permute-start = (bf16[8192,256]{1,0:T(8,128)(2,1)}, bf16[8192,256]{1,0:T(8,128)(2,1)}, u32[]{:S(2)}, u32[]{:S(2)}) collective-permute-start(bf16[8192,256]{1,0:T(8,128)(2,1)} %x_ref.3), channel_id=1, source_target_pairs={{0,4},{4,0},{8,12},{12,8},{16,20},{20,16},{24,28},{28,24},{32,36},... | collective-permute-start | bytes 12582920 | tf_op jit(solution)/shard_map/ppermute | solution.py:346
  24.0 1.0 copy-start.6
  25.0 11.6 %copy-start.5 = (bf16[8,512,256]{2,1,0:T(8,128)(2,1)}, bf16[8,512,256]{2,1,0:T(8,128)(2,1)S(1)}, u32[]{:S(2)}) copy-start(bf16[8,512,256]{2,1,0:T(8,128)(2,1)S(1)} %get-tuple-element.12.vo_ref) | copy-start | bytes 6291460
  25.7 10.1 %collective-permute-start.4 = (bf16[512,256]{1,0:T(8,128)(2,1)S(1)}, bf16[512,256]{1,0:T(8,128)(2,1)S(1)}, u32[]{:S(2)}, u32[]{:S(2)}) collective-permute-start(bf16[512,256]{1,0:T(8,128)(2,1)S(1)} %pad_maximum_fusion), channel_id=1, source_target_pairs={{0,16},{4,20},{8,24},{12,28},{16,0},{20,4},{24,8},{28,12},{32,48},... | collective-permute-start | bytes 786440 | tf_op jit(solution)/shard_map/ppermute | solution.py:327
  36.6 53.2 %collective-permute-start.7 = (bf16[1024,256]{1,0:T(8,128)(2,1)}, bf16[1024,256]{1,0:T(8,128)(2,1)S(1)}, u32[]{:S(2)}, u32[]{:S(2)}) collective-permute-start(bf16[1024,256]{1,0:T(8,128)(2,1)} %get-tuple-element.16), channel_id=1, source_target_pairs={{0,96},{4,100},{8,104},{12,108},{16,112},{20,116},{24,120},{28,124... | collective-permute-start | bytes 1572872 | tf_op jit(solution)/shard_map/ppermute | solution.py:327
  37.4 51.3 %collective-permute-start.6 = (bf16[1024,256]{1,0:T(8,128)(2,1)}, bf16[1024,256]{1,0:T(8,128)(2,1)}, u32[]{:S(2)}, u32[]{:S(2)}) collective-permute-start(bf16[1024,256]{1,0:T(8,128)(2,1)} %get-tuple-element.16), channel_id=1, source_target_pairs={{0,64},{4,68},{8,72},{12,76},{16,80},{20,84},{24,88},{28,92},{32,9... | collective-permute-start | bytes 1572872 | tf_op jit(solution)/shard_map/ppermute | solution.py:327
  38.5 49.1 %collective-permute-start.5 = (bf16[1024,256]{1,0:T(8,128)(2,1)}, bf16[1024,256]{1,0:T(8,128)(2,1)}, u32[]{:S(2)}, u32[]{:S(2)}) collective-permute-start(bf16[1024,256]{1,0:T(8,128)(2,1)} %get-tuple-element.16), channel_id=1, source_target_pairs={{0,32},{4,36},{8,40},{12,44},{16,48},{20,52},{24,56},{28,60},{32,6... | collective-permute-start | bytes 1572872 | tf_op jit(solution)/shard_map/ppermute | solution.py:327
  40.6 46.7 %copy-start.7 = (s32[128,8]{0,1:T(8,128)S(1)}, s32[128,8]{0,1:T(8,128)}, u32[]{:S(2)}) copy-start(s32[128,8]{0,1:T(8,128)} %param.11) | copy-start | bytes 12292
  92.9 0.8 copy-start
where the time goes:
time: 238 us
  Pallas kernels  188 us (79%)
  waiting for transfers between devices  21.9 us (9%)
  local copies, waits for them, and re-layouts  11.3 us (5%)
  starting transfers between devices  11.2 us (5%)
  blocking collectives  5.77 us (2%)
    pallas_call x1, Pallas kernels, window(): pl.pallas_call(window_body, grid_spec=pltpu.PrefetchScalarGridSpec(num_sc...  130 us
    pallas_call x1, Pallas kernels, coarse(): pl.pallas_call(coarse_body, grid=(pixels // rows,), in_specs=[pl.BlockSpe...  46.7 us
    ppermute x1, waiting for transfers between devices, local(): part = lax.ppermute(pixel_state, 'face', [(i, i ^ 1) for i in range(32)])  14.3 us
    ppermute x7, starting transfers between devices, gather_face(): lax.ppermute(block, 'face', rotation(*s))  9.29 us
    unnamed x22, local copies, waits for them, and re-layouts  9.23 us
    ppermute x7, waiting for transfers between devices, gather_face(): lax.ppermute(block, 'face', rotation(*s))  7.61 us
    pallas_call x1, Pallas kernels, first(): pl.pallas_call(first_body, grid=(pixels // rows,), in_specs=[pl.BlockSpec...  7.36 us
    all_gather x1, blocking collectives, local(): group_rows = lax.all_gather(pooled, 'sub', axis=0, tiled=True)  5.77 us
  transfers between devices with their start and end apart: 8, of which 2 were waited for; matrix products, arithmetic and copies ran while one was open for 2% of the time, Pallas kernels for 21%

commit v1 on v0

v1 whole, which is shorter than its diff:
```python
import functools
import math

import jax
import jax.numpy as jnp
from jax import lax
from jax.experimental import pallas as pl
from jax.experimental.pallas import tpu as pltpu
from jax.sharding import PartitionSpec as P

HEADS = 8
HALF = HEADS // 2
DIM = 32
C = 256
WIN = 64
SEAM = 8
EPS = 1e-05
SCALE = math.log2(math.e) / math.sqrt(DIM)
BF = jnp.bfloat16
F32 = jnp.float32
HIGH = 2.0 ** 100
NEG = -1e30
MB = 1024 * 1024
PARTS = ((0, 6144, 4192), (6144, 2048, 1600))
MARK = 16


def params(limit):
    return pltpu.CompilerParams(vmem_limit_bytes=limit * MB)


def exp2(x):
    return jnp.exp2(x)


def dot(a, b):
    return jnp.dot(a, b, preferred_element_type=F32)


def dot_nt(a, b):
    return lax.dot_general(a, b, (((1,), (1,)), ((), ())), preferred_element_type=F32)


def sent(offset):
    return (offset + 7) // 8 * 8


def norm_rows(x, gain):
    centre = jnp.mean(x, axis=-1, keepdims=True)
    x = x - centre
    spread = jnp.mean(x * x, axis=-1, keepdims=True)
    return (x * lax.rsqrt(spread + EPS) * gain).astype(BF)


def pool_body(x_ref, gain_ref, pooled_ref):
    rows = x_ref.shape[0]
    normed = norm_rows(x_ref[...].astype(F32), gain_ref[...])
    count = rows // WIN
    row = lax.broadcasted_iota(jnp.int32, (count, rows), 1) // WIN
    pick = jnp.where(row == lax.broadcasted_iota(jnp.int32, (count, rows), 0), 1.0, 0.0).astype(BF)
    pooled_ref[...] = (dot(pick, normed) * (1.0 / math.sqrt(WIN))).astype(BF)


def pool_rows(x, gain, rows=1024):
    pixels = x.shape[0]
    return pl.pallas_call(
        pool_body,
        grid=(pixels // rows,),
        in_specs=[
            pl.BlockSpec((rows, C), lambda i: (i, 0)),
            pl.BlockSpec((1, C), lambda i: (0, 0)),
        ],
        out_specs=pl.BlockSpec((rows // WIN, C), lambda i: (i, 0)),
        out_shape=jax.ShapeDtypeStruct((pixels // WIN, C), BF),
        compiler_params=params(48),
        cost_estimate=pl.CostEstimate(flops=2 * pixels * C * C, bytes_accessed=4 * pixels * C, transcendentals=0),
        name="norm_pool",
    )(x, gain)


def pack_body(first, offset_ref, x_ref, main_ref, rest_ref, packed, at_row):
    step = pl.program_id(0)
    count = x_ref.shape[0] // WIN
    limit = main_ref.shape[0]

    @pl.when(step == 0)
    def _():
        at_row[0] = 0

    start = at_row[0]
    for w in range(count):
        packed[pl.ds(pl.multiple_of(start, 8), WIN), :] = x_ref[w * WIN:w * WIN + WIN, :].astype(F32)
        start = start + sent(offset_ref[first + step * count + w])
    at_row[0] = start

    @pl.when(step == pl.num_programs(0) - 1)
    def _():
        main_ref[...] = packed[0:limit, :].astype(BF)

        @pl.when(start > limit)
        def _():
            rest_ref[...] = packed[limit:, :].astype(BF)


def pack(part, offsets, x, rows=1024):
    first, run, limit = part
    whole = lambda i, s: (0, 0)
    return pl.pallas_call(
        functools.partial(pack_body, first // WIN),
        grid_spec=pltpu.PrefetchScalarGridSpec(
            num_scalar_prefetch=1,
            grid=(run // rows,),
            in_specs=[pl.BlockSpec((rows, C), lambda i, s: (first // rows + i, 0))],
            out_specs=[pl.BlockSpec((limit, C), whole), pl.BlockSpec((run - limit, C), whole)],
            scratch_shapes=[pltpu.VMEM((run, C), F32), pltpu.SMEM((1,), jnp.int32)],
        ),
        out_shape=[
            jax.ShapeDtypeStruct((limit, C), BF),
            jax.ShapeDtypeStruct((run - limit, C), BF),
        ],
        compiler_params=params(32),
        cost_estimate=pl.CostEstimate(flops=0, bytes_accessed=10 * run * C, transcendentals=0),
        name="pack_rows",
    )(offsets, x)


def join_body(*refs):
    lo = 0
    for ref in refs[:-1]:
        refs[-1][lo:lo + ref.shape[0]] = ref[...]
        lo += ref.shape[0]


def join(*blocks):
    rows = sum(b.shape[0] for b in blocks)
    return pl.pallas_call(
        join_body, out_shape=jax.ShapeDtypeStruct((rows, C), BF), compiler_params=params(32), name="join_blocks"
    )(*blocks)


def group_body(*refs):
    wk_ref, wv_ref, kt_ref, vo_ref = refs[-4:]
    g = jnp.concatenate([ref[...] for ref in refs[:-4]], axis=0)
    count = g.shape[0]
    kt = lax.dot_general(wk_ref[...], g, (((0,), (1,)), ((), ())), preferred_element_type=F32)
    v = dot(g, wv_ref[...])
    feat = lax.broadcasted_iota(jnp.int32, (128, count), 0) // DIM
    lane = lax.broadcasted_iota(jnp.int32, (count, 128), 1) // DIM
    for h in range(HEADS):
        lo = (h // HALF) * 128
        kt_ref[h] = jnp.where(feat == h % HALF, kt[lo:lo + 128], 0.0).astype(BF)
        mine = lane == h % HALF
        vo_ref[h // HALF, h % HALF * count:h % HALF * count + count, 0:128] = jnp.where(mine, v[:, lo:lo + 128], 0.0).astype(BF)
        vo_ref[h // HALF, h % HALF * count:h % HALF * count + count, 128:256] = jnp.where(mine, 1.0, 0.0).astype(BF)


def group(blocks, w_qkv):
    count = sum(b.shape[0] for b in blocks)
    return pl.pallas_call(
        group_body,
        grid=(1,),
        in_specs=[pl.BlockSpec(b.shape, lambda i: (0, 0)) for b in blocks]
        + [pl.BlockSpec((C, C), lambda i: (0, 1)), pl.BlockSpec((C, C), lambda i: (0, 2))],
        out_specs=[
            pl.BlockSpec((HEADS, 128, count), lambda i: (0, 0, 0)),
            pl.BlockSpec((2, HALF * count, C), lambda i: (0, 0, 0)),
        ],
        out_shape=[
            jax.ShapeDtypeStruct((HEADS, 128, count), BF),
            jax.ShapeDtypeStruct((2, HALF * count, C), BF),
        ],
        compiler_params=params(32),
        name="group_keys_values",
    )(*blocks, w_qkv, w_qkv)


def coarse_body(x_ref, gain_ref, wq_ref, kt_ref, vo_ref, after_ref, q_ref, acc_ref):
    del after_ref
    normed = norm_rows(x_ref[...].astype(F32), gain_ref[...])
    q = (dot(normed, wq_ref[...]) * SCALE).astype(BF)
    q_ref[...] = q
    weights = []
    for half in range(2):
        heads = range(half * HALF, half * HALF + HALF)
        mine = q[:, half * 128:half * 128 + 128]
        weights.append(jnp.concatenate([exp2(dot(mine, kt_ref[h])).astype(BF) for h in heads], axis=1))
    for half in range(2):
        acc_ref[:, half * C:half * C + C] = dot(weights[half], vo_ref[half])


def coarse(part, x, gain, w_qkv, kt, vo, after, rows=1024):
    first, pixels, _ = part
    steps = pixels // rows
    count = kt.shape[2]
    return pl.pallas_call(
        coarse_body,
        grid=(steps,),
        in_specs=[
            pl.BlockSpec((rows, C), lambda i: (first // rows + i, 0)),
            pl.BlockSpec((1, C), lambda i: (0, 0)),
            pl.BlockSpec((C, C), lambda i: (0, 0)),
            pl.BlockSpec(kt.shape, lambda i: (0, 0, 0)),
            pl.BlockSpec(vo.shape, lambda i: (0, 0, 0)),
            pl.BlockSpec(memory_space=pl.ANY),
        ],
        out_specs=[
            pl.BlockSpec((rows, C), lambda i: (i, 0)),
            pl.BlockSpec((rows, 2 * C), lambda i: (i, 0)),
        ],
        out_shape=[
            jax.ShapeDtypeStruct((pixels, C), BF),
            jax.ShapeDtypeStruct((pixels, 2 * C), F32),
        ],
        compiler_params=params(60),
        cost_estimate=pl.CostEstimate(
            flops=4 * pixels * HEADS * count * C, bytes_accessed=10 * pixels * C, transcendentals=pixels * HEADS * count
        ),
        name="group_attention",
    )(x, gain, w_qkv, kt, vo, after)


def seam_body(index_ref, *refs):
    out_ref, mark_ref = refs[-2:]
    rows = index_ref.shape[0]
    total = jnp.zeros((rows, C), F32)
    lo = 0
    marks = jnp.zeros((MARK, 128), F32)
    for ref in refs[:-2]:
        step = ref.shape[0]
        for at in range(step // 8 - MARK, step, step // 8):
            marks = jnp.maximum(marks, ref[at:at + MARK, 0:128].astype(F32))
        at = lax.broadcasted_iota(jnp.int32, (rows, step), 1) + lo
        pick = jnp.where(at == index_ref[...], 1.0, 0.0).astype(BF)
        total = total + dot(pick, ref[...])
        lo += step
    out_ref[...] = total.astype(BF)
    mark_ref[...] = marks


def seam(index, pools, rows=256):
    count = index.shape[0]
    return pl.pallas_call(
        seam_body,
        grid=(count // rows,),
        in_specs=[pl.BlockSpec((rows, 1), lambda i: (i, 0))]
        + [pl.BlockSpec(pool.shape, lambda i: (0, 0)) for pool in pools],
        out_specs=[pl.BlockSpec((rows, C), lambda i: (i, 0)), pl.BlockSpec((MARK, 128), lambda i: (0, 0))],
        out_shape=[jax.ShapeDtypeStruct((count, C), BF), jax.ShapeDtypeStruct((MARK, 128), F32)],
        compiler_params=params(48),
        name="seam_rows",
    )(index, *pools)


def window_body(
    first, offset_ref, x_ref, main_ref, rest_ref, q_ref, acc_ref, seam_ref, gain_ref, wk_ref, wv_ref, wo_ref,
    kt_hbm, vo_hbm, given_ref, out_ref, kbd, vbd, vsm, ksm, sums, packed, wkt_ref, kt_ref, vo_ref, at_row, done,
):
    del given_ref
    limit = main_ref.shape[0]
    rows = x_ref.shape[0]
    count = rows // WIN
    pairs = count // 2
    near = 2 * SEAM
    step = pl.program_id(0)
    first_window = first + step * count

    def lanes_of(k):
        return jnp.where(lax.broadcasted_iota(jnp.int32, (1, 128), 1) // DIM == k, 1.0, 0.0).astype(BF)

    position = lax.broadcasted_iota(jnp.int32, (WIN, 1), 0)

    @pl.when(step == 0)
    def _():
        at_row[0] = 0
        wkt_ref[...] = wk_ref[...].astype(F32).T.astype(BF)
        packed[0:limit, :] = main_ref[...].astype(F32)

        def add(w, total):
            return total + sent(offset_ref[first + w])

        @pl.when(lax.fori_loop(0, pl.num_programs(0) * count, add, 0) > limit)
        def _():
            packed[limit:, :] = rest_ref[...].astype(F32)

        kbd[...] = jnp.zeros(kbd.shape, BF)
        vsm[...] = jnp.zeros(vsm.shape, BF)
        for half in range(2):
            for k in range(HALF):
                for w in range(count):
                    vbd[w, half, k * WIN:k * WIN + WIN, 128:256] = jnp.broadcast_to(lanes_of(k), (WIN, 128))
                h = half * HALF + k
                for p in range(pairs):
                    vsm[p, h * near:h * near + near, half * C + 128:half * C + C] = jnp.broadcast_to(
                        lanes_of(k), (near, 128)
                    )

    x = x_ref[...].astype(F32)
    chosen = []
    start = at_row[0]
    for w in range(count):
        offset = offset_ref[first_window + w]
        other = packed[pl.ds(pl.multiple_of(start, 8), WIN), :]
        chosen.append(jnp.where(position >= offset, x[w * WIN:w * WIN + WIN], other))
        start = start + sent(offset)
    at_row[0] = start
    normed = norm_rows(jnp.concatenate(chosen, axis=0), gain_ref[...])
    keys = dot_nt(wkt_ref[...], normed)
    values = dot(normed, wv_ref[...]).astype(BF)
    block = (lax.broadcasted_iota(jnp.int32, (64, 128), 0) // DIM) == (
        lax.broadcasted_iota(jnp.int32, (64, 128), 1) // WIN
    )
    first_lanes = lax.broadcasted_iota(jnp.int32, (64, 128), 1) < WIN
    for half in range(2):
        for b in range(2):
            lo = half * 128 + b * 64
            for p in range(pairs):
                pair = keys[lo:lo + 64, p * 128:p * 128 + 128]
                turned = pltpu.roll(pair, WIN, 1)
                to = (half, slice(b * 64, b * 64 + 64), slice(b * 128, b * 128 + 128))
                kbd[(2 * p,) + to] = jnp.where(block, jnp.where(first_lanes, pair, turned), 0.0).astype(BF)
                kbd[(2 * p + 1,) + to] = jnp.where(block, jnp.where(first_lanes, turned, pair), 0.0).astype(BF)
        for k in range(HALF):
            mine = lanes_of(k)
            for w in range(count):
                vbd[w, half, k * WIN:k * WIN + WIN, 0:128] = (
                    values[w * WIN:w * WIN + WIN, half * 128:half * 128 + 128] * mine
                )

    wide = pairs * 128
    seam_k = dot_nt(wkt_ref[...], seam_ref[...]).astype(BF)
    column = lax.broadcasted_iota(jnp.int32, (count * SEAM, wide), 1)
    spread = jnp.where(
        lax.broadcasted_iota(jnp.int32, (count * SEAM, wide), 0) == column // 128 * near + column % near, 1.0, 0.0
    ).astype(BF)
    of_head = (lax.broadcasted_iota(jnp.int32, (C, wide), 1) % 128) // near == (
        lax.broadcasted_iota(jnp.int32, (C, wide), 0) // DIM
    )
    seam_kt = jnp.where(of_head, dot(seam_k, spread), 0.0).astype(BF)
    for p in range(pairs):
        ksm[p] = seam_kt[:, p * 128:p * 128 + 128]
    seam_v = dot(seam_ref[...], wv_ref[...]).astype(BF)
    for h in range(HEADS):
        half, k = h // HALF, h % HALF
        for p in range(pairs):
            vsm[p, h * near:h * near + near, half * C:half * C + 128] = (
                seam_v[p * near:p * near + near, half * 128:half * 128 + 128] * lanes_of(k)
            )
    own = (lax.broadcasted_iota(jnp.int32, (128, 128), 1) % near) // SEAM == (
        lax.broadcasted_iota(jnp.int32, (128, 128), 0) // WIN
    )

    def window_scores(w, half):
        at = pl.ds(pl.multiple_of(w * WIN, WIN), WIN)
        return dot(q_ref[at, half * 128:half * 128 + 128], kbd[w, half])

    def seam_scores(p):
        return dot(q_ref[pl.ds(pl.multiple_of(p * 128, 128), 128), :], ksm[p])

    weights_s = [jnp.where(own, exp2(seam_scores(p)), 0.0).astype(BF) for p in range(pairs)]
    weights_w = [[exp2(window_scores(w, half)).astype(BF) for half in range(2)] for w in range(count)]
    for p in range(pairs):
        sums[p * 128:p * 128 + 128, :] = acc_ref[p * 128:p * 128 + 128, :] + dot(weights_s[p], vsm[p])
    for w in range(count):
        at = slice(w * WIN, w * WIN + WIN)
        for half in range(2):
            sums[at, half * C:half * C + C] += dot(weights_w[w][half], vbd[w, half])

    check = jnp.zeros((8, 128), F32)
    parts = []
    for half in range(2):
        den = sums[:, half * C + 128:half * C + C]
        inverse = 1.0 / den
        check = check + jnp.sum((den + inverse).reshape(rows // 8, 8, 128), axis=0)
        parts.append(sums[:, half * C:half * C + 128] * inverse)
    attended = jnp.concatenate(parts, axis=1).astype(BF)
    out_ref[...] = (x + dot(attended, wo_ref[...])).astype(BF)
    fine = jnp.sum(check) <= HIGH

    @pl.when(jnp.logical_not(fine))
    def _():
        copies = [pltpu.make_async_copy(kt_hbm, kt_ref, done.at[0]), pltpu.make_async_copy(vo_hbm, vo_ref, done.at[1])]
        for copy in copies:
            copy.start()
        for copy in copies:
            copy.wait()
        keys_g = kt_ref.shape[2]
        head_s = lax.broadcasted_iota(jnp.int32, (128, 128), 1) // near
        head_w = lax.broadcasted_iota(jnp.int32, (128, C), 1) // WIN

        def exact(p, carry):
            at = pl.ds(pl.multiple_of(p * 128, 128), 128)
            scores_s = jnp.where(own, seam_scores(p), NEG)
            tops_s = jnp.zeros((128, 128), F32)
            totals = []
            for half in range(2):
                q = q_ref[at, half * 128:half * 128 + 128]
                scores_w = jnp.concatenate([window_scores(2 * p + w, half) for w in range(2)], axis=0)
                tops_w = jnp.zeros((128, C), F32)
                total = jnp.zeros((128, C), F32)
                for k in range(HALF):
                    h = half * HALF + k
                    scores_g = dot(q, kt_ref[h])
                    top = jnp.max(scores_g, axis=1, keepdims=True)
                    top = jnp.maximum(top, jnp.max(jnp.where(head_s == h, scores_s, NEG), axis=1, keepdims=True))
                    top = jnp.maximum(top, jnp.max(jnp.where(head_w == k, scores_w, NEG), axis=1, keepdims=True))
                    tops_s = jnp.where(head_s == h, top, tops_s)
                    tops_w = jnp.where(head_w == k, top, tops_w)
                    total = total + dot(
                        exp2(scores_g - top).astype(BF), vo_ref[half, k * keys_g:k * keys_g + keys_g]
                    )
                weights = exp2(scores_w - tops_w).astype(BF)
                totals.append(total + jnp.concatenate(
                    [dot(weights[w * WIN:w * WIN + WIN], vbd[2 * p + w, half]) for w in range(2)], axis=0
                ))
            weights = jnp.where(own, exp2(jnp.where(own, scores_s - tops_s, NEG)), 0.0).astype(BF)
            total = jnp.concatenate(totals, axis=1) + dot(weights, vsm[p])
            again = jnp.concatenate(
                [total[:, half * C:half * C + 128] / total[:, half * C + 128:half * C + C] for half in range(2)], axis=1
            ).astype(BF)
            out_ref[at, :] = (x_ref[at, :].astype(F32) + dot(again, wo_ref[...])).astype(BF)
            return carry

        lax.fori_loop(0, pairs, exact, 0)


def window(part, offsets, x, main, rest, q, acc, seam_rows, gain, w_qkv, wo, kt, vo, given, rows=1024):
    first, run, _ = part
    pixels = x.shape[0]
    steps = run // rows
    count = rows // WIN
    whole = lambda i, s: (first // rows + i, 0)
    row = lambda i, s: (i, 0)
    fixed = lambda i, s: (0, 0)
    return pl.pallas_call(
        functools.partial(window_body, first // WIN),
        grid_spec=pltpu.PrefetchScalarGridSpec(
            num_scalar_prefetch=1,
            grid=(steps,),
            in_specs=[
                pl.BlockSpec((rows, C), whole),
                pl.BlockSpec(main.shape, fixed),
                pl.BlockSpec(rest.shape, fixed),
                pl.BlockSpec((rows, C), row),
                pl.BlockSpec((rows, 2 * C), row),
                pl.BlockSpec((count * SEAM, C), whole),
                pl.BlockSpec((1, C), fixed),
                pl.BlockSpec((C, C), lambda i, s: (0, 1)),
                pl.BlockSpec((C, C), lambda i, s: (0, 2)),
                pl.BlockSpec((C, C), fixed),
                pl.BlockSpec(memory_space=pl.ANY),
                pl.BlockSpec(memory_space=pl.ANY),
                pl.BlockSpec(memory_space=pl.ANY),
            ],
            out_specs=pl.BlockSpec((rows, C), whole),
            scratch_shapes=[
                pltpu.VMEM((count, 2, 128, C), BF),
                pltpu.VMEM((count, 2, HALF * WIN, C), BF),
                pltpu.VMEM((count // 2, 128, 2 * C), BF),
                pltpu.VMEM((count // 2, C, 128), BF),
                pltpu.VMEM((rows, 2 * C), F32),
                pltpu.VMEM((run, C), F32),
                pltpu.VMEM((C, C), BF),
                pltpu.VMEM(kt.shape, BF),
                pltpu.VMEM(vo.shape, BF),
                pltpu.SMEM((1,), jnp.int32),
                pltpu.SemaphoreType.DMA((2,)),
            ],
        ),
        out_shape=jax.ShapeDtypeStruct((pixels, C), BF),
        input_output_aliases={13: 0} if first else {},
        compiler_params=params(60),
        cost_estimate=pl.CostEstimate(
            flops=40 * run * C * C, bytes_accessed=20 * run * C, transcendentals=0
        ),
        name="window_attention",
    )(offsets, x, main, rest, q, acc, seam_rows, gain, w_qkv, w_qkv, wo, kt, vo, given)


def rotation(dx, dz, dy):
    pairs = []
    for f in range(32):
        x, z, y = f // 8, f // 4 % 2, f % 4
        pairs.append((f, (x + dx) % 4 * 8 + (z + dz) % 2 * 4 + (y + dy) % 4))
    return pairs


def partner(x):
    return lax.ppermute(x, "face", [(i, i ^ 1) for i in range(32)])


def turned(block, steps):
    return [block] + [lax.ppermute(block, "face", rotation(*s)) for s in steps]


def place_in_pool(index, windows):
    face, local = index // windows, index % windows
    me = lax.axis_index("face")
    dx = (me // 8 - face // 8) % 4
    dz = (me // 4 - face // 4) % 2
    dy = (me - face) % 4
    return ((dx * 2 + dz) * 4 + dy) * (windows + MARK) + local


def by_sub(x, k):
    return lax.ppermute(x, "sub", [(i, i ^ k) for i in range(4)])


def local(pixel_state, norm1_gain, w_qkv, w_out, shift_offsets, seam_table):
    gain = norm1_gain.reshape(1, C)
    asked = partner(shift_offsets)
    lengths = sent(shift_offsets)
    over = False
    for first, run, limit in PARTS:
        over = jnp.logical_or(over, lengths[first // WIN:(first + run) // WIN].sum() > limit)
    mark = jnp.broadcast_to(over.astype(BF), (MARK, C))
    mark = functools.reduce(jnp.maximum, [by_sub(mark, k) for k in (1, 2, 3)], mark)
    pooled = pool_rows(pixel_state, gain)
    groups = [pooled] + [by_sub(pooled, k) for k in (1, 2, 3)]
    columns = turned(join(pooled, mark), [(0, 0, 1), (0, 0, 2), (0, 0, 3)])
    mains, rests = zip(*[pack(part, asked, pixel_state) for part in PARTS])
    mains = [partner(main) for main in mains]
    planes = turned(join(*columns), [(0, 1, 0)])
    cube = join(*planes)
    pools = turned(cube, [(1, 0, 0), (2, 0, 0), (3, 0, 0)])
    kt, vo = group(groups, w_qkv)
    late = coarse(PARTS[1], pixel_state, gain, w_qkv, kt, vo, gain)
    early = coarse(PARTS[0], pixel_state, gain, w_qkv, kt, vo, cube)
    index = place_in_pool(seam_table, pooled.shape[0]).reshape(-1, 1)
    seam_rows, marks = seam(index, pools)
    rests = lax.cond(
        marks[0, 0] > 0.0, lambda r: [partner(x) for x in r], lambda r: [jnp.zeros_like(x) for x in r], list(rests)
    )
    out = pixel_state
    for part, main, rest, (q, acc) in zip(PARTS, mains, rests, (early, late)):
        out = window(
            part, shift_offsets, pixel_state, main, rest, q, acc, seam_rows, gain, w_qkv, w_out, kt, vo, out
        )
    return out


def solution(mesh):
    return jax.shard_map(
        local,
        mesh=mesh,
        in_specs=(
            P(("face", "sub"), None),
            P(),
            P(),
            P(),
            P(("face", "sub")),
            P(("face", "sub"), None),
        ),
        out_specs=P(("face", "sub"), None),
        check_vma=False,
    )
```

time: 238 us -> 249 us (1.046)
  the two profiles are of different devices: /device:TPU:102 before, /device:TPU:1 now
where the time goes in v1:
time: 249 us; the launch traced here: 247 us
  Pallas kernels  209 us (84%)
  starting transfers between devices  21.1 us (8%)
  local copies, waits for them, and re-layouts  11.9 us (5%)
    pallas_call x2, Pallas kernels, window(): pl.pallas_call(functools.partial(window_body, first // WIN), grid_spec=pl...  147 us
    pallas_call x2, Pallas kernels, coarse(): pl.pallas_call(coarse_body, grid=(steps,), in_specs=[pl.BlockSpec((rows,...  48.8 us
    ppermute x7, starting transfers between devices, turned(): return [block] + [lax.ppermute(block, 'face', rotation(*s)) for s in steps]  12.8 us
    unnamed x22, local copies, waits for them, and re-layouts  9.33 us
    ppermute x6, starting transfers between devices, by_sub(): return lax.ppermute(x, 'sub', [(i, i ^ k) for i in range(4)])  5.46 us
  transfers between devices with their start and end apart: 16, of which 1 were waited for; matrix products, arithmetic and copies ran while one was open for 1% of the time, Pallas kernels for 69%

profile of v1, /device:TPU:1, one launch (start us, length us, event | category | flops | bytes accessed | tf_op | source)
XLA Modules:
  0.0 247.1 jit_solution(15540211662439969882)
XLA Ops:
  0.0 0.7 fusion.16
  0.7 0.6 slice_reduce_fusion.1
  1.4 0.8 slice_reduce_fusion
  3.5 1.5 collective-permute-start.4
  5.0 1.7 collective-permute-start.5
  6.8 0.1 collective-permute-start.6
  6.8 2.2 copy-done
  9.0 0.7 copy-done.8
  9.7 4.1 %norm_pool.1.refs_0_ = bf16[128,256]{1,0:T(8,128)(2,1)S(1)} custom-call(bf16[8192,256]{1,0:T(8,128)(2,1)S(1)} %copy-done, f32[1,256]{1,0:T(1,128)S(1)} %bitcast.7), custom_call_target="tpu_custom_call" | custom-call | flops 1073741824 | bytes 8388608 | tf_op jit(solution)/shard_map/norm_pool/pallas_call | solution.py:66
  13.7 0.4 collective-permute-start.14
  14.1 1.4 collective-permute-start.15
  15.6 0.0 collective-permute-done.4
  15.6 0.4 collective-permute-start.16
  15.9 0.0 collective-permute-done.5
  15.9 0.0 copy-done.10
  15.9 1.3 collective-permute-start.2
  17.2 0.0 collective-permute-done.6
  17.2 0.3 collective-permute-start.7
  17.5 0.8 collective-permute-done.2.offset_ref
  18.3 2.9 %collective-permute-start.8 = (bf16[144,256]{1,0:T(8,128)(2,1)S(1)}, bf16[144,256]{1,0:T(8,128)(2,1)S(1)}, u32[]{:S(2)}, u32[]{:S(2)}) collective-permute-start(bf16[144,256]{1,0:T(8,128)(2,1)S(1)} %join_blocks.3.refs_0_), channel_id=1, source_target_pairs={{0,8},{4,12},{8,0},{12,4},{16,24},{20,28},{24,16},{28,20},{32,40},... | collective-permute-start | bytes 221192 | tf_op jit(solution)/shard_map/ppermute | solution.py:492
  21.2 0.0 collective-permute-done.14.refs_1_
  21.2 0.8 collective-permute-start.9
  22.0 0.0 copy-done.9
  22.1 0.1 copy.9
  22.2 0.2 reshape.13.index_ref
  22.3 0.0 copy-start.1
  22.4 2.2 copy-done.1
  24.5 3.5 %pack_rows.3 = (bf16[4192,256]{1,0:T(8,128)(2,1)}, bf16[1952,256]{1,0:T(8,128)(2,1)}) custom-call(s32[128]{0:T(128)S(1)} %collective-permute-done.2.offset_ref, bf16[8192,256]{1,0:T(8,128)(2,1)S(1)} %copy-done.1), custom_call_target="tpu_custom_call" | custom-call | bytes 15728640 | tf_op jit(solution)/shard_map/pack_rows/pallas_call | solution.py:108
  28.0 1.0 pack_rows.2
  29.0 0.0 collective-permute-done.15.refs_2_
  29.0 0.8 collective-permute-start.17
  29.8 0.0 collective-permute-done.16.refs_3_
  29.8 0.8 collective-permute-start.3
  30.6 0.0 copy-done.2
  30.6 0.5 group_keys_values.1
  31.1 0.0 copy-start.5
  31.1 1.3 copy-done.5
  32.5 1.1 copy-done.6
  33.5 0.0 collective-permute-done.7.refs_1_
  33.5 0.0 collective-permute-done.8.refs_2_
  33.5 0.0 collective-permute-done.9.refs_3_
  33.6 4.0 %collective-permute-start.10 = (bf16[576,256]{1,0:T(8,128)(2,1)S(1)}, bf16[576,256]{1,0:T(8,128)(2,1)S(1)}, u32[]{:S(2)}, u32[]{:S(2)}) collective-permute-start(bf16[576,256]{1,0:T(8,128)(2,1)S(1)} %join_blocks.4.refs_0_), channel_id=1, source_target_pairs={{0,16},{4,20},{8,24},{12,28},{16,0},{20,4},{24,8},{28,12},{32,48},... | collective-permute-start | bytes 884744 | tf_op jit(solution)/shard_map/ppermute | solution.py:492
  37.6 13.9 %group_attention.2 = (bf16[2048,256]{1,0:T(8,128)(2,1)}, f32[2048,512]{1,0:T(8,128)}) custom-call(bf16[8192,256]{1,0:T(8,128)(2,1)} %x_ref.13, f32[1,256]{1,0:T(1,128)} %bitcast.2, bf16[256,768]{1,0:T(8,128)(2,1)} %wv_ref.3, bf16[8,128,512]{2,1,0:T(8,128)(2,1)} %copy-done.6, bf16[2,2048,256]{2,1,0:T(8,128)(2,1)} %copy-done.5, f32[1,256]{1,0:T(1,128)} %bitcast.3), custom_call_target="tpu_custom_call" | custom-call | flops 8589934592 | bytes 5242880 | tf_op jit(solution)/shard_map/group_attention/pallas_call | solution.py:195
  51.5 0.0 collective-permute-done.10.refs_1_
  51.5 0.0 copy-start.3
  51.5 1.3 collective-permute-start.11
  52.8 2.5 collective-permute-start.12
  55.3 1.2 collective-permute-start.13
  56.4 0.0 copy-done.3
  56.4 34.9 %group_attention.3 = (bf16[6144,256]{1,0:T(8,128)(2,1)}, f32[6144,512]{1,0:T(8,128)}) custom-call(bf16[8192,256]{1,0:T(8,128)(2,1)} %x_ref.13, f32[1,256]{1,0:T(1,128)} %bitcast.4, bf16[256,768]{1,0:T(8,128)(2,1)} %wv_ref.3, bf16[8,128,512]{2,1,0:T(8,128)(2,1)} %copy-done.6, bf16[2,2048,256]{2,1,0:T(8,128)(2,1)} %copy-done.5, bf16[1152,256]{1,0:T(8,128)(2,1)} %copy-done.3), custom_call_target="tpu_custom_call" | custom-call | flops 25769803776 | bytes 15728640 | tf_op jit(solution)/shard_map/group_attention/pallas_call | solution.py:195
  91.3 0.0 collective-permute-done.11.refs_1_
  91.3 0.0 collective-permute-done.12.refs_2_
  91.3 0.0 collective-permute-done.13.refs_3_
  91.3 1.1 copy-done.4
  92.4 3.6 %seam_rows.1 = (bf16[1024,256]{1,0:T(8,128)(2,1)S(1)}, f32[16,128]{1,0:T(8,128)S(1)}) custom-call(s32[1024,1]{1,0:T(8,128)S(1)} %reshape.13.index_ref, bf16[1152,256]{1,0:T(8,128)(2,1)S(1)} %copy-done.4, bf16[1152,256]{1,0:T(8,128)(2,1)S(1)} %collective-permute-done.11.refs_1_, bf16[1152,256]{1,0:T(8,128)(2,1)S(1)} %collective-permute-done.12.refs_2_, ...), custom_call_target="tpu_custom_call" | custom-call | tf_op jit(solution)/shard_map/seam_rows/pallas_call | solution.py:242
  96.0 0.8 copy-done.7
  96.8 0.5 slice.11
  98.0 1.8 conditional.1
  98.0 1.0 broadcast.41
  99.0 0.7 broadcast.42
  99.8 0.0 collective-permute-done.17.main_ref
  99.8 108.3 %window_attention.2.given_ref = bf16[8192,256]{1,0:T(8,128)(2,1)} custom-call(s32[128]{0:T(128)} %offset_ref.3, bf16[8192,256]{1,0:T(8,128)(2,1)} %x_ref.13, bf16[4192,256]{1,0:T(8,128)(2,1)} %collective-permute-done.17.main_ref, bf16[1952,256]{1,0:T(8,128)(2,1)} %get-tuple-element.36.rest_ref, bf16[6144,256]{1,0:T(8,128)(2,1)} %get-tuple-element.37.q_ref, ...), custom_call_target="tpu_custom_call" | custom-call | flops 16106127360 | bytes 31457280 | tf_op jit(solution)/shard_map/window_attention/pallas_call | solution.py:434
  208.1 0.0 collective-permute-done.3.main_ref
  208.1 38.9 %window_attention.3 = bf16[8192,256]{1,0:T(8,128)(2,1)} custom-call(s32[128]{0:T(128)} %offset_ref.3, bf16[8192,256]{1,0:T(8,128)(2,1)} %x_ref.13, bf16[1600,256]{1,0:T(8,128)(2,1)} %collective-permute-done.3.main_ref, bf16[448,256]{1,0:T(8,128)(2,1)} %get-tuple-element.29.rest_ref, ...), custom_call_target="tpu_custom_call", output_to_operand_aliasing={{}: (13, {})} | custom-call | flops 5368709120 | bytes 10485760 | tf_op jit(solution)/shard_map/window_attention/pallas_call | solution.py:434
  (14 shorter events, 0.1 us)
Async XLA Ops:
  0.0 15.9 %copy-start.10 = (s32[128]{0:T(128)S(1)}, s32[128]{0:T(128)}, u32[]{:S(2)}) copy-start(s32[128]{0:T(128)} %offset_ref.3) | copy-start | bytes 1540
  0.0 22.0 %copy-start.9 = (s32[128,8]{0,1:T(8,128)S(1)}, s32[128,8]{0,1:T(8,128)}, u32[]{:S(2)}) copy-start(s32[128,8]{0,1:T(8,128)} %param.13) | copy-start | bytes 12292
  3.5 12.0 %collective-permute-start.4 = (bf16[16,256]{1,0:T(8,128)(2,1)S(1)}, bf16[16,256]{1,0:T(8,128)(2,1)S(1)}, u32[]{:S(2)}, u32[]{:S(2)}) collective-permute-start(bf16[16,256]{1,0:T(8,128)(2,1)S(1)} %broadcast_in_dim.3), channel_id=1, source_target_pairs={{0,1},{1,0},{2,3},{3,2},{4,5},{5,4},{6,7},{7,6},{8,9},{9,8},{10,11... | collective-permute-start | bytes 24584 | tf_op jit(solution)/shard_map/ppermute | solution.py:505
  5.0 10.9 %collective-permute-start.5 = (bf16[16,256]{1,0:T(8,128)(2,1)S(1)}, bf16[16,256]{1,0:T(8,128)(2,1)S(1)}, u32[]{:S(2)}, u32[]{:S(2)}) collective-permute-start(bf16[16,256]{1,0:T(8,128)(2,1)S(1)} %broadcast_in_dim.3), channel_id=1, source_target_pairs={{0,2},{1,3},{2,0},{3,1},{4,6},{5,7},{6,4},{7,5},{8,10},{9,11},{10,... | collective-permute-start | bytes 24584 | tf_op jit(solution)/shard_map/ppermute | solution.py:505
  6.8 10.5 %collective-permute-start.6 = (bf16[16,256]{1,0:T(8,128)(2,1)S(1)}, bf16[16,256]{1,0:T(8,128)(2,1)S(1)}, u32[]{:S(2)}, u32[]{:S(2)}) collective-permute-start(bf16[16,256]{1,0:T(8,128)(2,1)S(1)} %broadcast_in_dim.3), channel_id=1, source_target_pairs={{0,3},{1,2},{2,1},{3,0},{4,7},{5,6},{6,5},{7,4},{8,11},{9,10},{10,... | collective-permute-start | bytes 24584 | tf_op jit(solution)/shard_map/ppermute | solution.py:505
  6.8 2.2 copy-start
  9.0 0.7 copy-start.8
  13.7 7.5 %collective-permute-start.14 = (bf16[128,256]{1,0:T(8,128)(2,1)S(1)}, bf16[128,256]{1,0:T(8,128)(2,1)S(1)}, u32[]{:S(2)}, u32[]{:S(2)}) collective-permute-start(bf16[128,256]{1,0:T(8,128)(2,1)S(1)} %norm_pool.1.refs_0_), channel_id=1, source_target_pairs={{0,1},{1,0},{2,3},{3,2},{4,5},{5,4},{6,7},{7,6},{8,9},{9,8},{10,11... | collective-permute-start | bytes 196616 | tf_op jit(solution)/shard_map/ppermute | solution.py:505
  14.1 14.9 %collective-permute-start.15 = (bf16[128,256]{1,0:T(8,128)(2,1)S(1)}, bf16[128,256]{1,0:T(8,128)(2,1)S(1)}, u32[]{:S(2)}, u32[]{:S(2)}) collective-permute-start(bf16[128,256]{1,0:T(8,128)(2,1)S(1)} %norm_pool.1.refs_0_), channel_id=1, source_target_pairs={{0,2},{1,3},{2,0},{3,1},{4,6},{5,7},{6,4},{7,5},{8,10},{9,11},{10,... | collective-permute-start | bytes 196616 | tf_op jit(solution)/shard_map/ppermute | solution.py:505
  15.6 14.2 %collective-permute-start.16 = (bf16[128,256]{1,0:T(8,128)(2,1)S(1)}, bf16[128,256]{1,0:T(8,128)(2,1)S(1)}, u32[]{:S(2)}, u32[]{:S(2)}) collective-permute-start(bf16[128,256]{1,0:T(8,128)(2,1)S(1)} %norm_pool.1.refs_0_), channel_id=1, source_target_pairs={{0,3},{1,2},{2,1},{3,0},{4,7},{5,6},{6,5},{7,4},{8,11},{9,10},{10,... | collective-permute-start | bytes 196616 | tf_op jit(solution)/shard_map/ppermute | solution.py:505
  15.9 2.4 collective-permute-start.2
  17.2 16.3 %collective-permute-start.7 = (bf16[144,256]{1,0:T(8,128)(2,1)S(1)}, bf16[144,256]{1,0:T(8,128)(2,1)S(1)}, u32[]{:S(2)}, u32[]{:S(2)}) collective-permute-start(bf16[144,256]{1,0:T(8,128)(2,1)S(1)} %join_blocks.3.refs_0_), channel_id=1, source_target_pairs={{0,4},{4,8},{8,12},{12,0},{16,20},{20,24},{24,28},{28,16},{32,36},... | collective-permute-start | bytes 221192 | tf_op jit(solution)/shard_map/ppermute | solution.py:492
  18.3 15.2 %collective-permute-start.8 = (bf16[144,256]{1,0:T(8,128)(2,1)S(1)}, bf16[144,256]{1,0:T(8,128)(2,1)S(1)}, u32[]{:S(2)}, u32[]{:S(2)}) collective-permute-start(bf16[144,256]{1,0:T(8,128)(2,1)S(1)} %join_blocks.3.refs_0_), channel_id=1, source_target_pairs={{0,8},{4,12},{8,0},{12,4},{16,24},{20,28},{24,16},{28,20},{32,40},... | collective-permute-start | bytes 221192 | tf_op jit(solution)/shard_map/ppermute | solution.py:492
  21.2 12.3 %collective-permute-start.9 = (bf16[144,256]{1,0:T(8,128)(2,1)S(1)}, bf16[144,256]{1,0:T(8,128)(2,1)S(1)}, u32[]{:S(2)}, u32[]{:S(2)}) collective-permute-start(bf16[144,256]{1,0:T(8,128)(2,1)S(1)} %join_blocks.3.refs_0_), channel_id=1, source_target_pairs={{0,12},{4,0},{8,4},{12,8},{16,28},{20,16},{24,20},{28,24},{32,44},... | collective-permute-start | bytes 221192 | tf_op jit(solution)/shard_map/ppermute | solution.py:492
  22.3 2.2 copy-start.1
  24.5 6.1 %copy-start.2 = (bf16[256,768]{1,0:T(8,128)(2,1)S(1)}, bf16[256,768]{1,0:T(8,128)(2,1)}, u32[]{:S(2)}) copy-start(bf16[256,768]{1,0:T(8,128)(2,1)} %wv_ref.3) | copy-start | bytes 1179652
  29.0 70.7 %collective-permute-start.17 = (bf16[4192,256]{1,0:T(8,128)(2,1)}, bf16[4192,256]{1,0:T(8,128)(2,1)}, u32[]{:S(2)}, u32[]{:S(2)}) collective-permute-start(bf16[4192,256]{1,0:T(8,128)(2,1)} %get-tuple-element.35), channel_id=1, source_target_pairs={{0,4},{4,0},{8,12},{12,8},{16,20},{20,16},{24,28},{28,24},{32,36},... | collective-permute-start | bytes 6438920 | tf_op jit(solution)/shard_map/ppermute | solution.py:488
  29.8 178.3 %collective-permute-start.3 = (bf16[1600,256]{1,0:T(8,128)(2,1)S(1)}, bf16[1600,256]{1,0:T(8,128)(2,1)}, u32[]{:S(2)}, u32[]{:S(2)}) collective-permute-start(bf16[1600,256]{1,0:T(8,128)(2,1)S(1)} %get-tuple-element.25), channel_id=1, source_target_pairs={{0,4},{4,0},{8,12},{12,8},{16,20},{20,16},{24,28},{28,24},{32,36},... | collective-permute-start | bytes 2457608 | tf_op jit(solution)/shard_map/ppermute | solution.py:488
  31.1 1.3 copy-start.5
  32.5 1.1 copy-start.6
  33.6 17.9 %collective-permute-start.10 = (bf16[576,256]{1,0:T(8,128)(2,1)S(1)}, bf16[576,256]{1,0:T(8,128)(2,1)S(1)}, u32[]{:S(2)}, u32[]{:S(2)}) collective-permute-start(bf16[576,256]{1,0:T(8,128)(2,1)S(1)} %join_blocks.4.refs_0_), channel_id=1, source_target_pairs={{0,16},{4,20},{8,24},{12,28},{16,0},{20,4},{24,8},{28,12},{32,48},... | collective-permute-start | bytes 884744 | tf_op jit(solution)/shard_map/ppermute | solution.py:492
  51.5 4.9 %copy-start.3 = (bf16[1152,256]{1,0:T(8,128)(2,1)}, bf16[1152,256]{1,0:T(8,128)(2,1)S(1)}, u32[]{:S(2)}) copy-start(bf16[1152,256]{1,0:T(8,128)(2,1)S(1)} %join_blocks.5.refs_0_.after_ref) | copy-start | bytes 1769476
  51.5 39.8 %collective-permute-start.11 = (bf16[1152,256]{1,0:T(8,128)(2,1)S(1)}, bf16[1152,256]{1,0:T(8,128)(2,1)S(1)}, u32[]{:S(2)}, u32[]{:S(2)}) collective-permute-start(bf16[1152,256]{1,0:T(8,128)(2,1)S(1)} %join_blocks.5.refs_0_.after_ref), channel_id=1, source_target_pairs={{0,32},{4,36},{8,40},{12,44},{16,48},{20,52},{24,56},{28,60},{32,6... | collective-permute-start | bytes 1769480 | tf_op jit(solution)/shard_map/ppermute | solution.py:492
  52.8 38.5 %collective-permute-start.12 = (bf16[1152,256]{1,0:T(8,128)(2,1)S(1)}, bf16[1152,256]{1,0:T(8,128)(2,1)S(1)}, u32[]{:S(2)}, u32[]{:S(2)}) collective-permute-start(bf16[1152,256]{1,0:T(8,128)(2,1)S(1)} %join_blocks.5.refs_0_.after_ref), channel_id=1, source_target_pairs={{0,64},{4,68},{8,72},{12,76},{16,80},{20,84},{24,88},{28,92},{32,9... | collective-permute-start | bytes 1769480 | tf_op jit(solution)/shard_map/ppermute | solution.py:492
  55.3 36.0 %collective-permute-start.13 = (bf16[1152,256]{1,0:T(8,128)(2,1)S(1)}, bf16[1152,256]{1,0:T(8,128)(2,1)S(1)}, u32[]{:S(2)}, u32[]{:S(2)}) collective-permute-start(bf16[1152,256]{1,0:T(8,128)(2,1)S(1)} %join_blocks.5.refs_0_.after_ref), channel_id=1, source_target_pairs={{0,96},{4,100},{8,104},{12,108},{16,112},{20,116},{24,120},{28,124... | collective-permute-start | bytes 1769480 | tf_op jit(solution)/shard_map/ppermute | solution.py:492
  91.3 1.1 copy-start.4
  96.0 0.8 copy-start.7

commit v2 on v1

--- a/solution.py
+++ b/solution.py
@@ -21,8 +21,7 @@
 HIGH = 2.0 ** 100
 NEG = -1e30
 MB = 1024 * 1024
-PARTS = ((0, 6144, 4192), (6144, 2048, 1600))
-MARK = 16
+LIMIT = 5424
 
 
 def params(limit):
@@ -61,7 +60,7 @@
     pooled_ref[...] = (dot(pick, normed) * (1.0 / math.sqrt(WIN))).astype(BF)
 
 
-def pool_rows(x, gain, rows=1024):
+def pool_rows(x, gain, rows=2048):
     pixels = x.shape[0]
     return pl.pallas_call(
         pool_body,
@@ -72,17 +71,15 @@
         ],
         out_specs=pl.BlockSpec((rows // WIN, C), lambda i: (i, 0)),
         out_shape=jax.ShapeDtypeStruct((pixels // WIN, C), BF),
-        compiler_params=params(48),
+        compiler_params=params(60),
         cost_estimate=pl.CostEstimate(flops=2 * pixels * C * C, bytes_accessed=4 * pixels * C, transcendentals=0),
         name="norm_pool",
     )(x, gain)
 
 
-def pack_body(first, offset_ref, x_ref, main_ref, rest_ref, packed, at_row):
+def pack_body(offset_ref, x_ref, main_ref, rest_ref, packed, at_row):
     step = pl.program_id(0)
     count = x_ref.shape[0] // WIN
-    limit = main_ref.shape[0]
-
     @pl.when(step == 0)
     def _():
         at_row[0] = 0
@@ -90,36 +87,36 @@
     start = at_row[0]
     for w in range(count):
         packed[pl.ds(pl.multiple_of(start, 8), WIN), :] = x_ref[w * WIN:w * WIN + WIN, :].astype(F32)
-        start = start + sent(offset_ref[first + step * count + w])
+        start = start + sent(offset_ref[step * count + w])
     at_row[0] = start
 
     @pl.when(step == pl.num_programs(0) - 1)
     def _():
-        main_ref[...] = packed[0:limit, :].astype(BF)
-
-        @pl.when(start > limit)
+        main_ref[...] = packed[0:LIMIT, :].astype(BF)
+
+        @pl.when(start > LIMIT)
         def _():
-            rest_ref[...] = packed[limit:, :].astype(BF)
-
-
-def pack(part, offsets, x, rows=1024):
-    first, run, limit = part
+            rest_ref[...] = packed[LIMIT:, :].astype(BF)
+
+
+def pack(offsets, x, rows=4096):
+    pixels = x.shape[0]
     whole = lambda i, s: (0, 0)
     return pl.pallas_call(
-        functools.partial(pack_body, first // WIN),
+        pack_body,
         grid_spec=pltpu.PrefetchScalarGridSpec(
             num_scalar_prefetch=1,
-            grid=(run // rows,),
-            in_specs=[pl.BlockSpec((rows, C), lambda i, s: (first // rows + i, 0))],
-            out_specs=[pl.BlockSpec((limit, C), whole), pl.BlockSpec((run - limit, C), whole)],
-            scratch_shapes=[pltpu.VMEM((run, C), F32), pltpu.SMEM((1,), jnp.int32)],
+            grid=(pixels // rows,),
+            in_specs=[pl.BlockSpec((rows, C), lambda i, s: (i, 0))],
+            out_specs=[pl.BlockSpec((LIMIT, C), whole), pl.BlockSpec((pixels - LIMIT, C), whole)],
+            scratch_shapes=[pltpu.VMEM((pixels, C), F32), pltpu.SMEM((1,), jnp.int32)],
         ),
         out_shape=[
-            jax.ShapeDtypeStruct((limit, C), BF),
-            jax.ShapeDtypeStruct((run - limit, C), BF),
-        ],
-        compiler_params=params(32),
-        cost_estimate=pl.CostEstimate(flops=0, bytes_accessed=10 * run * C, transcendentals=0),
+            jax.ShapeDtypeStruct((LIMIT, C), BF),
+            jax.ShapeDtypeStruct((pixels - LIMIT, C), BF),
+        ],
+        compiler_params=params(60),
+        cost_estimate=pl.CostEstimate(flops=0, bytes_accessed=10 * pixels * C, transcendentals=0),
         name="pack_rows",
     )(offsets, x)
 
@@ -174,95 +171,101 @@
     )(*blocks, w_qkv, w_qkv)
 
 
-def coarse_body(x_ref, gain_ref, wq_ref, kt_ref, vo_ref, after_ref, q_ref, acc_ref):
-    del after_ref
-    normed = norm_rows(x_ref[...].astype(F32), gain_ref[...])
-    q = (dot(normed, wq_ref[...]) * SCALE).astype(BF)
+def coarse_body(x_ref, next_ref, gain_ref, wq_ref, kt_ref, vo_ref, *refs):
+    q_ref, acc_ref, held = refs[-3:]
+    step = pl.program_id(0)
+
+    def queries(ref):
+        return (dot(norm_rows(ref[...].astype(F32), gain_ref[...]), wq_ref[...]) * SCALE).astype(BF)
+
+    @pl.when(step == 0)
+    def _():
+        held[...] = queries(x_ref)
+
+    q = held[...]
     q_ref[...] = q
     weights = []
     for half in range(2):
         heads = range(half * HALF, half * HALF + HALF)
         mine = q[:, half * 128:half * 128 + 128]
         weights.append(jnp.concatenate([exp2(dot(mine, kt_ref[h])).astype(BF) for h in heads], axis=1))
-    for half in range(2):
-        acc_ref[:, half * C:half * C + C] = dot(weights[half], vo_ref[half])
-
-
-def coarse(part, x, gain, w_qkv, kt, vo, after, rows=1024):
-    first, pixels, _ = part
-    steps = pixels // rows
+    acc_ref[:, 0:C] = dot(weights[0], vo_ref[0])
+    acc_ref[:, C:2 * C] = dot(weights[1], vo_ref[1])
+    held[...] = queries(next_ref)
+
+
+def coarse(first, run, x, gain, w_qkv, kt, vo, after, given=(), rows=1024):
+    pixels = x.shape[0]
+    steps = run // rows
+    base = first // rows
     count = kt.shape[2]
     return pl.pallas_call(
         coarse_body,
         grid=(steps,),
         in_specs=[
-            pl.BlockSpec((rows, C), lambda i: (first // rows + i, 0)),
+            pl.BlockSpec((rows, C), lambda i: (base, 0)),
+            pl.BlockSpec((rows, C), lambda i: (base + jnp.minimum(i + 1, steps - 1), 0)),
             pl.BlockSpec((1, C), lambda i: (0, 0)),
             pl.BlockSpec((C, C), lambda i: (0, 0)),
             pl.BlockSpec(kt.shape, lambda i: (0, 0, 0)),
             pl.BlockSpec(vo.shape, lambda i: (0, 0, 0)),
-            pl.BlockSpec(memory_space=pl.ANY),
-        ],
+        ]
+        + [pl.BlockSpec(memory_space=pl.ANY)] * (1 + len(given)),
         out_specs=[
-            pl.BlockSpec((rows, C), lambda i: (i, 0)),
-            pl.BlockSpec((rows, 2 * C), lambda i: (i, 0)),
+            pl.BlockSpec((rows, C), lambda i: (base + i, 0)),
+            pl.BlockSpec((rows, 2 * C), lambda i: (base + i, 0)),
         ],
         out_shape=[
             jax.ShapeDtypeStruct((pixels, C), BF),
             jax.ShapeDtypeStruct((pixels, 2 * C), F32),
         ],
+        scratch_shapes=[pltpu.VMEM((rows, C), BF)],
+        input_output_aliases={7: 0, 8: 1} if given else {},
         compiler_params=params(60),
         cost_estimate=pl.CostEstimate(
-            flops=4 * pixels * HEADS * count * C, bytes_accessed=10 * pixels * C, transcendentals=pixels * HEADS * count
+            flops=4 * run * HEADS * count * C, bytes_accessed=10 * run * C, transcendentals=run * HEADS * count
         ),
         name="group_attention",
-    )(x, gain, w_qkv, kt, vo, after)
-
-
-def seam_body(index_ref, *refs):
-    out_ref, mark_ref = refs[-2:]
+    )(x, x, gain, w_qkv, kt, vo, after, *given)
+
+
+def seam_body(index_ref, pool_ref, out_ref):
     rows = index_ref.shape[0]
+    step = 1024
     total = jnp.zeros((rows, C), F32)
-    lo = 0
-    marks = jnp.zeros((MARK, 128), F32)
-    for ref in refs[:-2]:
-        step = ref.shape[0]
-        for at in range(step // 8 - MARK, step, step // 8):
-            marks = jnp.maximum(marks, ref[at:at + MARK, 0:128].astype(F32))
+    for lo in range(0, pool_ref.shape[0], step):
         at = lax.broadcasted_iota(jnp.int32, (rows, step), 1) + lo
         pick = jnp.where(at == index_ref[...], 1.0, 0.0).astype(BF)
-        total = total + dot(pick, ref[...])
-        lo += step
+        total = total + dot(pick, pool_ref[lo:lo + step])
     out_ref[...] = total.astype(BF)
-    mark_ref[...] = marks
-
-
-def seam(index, pools, rows=256):
+
+
+def seam(index, pool, rows=256):
     count = index.shape[0]
     return pl.pallas_call(
         seam_body,
         grid=(count // rows,),
-        in_specs=[pl.BlockSpec((rows, 1), lambda i: (i, 0))]
-        + [pl.BlockSpec(pool.shape, lambda i: (0, 0)) for pool in pools],
-        out_specs=[pl.BlockSpec((rows, C), lambda i: (i, 0)), pl.BlockSpec((MARK, 128), lambda i: (0, 0))],
-        out_shape=[jax.ShapeDtypeStruct((count, C), BF), jax.ShapeDtypeStruct((MARK, 128), F32)],
+        in_specs=[
+            pl.BlockSpec((rows, 1), lambda i: (i, 0)),
+            pl.BlockSpec(pool.shape, lambda i: (0, 0)),
+        ],
+        out_specs=pl.BlockSpec((rows, C), lambda i: (i, 0)),
+        out_shape=jax.ShapeDtypeStruct((count, C), BF),
         compiler_params=params(48),
         name="seam_rows",
-    )(index, *pools)
+    )(index, pool)
 
 
 def window_body(
-    first, offset_ref, x_ref, main_ref, rest_ref, q_ref, acc_ref, seam_ref, gain_ref, wk_ref, wv_ref, wo_ref,
-    kt_hbm, vo_hbm, given_ref, out_ref, kbd, vbd, vsm, ksm, sums, packed, wkt_ref, kt_ref, vo_ref, at_row, done,
+    offset_ref, x_ref, main_ref, rest_hbm, q_ref, acc_ref, seam_ref, gain_ref, wk_ref, wv_ref, wo_ref,
+    kt_hbm, vo_hbm, out_ref, kbd, vbd, vsm, ksm, sums, packed, rest_ref, wkt_ref, kt_ref, vo_ref, at_row, done,
 ):
-    del given_ref
-    limit = main_ref.shape[0]
     rows = x_ref.shape[0]
     count = rows // WIN
     pairs = count // 2
     near = 2 * SEAM
     step = pl.program_id(0)
-    first_window = first + step * count
+    first_window = step * count
 
     def lanes_of(k):
         return jnp.where(lax.broadcasted_iota(jnp.int32, (1, 128), 1) // DIM == k, 1.0, 0.0).astype(BF)
@@ -273,14 +276,17 @@
     def _():
         at_row[0] = 0
         wkt_ref[...] = wk_ref[...].astype(F32).T.astype(BF)
-        packed[0:limit, :] = main_ref[...].astype(F32)
+        packed[0:LIMIT, :] = main_ref[...].astype(F32)
 
         def add(w, total):
-            return total + sent(offset_ref[first + w])
-
-        @pl.when(lax.fori_loop(0, pl.num_programs(0) * count, add, 0) > limit)
+            return total + sent(offset_ref[w])
+
+        @pl.when(lax.fori_loop(0, pl.num_programs(0) * count, add, 0) > LIMIT)
         def _():
-            packed[limit:, :] = rest_ref[...].astype(F32)
+            copy = pltpu.make_async_copy(rest_hbm, rest_ref, done.at[0])
+            copy.start()
+            copy.wait()
+            packed[LIMIT:, :] = rest_ref[...].astype(F32)
 
         kbd[...] = jnp.zeros(kbd.shape, BF)
         vsm[...] = jnp.zeros(vsm.shape, BF)
@@ -423,42 +429,39 @@
         lax.fori_loop(0, pairs, exact, 0)
 
 
-def window(part, offsets, x, main, rest, q, acc, seam_rows, gain, w_qkv, wo, kt, vo, given, rows=1024):
-    first, run, _ = part
+def window(offsets, x, main, rest, q, acc, seam_rows, gain, w_qkv, wo, kt, vo, rows=1024):
     pixels = x.shape[0]
-    steps = run // rows
     count = rows // WIN
-    whole = lambda i, s: (first // rows + i, 0)
     row = lambda i, s: (i, 0)
     fixed = lambda i, s: (0, 0)
     return pl.pallas_call(
-        functools.partial(window_body, first // WIN),
+        window_body,
         grid_spec=pltpu.PrefetchScalarGridSpec(
             num_scalar_prefetch=1,
-            grid=(steps,),
+            grid=(pixels // rows,),
             in_specs=[
-                pl.BlockSpec((rows, C), whole),
+                pl.BlockSpec((rows, C), row),
                 pl.BlockSpec(main.shape, fixed),
-                pl.BlockSpec(rest.shape, fixed),
+                pl.BlockSpec(memory_space=pl.ANY),
                 pl.BlockSpec((rows, C), row),
                 pl.BlockSpec((rows, 2 * C), row),
-                pl.BlockSpec((count * SEAM, C), whole),
+                pl.BlockSpec((count * SEAM, C), row),
                 pl.BlockSpec((1, C), fixed),
                 pl.BlockSpec((C, C), lambda i, s: (0, 1)),
                 pl.BlockSpec((C, C), lambda i, s: (0, 2)),
                 pl.BlockSpec((C, C), fixed),
                 pl.BlockSpec(memory_space=pl.ANY),
                 pl.BlockSpec(memory_space=pl.ANY),
-                pl.BlockSpec(memory_space=pl.ANY),
             ],
-            out_specs=pl.BlockSpec((rows, C), whole),
+            out_specs=pl.BlockSpec((rows, C), row),
             scratch_shapes=[
                 pltpu.VMEM((count, 2, 128, C), BF),
                 pltpu.VMEM((count, 2, HALF * WIN, C), BF),
                 pltpu.VMEM((count // 2, 128, 2 * C), BF),
                 pltpu.VMEM((count // 2, C, 128), BF),
                 pltpu.VMEM((rows, 2 * C), F32),
-                pltpu.VMEM((run, C), F32),
+                pltpu.VMEM((pixels, C), F32),
+                pltpu.VMEM(rest.shape, BF),
                 pltpu.VMEM((C, C), BF),
                 pltpu.VMEM(kt.shape, BF),
                 pltpu.VMEM(vo.shape, BF),
@@ -467,13 +470,12 @@
             ],
         ),
         out_shape=jax.ShapeDtypeStruct((pixels, C), BF),
-        input_output_aliases={13: 0} if first else {},
         compiler_params=params(60),
         cost_estimate=pl.CostEstimate(
-            flops=40 * run * C * C, bytes_accessed=20 * run * C, transcendentals=0
+            flops=40 * pixels * C * C, bytes_accessed=20 * pixels * C, transcendentals=0
         ),
         name="window_attention",
-    )(offsets, x, main, rest, q, acc, seam_rows, gain, w_qkv, w_qkv, wo, kt, vo, given)
+    )(offsets, x, main, rest, q, acc, seam_rows, gain, w_qkv, w_qkv, wo, kt, vo)
 
 
 def rotation(dx, dz, dy):
@@ -495,10 +497,9 @@
 def place_in_pool(index, windows):
     face, local = index // windows, index % windows
     me = lax.axis_index("face")
-    dx = (me // 8 - face // 8) % 4
     dz = (me // 4 - face // 4) % 2
     dy = (me - face) % 4
-    return ((dx * 2 + dz) * 4 + dy) * (windows + MARK) + local
+    return ((face // 8 * 2 + dz) * 4 + dy) * windows + local
 
 
 def by_sub(x, k):
@@ -506,36 +507,27 @@
 
 
 def local(pixel_state, norm1_gain, w_qkv, w_out, shift_offsets, seam_table):
+    pixels = pixel_state.shape[0]
     gain = norm1_gain.reshape(1, C)
     asked = partner(shift_offsets)
-    lengths = sent(shift_offsets)
-    over = False
-    for first, run, limit in PARTS:
-        over = jnp.logical_or(over, lengths[first // WIN:(first + run) // WIN].sum() > limit)
-    mark = jnp.broadcast_to(over.astype(BF), (MARK, C))
-    mark = functools.reduce(jnp.maximum, [by_sub(mark, k) for k in (1, 2, 3)], mark)
+    more = (jnp.maximum(sent(shift_offsets).sum(), sent(asked).sum()) > LIMIT).astype(jnp.int32)
     pooled = pool_rows(pixel_state, gain)
     groups = [pooled] + [by_sub(pooled, k) for k in (1, 2, 3)]
-    columns = turned(join(pooled, mark), [(0, 0, 1), (0, 0, 2), (0, 0, 3)])
-    mains, rests = zip(*[pack(part, asked, pixel_state) for part in PARTS])
-    mains = [partner(main) for main in mains]
+    columns = turned(pooled, [(0, 0, 1), (0, 0, 2), (0, 0, 3)])
+    main, rest = pack(asked, pixel_state)
+    main = partner(main)
     planes = turned(join(*columns), [(0, 1, 0)])
     cube = join(*planes)
-    pools = turned(cube, [(1, 0, 0), (2, 0, 0), (3, 0, 0)])
+    lines = [[x * 8 + rest for x in range(4)] for rest in range(8)]
+    pool = lax.all_gather(cube, "face", axis=0, tiled=True, axis_index_groups=lines)
     kt, vo = group(groups, w_qkv)
-    late = coarse(PARTS[1], pixel_state, gain, w_qkv, kt, vo, gain)
-    early = coarse(PARTS[0], pixel_state, gain, w_qkv, kt, vo, cube)
+    split = pixels // 4
+    sums = coarse(0, split, pixel_state, gain, w_qkv, kt, vo, gain, rows=512)
+    q, acc = coarse(split, pixels - split, pixel_state, gain, w_qkv, kt, vo, cube, sums)
     index = place_in_pool(seam_table, pooled.shape[0]).reshape(-1, 1)
-    seam_rows, marks = seam(index, pools)
-    rests = lax.cond(
-        marks[0, 0] > 0.0, lambda r: [partner(x) for x in r], lambda r: [jnp.zeros_like(x) for x in r], list(rests)
-    )
-    out = pixel_state
-    for part, main, rest, (q, acc) in zip(PARTS, mains, rests, (early, late)):
-        out = window(
-            part, shift_offsets, pixel_state, main, rest, q, acc, seam_rows, gain, w_qkv, w_out, kt, vo, out
-        )
-    return out
+    seam_rows = seam(index, pool)
+    _, rest = lax.while_loop(lambda c: c[0] > 0, lambda c: (c[0] - 1, partner(c[1])), (more, rest))
+    return window(shift_offsets, pixel_state, main, rest, q, acc, seam_rows, gain, w_qkv, w_out, kt, vo)
 
 
 def solution(mesh):

time: 249 us -> 249 us (level)
  between operations: 2.32 us -> 14.8 us
  waiting for transfers between devices: 0.84 us -> 7.57 us
  local copies, waits for them, and re-layouts: 11.9 us -> 5.87 us
  starting transfers between devices: 21.1 us -> 15.1 us
  Pallas kernels: 209 us -> 204 us
    ppermute x3 -> x2, waiting for transfers between devices: 0.8 us -> 7.54 us  [partner(): return lax.ppermute(x, 'face', [(i, i ^ 1) for i in range(32)])]
    unnamed x22 -> x20, local copies, waits for them, and re-layouts: 9.33 us -> 5.59 us
    pallas_call x4 -> x2, Pallas kernels: 152 us -> 148 us  [the longest x1 143 us: window(): pl.pallas_call(window_body, grid_spec=pltpu.PrefetchScalarGridSpec(num_sc...]
    ppermute x7 -> x4, starting transfers between devices: 12.8 us -> 9.2 us  [turned(): return [block] + [lax.ppermute(block, 'face', rotation(*s)) for s in steps]]
    pallas_call x2, Pallas kernels: 48.8 us -> 45.4 us  [coarse(): pl.pallas_call(coarse_body, grid=(steps,), in_specs=[pl.BlockSpec((rows,...]
    ppermute x6 -> x3, starting transfers between devices: 5.46 us -> 5.51 us  [by_sub(): return lax.ppermute(x, 'sub', [(i, i ^ k) for i in range(4)])]
  transfers between devices with their start and end apart: 16 -> 10, of which waited for: 1 -> 1; matrix products, arithmetic and copies ran while one was open for 1% -> 1% of each run, Pallas kernels for 69% -> 22%
where the time goes in v2:
time: 249 us
  Pallas kernels  204 us (82%)
  starting transfers between devices  15.1 us (6%)
  between operations  14.8 us (6%)
  waiting for transfers between devices  7.57 us (3%)
  local copies, waits for them, and re-layouts  5.87 us (2%)
    pallas_call x1, Pallas kernels, window(): pl.pallas_call(window_body, grid_spec=pltpu.PrefetchScalarGridSpec(num_sc...  143 us
    pallas_call x2, Pallas kernels, coarse(): pl.pallas_call(coarse_body, grid=(steps,), in_specs=[pl.BlockSpec((rows,...  45.4 us
    ppermute x4, starting transfers between devices, turned(): return [block] + [lax.ppermute(block, 'face', rotation(*s)) for s in steps]  9.2 us
    ppermute x2, waiting for transfers between devices, partner(): return lax.ppermute(x, 'face', [(i, i ^ 1) for i in range(32)])  7.54 us
    pallas_call x1, Pallas kernels, pool_rows(): pl.pallas_call(pool_body, grid=(pixels // rows,), in_specs=[pl.BlockSpec(...  5.87 us
    unnamed x20, local copies, waits for them, and re-layouts  5.59 us
    ppermute x3, starting transfers between devices, by_sub(): return lax.ppermute(x, 'sub', [(i, i ^ k) for i in range(4)])  5.51 us
    pallas_call x1, Pallas kernels, pack(): pl.pallas_call(pack_body, grid_spec=pltpu.PrefetchScalarGridSpec(num_scal...  5.4 us
  transfers between devices with their start and end apart: 10, of which 1 were waited for; matrix products, arithmetic and copies ran while one was open for 1% of the time, Pallas kernels for 22%

profile of v2, /device:TPU:1, one launch (start us, length us, event | category | flops | bytes accessed | tf_op | source)
XLA Modules:
  0.0 248.6 jit_solution(7600950811337524703)
XLA Ops:
  6.5 0.0 copy-start.9
  6.5 0.0 copy-start.7
  6.5 0.0 all-gather.2.cloned.1.call-start
  6.5 5.9 %norm_pool.1.refs_0_ = bf16[128,256]{1,0:T(8,128)(2,1)} custom-call(bf16[8192,256]{1,0:T(8,128)(2,1)} %x_ref.9, f32[1,256]{1,0:T(1,128)} %bitcast.1), custom_call_target="tpu_custom_call" | custom-call | flops 1073741824 | bytes 8388608 | tf_op jit(solution)/shard_map/norm_pool/pallas_call | solution.py:65
  12.4 0.0 copy-start.1
  12.4 2.1 collective-permute-start.6
  14.5 2.6 %collective-permute-start.7 = (bf16[128,256]{1,0:T(8,128)(2,1)}, bf16[128,256]{1,0:T(8,128)(2,1)S(1)}, u32[]{:S(2)}, u32[]{:S(2)}) collective-permute-start(bf16[128,256]{1,0:T(8,128)(2,1)} %norm_pool.1.refs_0_), channel_id=1, source_target_pairs={{0,8},{4,12},{8,0},{12,4},{16,24},{20,28},{24,16},{28,20},{32,40},... | collective-permute-start | bytes 196616 | tf_op jit(solution)/shard_map/ppermute | solution.py:494
  17.2 1.1 collective-permute-start.8
  18.2 1.5 collective-permute-start.3
  19.8 1.6 collective-permute-start.4
  21.4 0.0 collective-permute-done.6.refs_1_
  21.4 0.0 copy-done.9
  21.4 0.4 collective-permute-start.1
  21.8 0.0 collective-permute-done.7.refs_2_
  21.8 0.0 collective-permute-done.8.refs_3_
  21.8 0.0 copy-start.2
  21.8 0.8 copy-done.2
  22.6 0.0 copy-start.3
  22.7 3.4 %collective-permute-start.9 = (bf16[512,256]{1,0:T(8,128)(2,1)S(1)}, bf16[512,256]{1,0:T(8,128)(2,1)S(1)}, u32[]{:S(2)}, u32[]{:S(2)}) collective-permute-start(bf16[512,256]{1,0:T(8,128)(2,1)S(1)} %join_blocks.2.refs_0_), channel_id=1, source_target_pairs={{0,16},{4,20},{8,24},{12,28},{16,0},{20,4},{24,8},{28,12},{32,48},... | collective-permute-start | bytes 786440 | tf_op jit(solution)/shard_map/ppermute | solution.py:494
  26.0 0.0 copy-done.7
  26.1 0.6 multiply_reduce_fusion.1
  26.7 0.1 copy.10
  26.8 0.2 reshape.8.index_ref
  27.0 2.4 collective-permute-start.5
  29.4 0.0 collective-permute-done.1.offset_ref
  29.4 0.0 copy-start.8
  29.4 0.7 multiply_reduce_fusion
  31.4 0.0 copy-done.8
  31.4 5.4 %pack_rows.1 = (bf16[5424,256]{1,0:T(8,128)(2,1)}, bf16[2768,256]{1,0:T(8,128)(2,1)S(1)}) custom-call(s32[128]{0:T(128)} %copy-done.8, bf16[8192,256]{1,0:T(8,128)(2,1)} %x_ref.9), custom_call_target="tpu_custom_call" | custom-call | bytes 20971520 | tf_op jit(solution)/shard_map/pack_rows/pallas_call | solution.py:105
  36.8 0.0 collective-permute-start.2
  36.9 0.0 collective-permute-done.3.refs_1_
  36.9 0.0 collective-permute-done.4.refs_2_
  36.9 0.0 collective-permute-done.5.refs_3_
  36.9 0.0 copy-done.1
  36.9 0.0 copy-done.3
  36.9 0.5 group_keys_values.1
  37.4 0.0 copy-start.5
  37.4 1.4 copy-done.5
  38.8 0.0 copy-start.6
  38.8 1.0 copy-done.6
  39.8 0.0 collective-permute-done.9.refs_1_
  39.8 0.9 join_blocks.3.refs_0_
  40.7 0.0 all-gather.2.cloned.1.call-update
  40.7 13.2 %group_attention.2 = (bf16[8192,256]{1,0:T(8,128)(2,1)}, f32[8192,512]{1,0:T(8,128)}) custom-call(bf16[8192,256]{1,0:T(8,128)(2,1)} %x_ref.9, bf16[8192,256]{1,0:T(8,128)(2,1)} %x_ref.9, f32[1,256]{1,0:T(1,128)} %bitcast.2, bf16[256,768]{1,0:T(8,128)(2,1)} %wv_ref.1, bf16[8,128,512]{2,1,0:T(8,128)(2,1)} %copy-done.6, bf16[2,2048,256]{2,1,0:T(8,128)(2,1)} %copy-done.5, ...), custom_call_target="tpu_custom_call" | custom-call | flops 8589934592 | bytes 5242880 | tf_op jit(solution)/shard_map/group_attention/pallas_call | solution.py:202
  53.9 32.2 %group_attention.3 = (bf16[8192,256]{1,0:T(8,128)(2,1)}, f32[8192,512]{1,0:T(8,128)}) custom-call(bf16[8192,256]{1,0:T(8,128)(2,1)} %x_ref.9, bf16[8192,256]{1,0:T(8,128)(2,1)} %x_ref.9, f32[1,256]{1,0:T(1,128)} %bitcast.4, bf16[256,768]{1,0:T(8,128)(2,1)} %wv_ref.1, bf16[8,128,512]{2,1,0:T(8,128)(2,1)} %copy-done.6, ...), custom_call_target="tpu_custom_call", output_to_operand_aliasing={{0}: (7, {}), {1}: (8, {})} | custom-call | flops 25769803776 | bytes 15728640 | tf_op jit(solution)/shard_map/group_attention/pallas_call | solution.py:202
  86.1 0.0 all-gather.2.cloned.1.call-done.pool_ref
  86.1 0.0 copy-start
  86.1 1.6 copy-done
  87.7 3.0 %seam_rows.1.seam_ref = bf16[1024,256]{1,0:T(8,128)(2,1)S(1)} custom-call(s32[1024,1]{1,0:T(8,128)S(1)} %reshape.8.index_ref, bf16[4096,256]{1,0:T(8,128)(2,1)S(1)} %copy-done), custom_call_target="tpu_custom_call" | custom-call | tf_op jit(solution)/shard_map/seam_rows/pallas_call | solution.py:245
  90.7 0.0 copy-start.4
  90.8 0.8 copy-done.4
  91.5 7.5 %collective-permute-done.2.main_ref = bf16[5424,256]{1,0:T(8,128)(2,1)} collective-permute-done((bf16[5424,256]{1,0:T(8,128)(2,1)}, bf16[5424,256]{1,0:T(8,128)(2,1)}, u32[]{:S(2)}, u32[]{:S(2)}) %collective-permute-start.2) | collective-permute-done | bytes 2777120 | tf_op jit(solution)/shard_map/ppermute | solution.py:490
  99.1 142.7 %window_attention.1 = bf16[8192,256]{1,0:T(8,128)(2,1)} custom-call(s32[128]{0:T(128)} %offset_ref.1, bf16[8192,256]{1,0:T(8,128)(2,1)} %x_ref.9, bf16[5424,256]{1,0:T(8,128)(2,1)} %collective-permute-done.2.main_ref, bf16[2768,256]{1,0:T(8,128)(2,1)S(1)} %get-tuple-element.27.rest_hbm, bf16[8192,256]{1,0:T(8,128)(2,1)} %get-tuple-element.32.q_ref, ...), custom_call_target="tpu_custom_call" | custom-call | flops 21474836480 | bytes 41943040 | tf_op jit(solution)/shard_map/window_attention/pallas_call | solution.py:437
  (3 shorter events, 0.1 us)
Async XLA Ops:
  6.5 14.9 %copy-start.9 = (s32[128]{0:T(128)S(1)}, s32[128]{0:T(128)}, u32[]{:S(2)}) copy-start(s32[128]{0:T(128)} %offset_ref.1) | copy-start | bytes 1540
  6.5 19.5 %copy-start.7 = (s32[128,8]{0,1:T(8,128)S(1)}, s32[128,8]{0,1:T(8,128)}, u32[]{:S(2)}) copy-start(s32[128,8]{0,1:T(8,128)} %param.13) | copy-start | bytes 12292
  6.5 79.6 %all-gather.2.cloned.1.call-start = ((), (), s32[]{:S(2)}) async-start(), calls=%async_computation | async-start | bytes 2621440 | tf_op jit(solution)/shard_map/all_gather | solution.py:522
  12.4 24.5 %copy-start.1 = (bf16[256,768]{1,0:T(8,128)(2,1)S(1)}, bf16[256,768]{1,0:T(8,128)(2,1)}, u32[]{:S(2)}) copy-start(bf16[256,768]{1,0:T(8,128)(2,1)} %wv_ref.1) | copy-start | bytes 1179652
  12.4 9.0 %collective-permute-start.6 = (bf16[128,256]{1,0:T(8,128)(2,1)}, bf16[128,256]{1,0:T(8,128)(2,1)S(1)}, u32[]{:S(2)}, u32[]{:S(2)}) collective-permute-start(bf16[128,256]{1,0:T(8,128)(2,1)} %norm_pool.1.refs_0_), channel_id=1, source_target_pairs={{0,4},{4,8},{8,12},{12,0},{16,20},{20,24},{24,28},{28,16},{32,36},... | collective-permute-start | bytes 196616 | tf_op jit(solution)/shard_map/ppermute | solution.py:494
  14.5 7.3 %collective-permute-start.7 = (bf16[128,256]{1,0:T(8,128)(2,1)}, bf16[128,256]{1,0:T(8,128)(2,1)S(1)}, u32[]{:S(2)}, u32[]{:S(2)}) collective-permute-start(bf16[128,256]{1,0:T(8,128)(2,1)} %norm_pool.1.refs_0_), channel_id=1, source_target_pairs={{0,8},{4,12},{8,0},{12,4},{16,24},{20,28},{24,16},{28,20},{32,40},... | collective-permute-start | bytes 196616 | tf_op jit(solution)/shard_map/ppermute | solution.py:494
  17.2 4.6 %collective-permute-start.8 = (bf16[128,256]{1,0:T(8,128)(2,1)}, bf16[128,256]{1,0:T(8,128)(2,1)S(1)}, u32[]{:S(2)}, u32[]{:S(2)}) collective-permute-start(bf16[128,256]{1,0:T(8,128)(2,1)} %norm_pool.1.refs_0_), channel_id=1, source_target_pairs={{0,12},{4,0},{8,4},{12,8},{16,28},{20,16},{24,20},{28,24},{32,44},... | collective-permute-start | bytes 196616 | tf_op jit(solution)/shard_map/ppermute | solution.py:494
  18.2 18.6 %collective-permute-start.3 = (bf16[128,256]{1,0:T(8,128)(2,1)}, bf16[128,256]{1,0:T(8,128)(2,1)S(1)}, u32[]{:S(2)}, u32[]{:S(2)}) collective-permute-start(bf16[128,256]{1,0:T(8,128)(2,1)} %norm_pool.1.refs_0_), channel_id=1, source_target_pairs={{0,1},{1,0},{2,3},{3,2},{4,5},{5,4},{6,7},{7,6},{8,9},{9,8},{10,11... | collective-permute-start | bytes 196616 | tf_op jit(solution)/shard_map/ppermute | solution.py:506
  19.8 17.1 %collective-permute-start.4 = (bf16[128,256]{1,0:T(8,128)(2,1)}, bf16[128,256]{1,0:T(8,128)(2,1)S(1)}, u32[]{:S(2)}, u32[]{:S(2)}) collective-permute-start(bf16[128,256]{1,0:T(8,128)(2,1)} %norm_pool.1.refs_0_), channel_id=1, source_target_pairs={{0,2},{1,3},{2,0},{3,1},{4,6},{5,7},{6,4},{7,5},{8,10},{9,11},{10,... | collective-permute-start | bytes 196616 | tf_op jit(solution)/shard_map/ppermute | solution.py:506
  21.4 8.0 %collective-permute-start.1 = (s32[128]{0:T(128)S(1)}, s32[128]{0:T(128)S(1)}, u32[]{:S(2)}, u32[]{:S(2)}) collective-permute-start(s32[128]{0:T(128)S(1)} %copy-done.9), channel_id=1, source_target_pairs={{0,4},{4,0},{8,12},{12,8},{16,20},{20,16},{24,28},{28,24},{32,36},... | collective-permute-start | bytes 1544 | tf_op jit(solution)/shard_map/ppermute | solution.py:490
  21.8 0.8 copy-start.2
  22.6 14.2 %copy-start.3 = (bf16[128,256]{1,0:T(8,128)(2,1)S(1)}, bf16[128,256]{1,0:T(8,128)(2,1)}, u32[]{:S(2)}) copy-start(bf16[128,256]{1,0:T(8,128)(2,1)} %norm_pool.1.refs_0_) | copy-start | bytes 196612
  22.7 17.1 %collective-permute-start.9 = (bf16[512,256]{1,0:T(8,128)(2,1)S(1)}, bf16[512,256]{1,0:T(8,128)(2,1)S(1)}, u32[]{:S(2)}, u32[]{:S(2)}) collective-permute-start(bf16[512,256]{1,0:T(8,128)(2,1)S(1)} %join_blocks.2.refs_0_), channel_id=1, source_target_pairs={{0,16},{4,20},{8,24},{12,28},{16,0},{20,4},{24,8},{28,12},{32,48},... | collective-permute-start | bytes 786440 | tf_op jit(solution)/shard_map/ppermute | solution.py:494
  27.0 9.9 %collective-permute-start.5 = (bf16[128,256]{1,0:T(8,128)(2,1)}, bf16[128,256]{1,0:T(8,128)(2,1)S(1)}, u32[]{:S(2)}, u32[]{:S(2)}) collective-permute-start(bf16[128,256]{1,0:T(8,128)(2,1)} %norm_pool.1.refs_0_), channel_id=1, source_target_pairs={{0,3},{1,2},{2,1},{3,0},{4,7},{5,6},{6,5},{7,4},{8,11},{9,10},{10,... | collective-permute-start | bytes 196616 | tf_op jit(solution)/shard_map/ppermute | solution.py:506
  29.4 2.0 copy-start.8
  36.8 62.3 %collective-permute-start.2 = (bf16[5424,256]{1,0:T(8,128)(2,1)}, bf16[5424,256]{1,0:T(8,128)(2,1)}, u32[]{:S(2)}, u32[]{:S(2)}) collective-permute-start(bf16[5424,256]{1,0:T(8,128)(2,1)} %get-tuple-element.25), channel_id=1, source_target_pairs={{0,4},{4,0},{8,12},{12,8},{16,20},{20,16},{24,28},{28,24},{32,36},... | collective-permute-start | bytes 8331272 | tf_op jit(solution)/shard_map/ppermute | solution.py:490
  37.4 1.4 copy-start.5
  38.8 1.0 copy-start.6
  86.1 1.6 copy-start
  90.7 0.8 copy-start.4
Sparse Core Ops, SparseCore 0:
  40.8 30.2 all-gather.1

commit v3 on v2

--- a/solution.py
+++ b/solution.py
@@ -22,6 +22,7 @@
 NEG = -1e30
 MB = 1024 * 1024
 LIMIT = 5424
+PIECES = 2
 
 
 def params(limit):
@@ -77,7 +78,7 @@
     )(x, gain)
 
 
-def pack_body(offset_ref, x_ref, main_ref, rest_ref, packed, at_row):
+def pack_body(offset_ref, mine_ref, x_ref, main_ref, rest_ref, more_ref, packed, at_row):
     step = pl.program_id(0)
     count = x_ref.shape[0] // WIN
     @pl.when(step == 0)
@@ -93,32 +94,39 @@
     @pl.when(step == pl.num_programs(0) - 1)
     def _():
         main_ref[...] = packed[0:LIMIT, :].astype(BF)
+        mine = lax.fori_loop(0, mine_ref.shape[0], lambda w, total: total + sent(mine_ref[w]), 0)
+        more_ref[0] = (jnp.maximum(start, mine) > LIMIT).astype(jnp.int32)
 
         @pl.when(start > LIMIT)
         def _():
             rest_ref[...] = packed[LIMIT:, :].astype(BF)
 
 
-def pack(offsets, x, rows=4096):
+def pack(offsets, mine, x, rows=4096):
     pixels = x.shape[0]
-    whole = lambda i, s: (0, 0)
+    whole = lambda i, s, t: (0, 0)
     return pl.pallas_call(
         pack_body,
         grid_spec=pltpu.PrefetchScalarGridSpec(
-            num_scalar_prefetch=1,
+            num_scalar_prefetch=2,
             grid=(pixels // rows,),
-            in_specs=[pl.BlockSpec((rows, C), lambda i, s: (i, 0))],
-            out_specs=[pl.BlockSpec((LIMIT, C), whole), pl.BlockSpec((pixels - LIMIT, C), whole)],
+            in_specs=[pl.BlockSpec((rows, C), lambda i, s, t: (i, 0))],
+            out_specs=[
+                pl.BlockSpec((LIMIT, C), whole),
+                pl.BlockSpec((pixels - LIMIT, C), whole),
+                pl.BlockSpec(memory_space=pltpu.SMEM),
+            ],
             scratch_shapes=[pltpu.VMEM((pixels, C), F32), pltpu.SMEM((1,), jnp.int32)],
         ),
         out_shape=[
             jax.ShapeDtypeStruct((LIMIT, C), BF),
             jax.ShapeDtypeStruct((pixels - LIMIT, C), BF),
+            jax.ShapeDtypeStruct((1,), jnp.int32),
         ],
         compiler_params=params(60),
         cost_estimate=pl.CostEstimate(flops=0, bytes_accessed=10 * pixels * C, transcendentals=0),
         name="pack_rows",
-    )(offsets, x)
+    )(offsets, mine, x)
 
 
 def join_body(*refs):
@@ -229,31 +237,32 @@
     )(x, x, gain, w_qkv, kt, vo, after, *given)
 
 
-def seam_body(index_ref, pool_ref, out_ref):
+def seam_body(index_ref, *refs):
+    out_ref = refs[-1]
     rows = index_ref.shape[0]
-    step = 1024
     total = jnp.zeros((rows, C), F32)
-    for lo in range(0, pool_ref.shape[0], step):
+    lo = 0
+    for ref in refs[:-1]:
+        step = ref.shape[0]
         at = lax.broadcasted_iota(jnp.int32, (rows, step), 1) + lo
         pick = jnp.where(at == index_ref[...], 1.0, 0.0).astype(BF)
-        total = total + dot(pick, pool_ref[lo:lo + step])
+        total = total + dot(pick, ref[...])
+        lo += step
     out_ref[...] = total.astype(BF)
 
 
-def seam(index, pool, rows=256):
+def seam(index, pools, rows=256):
     count = index.shape[0]
     return pl.pallas_call(
         seam_body,
         grid=(count // rows,),
-        in_specs=[
-            pl.BlockSpec((rows, 1), lambda i: (i, 0)),
-            pl.BlockSpec(pool.shape, lambda i: (0, 0)),
-        ],
+        in_specs=[pl.BlockSpec((rows, 1), lambda i: (i, 0))]
+        + [pl.BlockSpec(pool.shape, lambda i: (0, 0)) for pool in pools],
         out_specs=pl.BlockSpec((rows, C), lambda i: (i, 0)),
         out_shape=jax.ShapeDtypeStruct((count, C), BF),
         compiler_params=params(48),
         name="seam_rows",
-    )(index, pool)
+    )(index, *pools)
 
 
 def window_body(
@@ -300,60 +309,66 @@
                         lanes_of(k), (near, 128)
                     )
 
-    x = x_ref[...].astype(F32)
-    chosen = []
-    start = at_row[0]
-    for w in range(count):
-        offset = offset_ref[first_window + w]
-        other = packed[pl.ds(pl.multiple_of(start, 8), WIN), :]
-        chosen.append(jnp.where(position >= offset, x[w * WIN:w * WIN + WIN], other))
-        start = start + sent(offset)
-    at_row[0] = start
-    normed = norm_rows(jnp.concatenate(chosen, axis=0), gain_ref[...])
-    keys = dot_nt(wkt_ref[...], normed)
-    values = dot(normed, wv_ref[...]).astype(BF)
     block = (lax.broadcasted_iota(jnp.int32, (64, 128), 0) // DIM) == (
         lax.broadcasted_iota(jnp.int32, (64, 128), 1) // WIN
     )
     first_lanes = lax.broadcasted_iota(jnp.int32, (64, 128), 1) < WIN
-    for half in range(2):
-        for b in range(2):
-            lo = half * 128 + b * 64
-            for p in range(pairs):
-                pair = keys[lo:lo + 64, p * 128:p * 128 + 128]
-                turned = pltpu.roll(pair, WIN, 1)
-                to = (half, slice(b * 64, b * 64 + 64), slice(b * 128, b * 128 + 128))
-                kbd[(2 * p,) + to] = jnp.where(block, jnp.where(first_lanes, pair, turned), 0.0).astype(BF)
-                kbd[(2 * p + 1,) + to] = jnp.where(block, jnp.where(first_lanes, turned, pair), 0.0).astype(BF)
-        for k in range(HALF):
-            mine = lanes_of(k)
-            for w in range(count):
-                vbd[w, half, k * WIN:k * WIN + WIN, 0:128] = (
-                    values[w * WIN:w * WIN + WIN, half * 128:half * 128 + 128] * mine
-                )
-
-    wide = pairs * 128
-    seam_k = dot_nt(wkt_ref[...], seam_ref[...]).astype(BF)
-    column = lax.broadcasted_iota(jnp.int32, (count * SEAM, wide), 1)
-    spread = jnp.where(
-        lax.broadcasted_iota(jnp.int32, (count * SEAM, wide), 0) == column // 128 * near + column % near, 1.0, 0.0
-    ).astype(BF)
-    of_head = (lax.broadcasted_iota(jnp.int32, (C, wide), 1) % 128) // near == (
-        lax.broadcasted_iota(jnp.int32, (C, wide), 0) // DIM
-    )
-    seam_kt = jnp.where(of_head, dot(seam_k, spread), 0.0).astype(BF)
-    for p in range(pairs):
-        ksm[p] = seam_kt[:, p * 128:p * 128 + 128]
-    seam_v = dot(seam_ref[...], wv_ref[...]).astype(BF)
-    for h in range(HEADS):
-        half, k = h // HALF, h % HALF
-        for p in range(pairs):
-            vsm[p, h * near:h * near + near, half * C:half * C + 128] = (
-                seam_v[p * near:p * near + near, half * 128:half * 128 + 128] * lanes_of(k)
-            )
     own = (lax.broadcasted_iota(jnp.int32, (128, 128), 1) % near) // SEAM == (
         lax.broadcasted_iota(jnp.int32, (128, 128), 0) // WIN
     )
+    some = count // PIECES
+    some_pairs = some // 2
+
+    def build(piece):
+        w0 = piece * some
+        p0 = piece * some_pairs
+        chosen = []
+        start = at_row[0]
+        for w in range(w0, w0 + some):
+            offset = offset_ref[first_window + w]
+            other = packed[pl.ds(pl.multiple_of(start, 8), WIN), :]
+            chosen.append(jnp.where(position >= offset, x_ref[w * WIN:w * WIN + WIN, :].astype(F32), other))
+            start = start + sent(offset)
+        at_row[0] = start
+        normed = norm_rows(jnp.concatenate(chosen, axis=0), gain_ref[...])
+        keys = dot_nt(wkt_ref[...], normed)
+        values = dot(normed, wv_ref[...]).astype(BF)
+        for half in range(2):
+            for b in range(2):
+                lo = half * 128 + b * 64
+                for p in range(some_pairs):
+                    pair = keys[lo:lo + 64, p * 128:p * 128 + 128]
+                    turn = pltpu.roll(pair, WIN, 1)
+                    to = (half, slice(b * 64, b * 64 + 64), slice(b * 128, b * 128 + 128))
+                    w = w0 + 2 * p
+                    kbd[(w,) + to] = jnp.where(block, jnp.where(first_lanes, pair, turn), 0.0).astype(BF)
+                    kbd[(w + 1,) + to] = jnp.where(block, jnp.where(first_lanes, turn, pair), 0.0).astype(BF)
+            for k in range(HALF):
+                for w in range(some):
+                    vbd[w0 + w, half, k * WIN:k * WIN + WIN, 0:128] = (
+                        values[w * WIN:w * WIN + WIN, half * 128:half * 128 + 128] * lanes_of(k)
+                    )
+
+        wide = some_pairs * 128
+        rows_s = some * SEAM
+        seam_in = seam_ref[piece * rows_s:piece * rows_s + rows_s, :]
+        seam_k = dot_nt(wkt_ref[...], seam_in).astype(BF)
+        column = lax.broadcasted_iota(jnp.int32, (rows_s, wide), 1)
+        spread = jnp.where(
+            lax.broadcasted_iota(jnp.int32, (rows_s, wide), 0) == column // 128 * near + column % near, 1.0, 0.0
+        ).astype(BF)
+        of_head = (lax.broadcasted_iota(jnp.int32, (C, wide), 1) % 128) // near == (
+            lax.broadcasted_iota(jnp.int32, (C, wide), 0) // DIM
+        )
+        seam_kt = jnp.where(of_head, dot(seam_k, spread), 0.0).astype(BF)
+        seam_v = dot(seam_in, wv_ref[...]).astype(BF)
+        for p in range(some_pairs):
+            ksm[p0 + p] = seam_kt[:, p * 128:p * 128 + 128]
+            for h in range(HEADS):
+                half, k = h // HALF, h % HALF
+                vsm[p0 + p, h * near:h * near + near, half * C:half * C + 128] = (
+                    seam_v[p * near:p * near + near, half * 128:half * 128 + 128] * lanes_of(k)
+                )
 
     def window_scores(w, half):
         at = pl.ds(pl.multiple_of(w * WIN, WIN), WIN)
@@ -362,24 +377,47 @@
     def seam_scores(p):
         return dot(q_ref[pl.ds(pl.multiple_of(p * 128, 128), 128), :], ksm[p])
 
-    weights_s = [jnp.where(own, exp2(seam_scores(p)), 0.0).astype(BF) for p in range(pairs)]
-    weights_w = [[exp2(window_scores(w, half)).astype(BF) for half in range(2)] for w in range(count)]
-    for p in range(pairs):
-        sums[p * 128:p * 128 + 128, :] = acc_ref[p * 128:p * 128 + 128, :] + dot(weights_s[p], vsm[p])
-    for w in range(count):
-        at = slice(w * WIN, w * WIN + WIN)
+    def weigh(piece):
+        pairs_here = range(piece * some_pairs, piece * some_pairs + some_pairs)
+        windows_here = range(piece * some, piece * some + some)
+        weights_s = [jnp.where(own, exp2(seam_scores(p)), 0.0).astype(BF) for p in pairs_here]
+        weights_w = [[exp2(window_scores(w, half)).astype(BF) for half in range(2)] for w in windows_here]
+        return weights_s, weights_w
+
+    def add_up(piece, weights):
+        weights_s, weights_w = weights
+        for p in range(some_pairs):
+            at = slice((piece * some_pairs + p) * 128, (piece * some_pairs + p) * 128 + 128)
+            sums[at, :] = acc_ref[at, :] + dot(weights_s[p], vsm[piece * some_pairs + p])
+        for w in range(some):
+            at = slice((piece * some + w) * WIN, (piece * some + w) * WIN + WIN)
+            for half in range(2):
+                sums[at, half * C:half * C + C] += dot(weights_w[w][half], vbd[piece * some + w, half])
+
+    def finish(piece):
+        size = some * WIN
+        at = slice(piece * size, piece * size + size)
+        check = jnp.zeros((8, 128), F32)
+        parts = []
         for half in range(2):
-            sums[at, half * C:half * C + C] += dot(weights_w[w][half], vbd[w, half])
-
+            den = sums[at, half * C + 128:half * C + C]
+            inverse = 1.0 / den
+            check = check + jnp.sum((den + inverse).reshape(size // 8, 8, 128), axis=0)
+            parts.append(sums[at, half * C:half * C + 128] * inverse)
+        attended = jnp.concatenate(parts, axis=1).astype(BF)
+        out_ref[at, :] = (x_ref[at, :].astype(F32) + dot(attended, wo_ref[...])).astype(BF)
+        return check
+
+    build(0)
     check = jnp.zeros((8, 128), F32)
-    parts = []
-    for half in range(2):
-        den = sums[:, half * C + 128:half * C + C]
-        inverse = 1.0 / den
-        check = check + jnp.sum((den + inverse).reshape(rows // 8, 8, 128), axis=0)
-        parts.append(sums[:, half * C:half * C + 128] * inverse)
-    attended = jnp.concatenate(parts, axis=1).astype(BF)
-    out_ref[...] = (x + dot(attended, wo_ref[...])).astype(BF)
+    for piece in range(PIECES):
+        weights = weigh(piece)
+        if piece + 1 < PIECES:
+            build(piece + 1)
+        add_up(piece, weights)
+        if piece > 0:
+            check = check + finish(piece - 1)
+    check = check + finish(PIECES - 1)
     fine = jnp.sum(check) <= HIGH
 
     @pl.when(jnp.logical_not(fine))
@@ -497,9 +535,10 @@
 def place_in_pool(index, windows):
     face, local = index // windows, index % windows
     me = lax.axis_index("face")
+    dx = (me // 8 - face // 8) % 4
     dz = (me // 4 - face // 4) % 2
     dy = (me - face) % 4
-    return ((face // 8 * 2 + dz) * 4 + dy) * windows + local
+    return ((dx * 2 + dz) * 4 + dy) * windows + local
 
 
 def by_sub(x, k):
@@ -510,23 +549,21 @@
     pixels = pixel_state.shape[0]
     gain = norm1_gain.reshape(1, C)
     asked = partner(shift_offsets)
-    more = (jnp.maximum(sent(shift_offsets).sum(), sent(asked).sum()) > LIMIT).astype(jnp.int32)
-    pooled = pool_rows(pixel_state, gain)
+    pooled, asked = lax.optimization_barrier((pool_rows(pixel_state, gain), asked))
     groups = [pooled] + [by_sub(pooled, k) for k in (1, 2, 3)]
     columns = turned(pooled, [(0, 0, 1), (0, 0, 2), (0, 0, 3)])
-    main, rest = pack(asked, pixel_state)
+    main, rest, more = pack(asked, shift_offsets, pixel_state)
     main = partner(main)
     planes = turned(join(*columns), [(0, 1, 0)])
     cube = join(*planes)
-    lines = [[x * 8 + rest for x in range(4)] for rest in range(8)]
-    pool = lax.all_gather(cube, "face", axis=0, tiled=True, axis_index_groups=lines)
+    pools = turned(cube, [(1, 0, 0), (2, 0, 0), (3, 0, 0)])
     kt, vo = group(groups, w_qkv)
     split = pixels // 4
     sums = coarse(0, split, pixel_state, gain, w_qkv, kt, vo, gain, rows=512)
     q, acc = coarse(split, pixels - split, pixel_state, gain, w_qkv, kt, vo, cube, sums)
     index = place_in_pool(seam_table, pooled.shape[0]).reshape(-1, 1)
-    seam_rows = seam(index, pool)
-    _, rest = lax.while_loop(lambda c: c[0] > 0, lambda c: (c[0] - 1, partner(c[1])), (more, rest))
+    seam_rows = seam(index, pools)
+    _, rest = lax.while_loop(lambda c: c[0] > 0, lambda c: (c[0] - 1, partner(c[1])), (more[0], rest))
     return window(shift_offsets, pixel_state, main, rest, q, acc, seam_rows, gain, w_qkv, w_out, kt, vo)
 
 

time: 249 us -> 229 us (0.920)
  between operations: 14.8 us -> 0.36 us
  waiting for transfers between devices: 7.57 us -> 0.03 us
  starting transfers between devices: 15.1 us -> 18.4 us
    ppermute x2, waiting for transfers between devices: 7.54 us -> 0.01 us  [partner(): return lax.ppermute(x, 'face', [(i, i ^ 1) for i in range(32)])]
    ppermute x4 -> x7, starting transfers between devices: 9.2 us -> 13.2 us  [turned(): return [block] + [lax.ppermute(block, 'face', rotation(*s)) for s in steps]]
    ppermute x3, starting transfers between devices: 5.51 us -> 3.01 us  [by_sub(): return lax.ppermute(x, 'sub', [(i, i ^ k) for i in range(4)])]
    unnamed x20 -> x18, local copies, waits for them, and re-layouts: 5.59 us -> 4.18 us
  transfers between devices with their start and end apart: 10 -> 12, of which waited for: 1 -> 0; matrix products, arithmetic and copies ran while one was open for 1% -> 0% of each run, Pallas kernels for 22% -> 27%
where the time goes in v3:
time: 229 us; the launch traced here: 228 us
  Pallas kernels  204 us (89%)
  starting transfers between devices  18.4 us (8%)
  local copies, waits for them, and re-layouts  4.47 us (2%)
    pallas_call x1, Pallas kernels, window(): pl.pallas_call(window_body, grid_spec=pltpu.PrefetchScalarGridSpec(num_sc...  141 us
    pallas_call x2, Pallas kernels, coarse(): pl.pallas_call(coarse_body, grid=(steps,), in_specs=[pl.BlockSpec((rows,...  45.3 us
    ppermute x7, starting transfers between devices, turned(): return [block] + [lax.ppermute(block, 'face', rotation(*s)) for s in steps]  13.2 us
    pallas_call x1, Pallas kernels, pack(): pl.pallas_call(pack_body, grid_spec=pltpu.PrefetchScalarGridSpec(num_scal...  7.43 us
    pallas_call x1, Pallas kernels, pool_rows(): pl.pallas_call(pool_body, grid=(pixels // rows,), in_specs=[pl.BlockSpec(...  5.85 us
  transfers between devices with their start and end apart: 12, of which 0 were waited for; matrix products, arithmetic and copies ran while one was open for 0% of the time, Pallas kernels for 27%

profile of v3, /device:TPU:1, one launch (start us, length us, event | category | flops | bytes accessed | tf_op | source)
XLA Modules:
  0.0 227.6 jit_solution(12759472104396865806)
XLA Ops:
  0.0 0.0 copy-start.7
  0.0 2.1 collective-permute-start.1
  2.1 5.9 %norm_pool.1.refs_0_ = bf16[128,256]{1,0:T(8,128)(2,1)} custom-call(bf16[8192,256]{1,0:T(8,128)(2,1)} %x_ref.9, f32[1,256]{1,0:T(1,128)} %bitcast.2), custom_call_target="tpu_custom_call" | custom-call | flops 1073741824 | bytes 8388608 | tf_op jit(solution)/shard_map/norm_pool/pallas_call | solution.py:66
  8.0 0.0 copy-start.3
  8.0 0.0 copy-start.2
  8.0 0.0 collective-permute-done.1.offset_ref
  8.0 0.0 copy-start.8
  8.0 0.1 collective-permute-start.6
  8.1 1.3 collective-permute-start.3
  9.4 1.7 collective-permute-start.4
  11.1 0.0 collective-permute-start.5
  11.1 2.9 %collective-permute-start.7 = (bf16[128,256]{1,0:T(8,128)(2,1)}, bf16[128,256]{1,0:T(8,128)(2,1)S(1)}, u32[]{:S(2)}, u32[]{:S(2)}) collective-permute-start(bf16[128,256]{1,0:T(8,128)(2,1)} %norm_pool.1.refs_0_), channel_id=1, source_target_pairs={{0,8},{4,12},{8,0},{12,4},{16,24},{20,28},{24,16},{28,20},{32,40},... | collective-permute-start | bytes 196616 | tf_op jit(solution)/shard_map/ppermute | solution.py:532
  14.1 0.0 collective-permute-done.6.refs_1_
  14.1 1.6 collective-permute-start.8
  15.7 0.0 copy-done.7
  15.7 0.1 copy.10
  15.8 0.2 reshape.8.index_ref
  16.0 0.0 copy-done.8
  16.0 7.4 %pack_rows.1 = (bf16[5424,256]{1,0:T(8,128)(2,1)}, bf16[2768,256]{1,0:T(8,128)(2,1)}, s32[1]{0:T(128)}) custom-call(s32[128]{0:T(128)} %copy-done.8, s32[128]{0:T(128)} %offset_ref.1, bf16[8192,256]{1,0:T(8,128)(2,1)} %x_ref.9), custom_call_target="tpu_custom_call" | custom-call | bytes 20971520 | tf_op jit(solution)/shard_map/pack_rows/pallas_call | solution.py:108
  23.4 0.0 collective-permute-done.7.refs_2_
  23.5 0.1 collective-permute-start.2
  23.6 0.0 collective-permute-done.8.refs_3_
  23.6 0.0 copy-done.3
  23.6 3.6 %collective-permute-start.9 = (bf16[512,256]{1,0:T(8,128)(2,1)S(1)}, bf16[512,256]{1,0:T(8,128)(2,1)S(1)}, u32[]{:S(2)}, u32[]{:S(2)}) collective-permute-start(bf16[512,256]{1,0:T(8,128)(2,1)S(1)} %join_blocks.2.refs_0_), channel_id=1, source_target_pairs={{0,16},{4,20},{8,24},{12,28},{16,0},{20,4},{24,8},{28,12},{32,48},... | collective-permute-start | bytes 786440 | tf_op jit(solution)/shard_map/ppermute | solution.py:532
  27.2 0.0 collective-permute-done.3.refs_1_
  27.2 0.0 collective-permute-done.4.refs_2_
  27.2 0.0 collective-permute-done.5.refs_3_
  27.3 0.0 copy-done.2
  27.3 0.5 group_keys_values.1
  27.8 0.0 copy-start.5
  27.8 1.4 copy-done.5
  29.2 0.0 copy-start.6
  29.2 1.0 copy-done.6
  30.2 13.2 %group_attention.2 = (bf16[8192,256]{1,0:T(8,128)(2,1)}, f32[8192,512]{1,0:T(8,128)}) custom-call(bf16[8192,256]{1,0:T(8,128)(2,1)} %x_ref.9, bf16[8192,256]{1,0:T(8,128)(2,1)} %x_ref.9, f32[1,256]{1,0:T(1,128)} %bitcast.3, bf16[256,768]{1,0:T(8,128)(2,1)} %wv_ref.1, bf16[8,128,512]{2,1,0:T(8,128)(2,1)} %copy-done.6, bf16[2,2048,256]{2,1,0:T(8,128)(2,1)} %copy-done.5, ...), custom_call_target="tpu_custom_call" | custom-call | flops 8589934592 | bytes 5242880 | tf_op jit(solution)/shard_map/group_attention/pallas_call | solution.py:210
  43.3 0.0 collective-permute-done.9.refs_1_
  43.4 0.0 copy-start
  43.4 1.3 collective-permute-start.10
  44.7 2.4 %collective-permute-start.11 = (bf16[1024,256]{1,0:T(8,128)(2,1)S(1)}, bf16[1024,256]{1,0:T(8,128)(2,1)S(1)}, u32[]{:S(2)}, u32[]{:S(2)}) collective-permute-start(bf16[1024,256]{1,0:T(8,128)(2,1)S(1)} %join_blocks.3.refs_0_), channel_id=1, source_target_pairs={{0,64},{4,68},{8,72},{12,76},{16,80},{20,84},{24,88},{28,92},{32,9... | collective-permute-start | bytes 1572872 | tf_op jit(solution)/shard_map/ppermute | solution.py:532
  47.1 1.2 collective-permute-start.12
  48.3 0.0 copy-done
  48.3 32.2 %group_attention.3 = (bf16[8192,256]{1,0:T(8,128)(2,1)}, f32[8192,512]{1,0:T(8,128)}) custom-call(bf16[8192,256]{1,0:T(8,128)(2,1)} %x_ref.9, bf16[8192,256]{1,0:T(8,128)(2,1)} %x_ref.9, f32[1,256]{1,0:T(1,128)} %bitcast.5, bf16[256,768]{1,0:T(8,128)(2,1)} %wv_ref.1, bf16[8,128,512]{2,1,0:T(8,128)(2,1)} %copy-done.6, ...), custom_call_target="tpu_custom_call", output_to_operand_aliasing={{0}: (7, {}), {1}: (8, {})} | custom-call | flops 25769803776 | bytes 15728640 | tf_op jit(solution)/shard_map/group_attention/pallas_call | solution.py:210
  80.4 0.0 collective-permute-done.10.refs_1_
  80.5 0.0 collective-permute-done.11.refs_2_
  80.5 0.0 collective-permute-done.12.refs_3_
  80.5 0.0 copy-start.1
  80.5 1.0 copy-done.1
  81.5 3.0 %seam_rows.1.seam_ref = bf16[1024,256]{1,0:T(8,128)(2,1)S(1)} custom-call(s32[1024,1]{1,0:T(8,128)S(1)} %reshape.8.index_ref, bf16[1024,256]{1,0:T(8,128)(2,1)S(1)} %copy-done.1, bf16[1024,256]{1,0:T(8,128)(2,1)S(1)} %collective-permute-done.10.refs_1_, bf16[1024,256]{1,0:T(8,128)(2,1)S(1)} %collective-permute-done.11.refs_2_, ...), custom_call_target="tpu_custom_call" | custom-call | tf_op jit(solution)/shard_map/seam_rows/pallas_call | solution.py:256
  84.6 0.0 copy-start.4
  84.6 0.8 copy-done.4
  85.3 0.6 while.10
  86.0 0.0 collective-permute-done.2.main_ref
  86.0 141.5 %window_attention.1 = bf16[8192,256]{1,0:T(8,128)(2,1)} custom-call(s32[128]{0:T(128)} %offset_ref.1, bf16[8192,256]{1,0:T(8,128)(2,1)} %x_ref.9, bf16[5424,256]{1,0:T(8,128)(2,1)} %collective-permute-done.2.main_ref, bf16[2768,256]{1,0:T(8,128)(2,1)} %get-tuple-element.32.rest_hbm, bf16[8192,256]{1,0:T(8,128)(2,1)} %get-tuple-element.38.q_ref, ...), custom_call_target="tpu_custom_call" | custom-call | flops 21474836480 | bytes 41943040 | tf_op jit(solution)/shard_map/window_attention/pallas_call | solution.py:475
  (3 shorter events, 0.1 us)
Async XLA Ops:
  0.0 15.7 %copy-start.7 = (s32[128,8]{0,1:T(8,128)S(1)}, s32[128,8]{0,1:T(8,128)}, u32[]{:S(2)}) copy-start(s32[128,8]{0,1:T(8,128)} %param.13) | copy-start | bytes 12292
  0.0 8.0 %collective-permute-start.1 = (s32[128]{0:T(128)}, s32[128]{0:T(128)S(1)}, u32[]{:S(2)}, u32[]{:S(2)}) collective-permute-start(s32[128]{0:T(128)} %offset_ref.1), channel_id=1, source_target_pairs={{0,4},{4,0},{8,12},{12,8},{16,20},{20,16},{24,28},{28,24},{32,36},... | collective-permute-start | bytes 1544 | tf_op jit(solution)/shard_map/ppermute | solution.py:528
  8.0 15.6 %copy-start.3 = (bf16[128,256]{1,0:T(8,128)(2,1)S(1)}, bf16[128,256]{1,0:T(8,128)(2,1)}, u32[]{:S(2)}) copy-start(bf16[128,256]{1,0:T(8,128)(2,1)} %norm_pool.1.refs_0_) | copy-start | bytes 196612
  8.0 19.3 %copy-start.2 = (bf16[256,768]{1,0:T(8,128)(2,1)S(1)}, bf16[256,768]{1,0:T(8,128)(2,1)}, u32[]{:S(2)}) copy-start(bf16[256,768]{1,0:T(8,128)(2,1)} %wv_ref.1) | copy-start | bytes 1179652
  8.0 8.0 %copy-start.8 = (s32[128]{0:T(128)}, s32[128]{0:T(128)S(1)}, u32[]{:S(2)}) copy-start(s32[128]{0:T(128)S(1)} %collective-permute-done.1.offset_ref) | copy-start | bytes 1540
  8.0 6.1 %collective-permute-start.6 = (bf16[128,256]{1,0:T(8,128)(2,1)}, bf16[128,256]{1,0:T(8,128)(2,1)S(1)}, u32[]{:S(2)}, u32[]{:S(2)}) collective-permute-start(bf16[128,256]{1,0:T(8,128)(2,1)} %norm_pool.1.refs_0_), channel_id=1, source_target_pairs={{0,4},{4,8},{8,12},{12,0},{16,20},{20,24},{24,28},{28,16},{32,36},... | collective-permute-start | bytes 196616 | tf_op jit(solution)/shard_map/ppermute | solution.py:532
  8.1 19.1 %collective-permute-start.3 = (bf16[128,256]{1,0:T(8,128)(2,1)}, bf16[128,256]{1,0:T(8,128)(2,1)S(1)}, u32[]{:S(2)}, u32[]{:S(2)}) collective-permute-start(bf16[128,256]{1,0:T(8,128)(2,1)} %norm_pool.1.refs_0_), channel_id=1, source_target_pairs={{0,1},{1,0},{2,3},{3,2},{4,5},{5,4},{6,7},{7,6},{8,9},{9,8},{10,11... | collective-permute-start | bytes 196616 | tf_op jit(solution)/shard_map/ppermute | solution.py:545
  9.4 17.9 %collective-permute-start.4 = (bf16[128,256]{1,0:T(8,128)(2,1)}, bf16[128,256]{1,0:T(8,128)(2,1)S(1)}, u32[]{:S(2)}, u32[]{:S(2)}) collective-permute-start(bf16[128,256]{1,0:T(8,128)(2,1)} %norm_pool.1.refs_0_), channel_id=1, source_target_pairs={{0,2},{1,3},{2,0},{3,1},{4,6},{5,7},{6,4},{7,5},{8,10},{9,11},{10,... | collective-permute-start | bytes 196616 | tf_op jit(solution)/shard_map/ppermute | solution.py:545
  11.1 16.1 %collective-permute-start.5 = (bf16[128,256]{1,0:T(8,128)(2,1)}, bf16[128,256]{1,0:T(8,128)(2,1)S(1)}, u32[]{:S(2)}, u32[]{:S(2)}) collective-permute-start(bf16[128,256]{1,0:T(8,128)(2,1)} %norm_pool.1.refs_0_), channel_id=1, source_target_pairs={{0,3},{1,2},{2,1},{3,0},{4,7},{5,6},{6,5},{7,4},{8,11},{9,10},{10,... | collective-permute-start | bytes 196616 | tf_op jit(solution)/shard_map/ppermute | solution.py:545
  11.1 12.3 %collective-permute-start.7 = (bf16[128,256]{1,0:T(8,128)(2,1)}, bf16[128,256]{1,0:T(8,128)(2,1)S(1)}, u32[]{:S(2)}, u32[]{:S(2)}) collective-permute-start(bf16[128,256]{1,0:T(8,128)(2,1)} %norm_pool.1.refs_0_), channel_id=1, source_target_pairs={{0,8},{4,12},{8,0},{12,4},{16,24},{20,28},{24,16},{28,20},{32,40},... | collective-permute-start | bytes 196616 | tf_op jit(solution)/shard_map/ppermute | solution.py:532
  14.1 9.5 %collective-permute-start.8 = (bf16[128,256]{1,0:T(8,128)(2,1)}, bf16[128,256]{1,0:T(8,128)(2,1)S(1)}, u32[]{:S(2)}, u32[]{:S(2)}) collective-permute-start(bf16[128,256]{1,0:T(8,128)(2,1)} %norm_pool.1.refs_0_), channel_id=1, source_target_pairs={{0,12},{4,0},{8,4},{12,8},{16,28},{20,16},{24,20},{28,24},{32,44},... | collective-permute-start | bytes 196616 | tf_op jit(solution)/shard_map/ppermute | solution.py:532
  23.5 62.5 %collective-permute-start.2 = (bf16[5424,256]{1,0:T(8,128)(2,1)}, bf16[5424,256]{1,0:T(8,128)(2,1)}, u32[]{:S(2)}, u32[]{:S(2)}) collective-permute-start(bf16[5424,256]{1,0:T(8,128)(2,1)} %get-tuple-element.29), channel_id=1, source_target_pairs={{0,4},{4,0},{8,12},{12,8},{16,20},{20,16},{24,28},{28,24},{32,36},... | collective-permute-start | bytes 8331272 | tf_op jit(solution)/shard_map/ppermute | solution.py:528
  23.6 19.7 %collective-permute-start.9 = (bf16[512,256]{1,0:T(8,128)(2,1)S(1)}, bf16[512,256]{1,0:T(8,128)(2,1)S(1)}, u32[]{:S(2)}, u32[]{:S(2)}) collective-permute-start(bf16[512,256]{1,0:T(8,128)(2,1)S(1)} %join_blocks.2.refs_0_), channel_id=1, source_target_pairs={{0,16},{4,20},{8,24},{12,28},{16,0},{20,4},{24,8},{28,12},{32,48},... | collective-permute-start | bytes 786440 | tf_op jit(solution)/shard_map/ppermute | solution.py:532
  27.8 1.4 copy-start.5
  29.2 1.0 copy-start.6
  43.4 4.9 %copy-start = (bf16[1024,256]{1,0:T(8,128)(2,1)}, bf16[1024,256]{1,0:T(8,128)(2,1)S(1)}, u32[]{:S(2)}) copy-start(bf16[1024,256]{1,0:T(8,128)(2,1)S(1)} %join_blocks.3.refs_0_) | copy-start | bytes 1572868
  43.4 37.1 %collective-permute-start.10 = (bf16[1024,256]{1,0:T(8,128)(2,1)S(1)}, bf16[1024,256]{1,0:T(8,128)(2,1)S(1)}, u32[]{:S(2)}, u32[]{:S(2)}) collective-permute-start(bf16[1024,256]{1,0:T(8,128)(2,1)S(1)} %join_blocks.3.refs_0_), channel_id=1, source_target_pairs={{0,32},{4,36},{8,40},{12,44},{16,48},{20,52},{24,56},{28,60},{32,6... | collective-permute-start | bytes 1572872 | tf_op jit(solution)/shard_map/ppermute | solution.py:532
  44.7 35.8 %collective-permute-start.11 = (bf16[1024,256]{1,0:T(8,128)(2,1)S(1)}, bf16[1024,256]{1,0:T(8,128)(2,1)S(1)}, u32[]{:S(2)}, u32[]{:S(2)}) collective-permute-start(bf16[1024,256]{1,0:T(8,128)(2,1)S(1)} %join_blocks.3.refs_0_), channel_id=1, source_target_pairs={{0,64},{4,68},{8,72},{12,76},{16,80},{20,84},{24,88},{28,92},{32,9... | collective-permute-start | bytes 1572872 | tf_op jit(solution)/shard_map/ppermute | solution.py:532
  47.1 33.3 %collective-permute-start.12 = (bf16[1024,256]{1,0:T(8,128)(2,1)S(1)}, bf16[1024,256]{1,0:T(8,128)(2,1)S(1)}, u32[]{:S(2)}, u32[]{:S(2)}) collective-permute-start(bf16[1024,256]{1,0:T(8,128)(2,1)S(1)} %join_blocks.3.refs_0_), channel_id=1, source_target_pairs={{0,96},{4,100},{8,104},{12,108},{16,112},{20,116},{24,120},{28,124... | collective-permute-start | bytes 1572872 | tf_op jit(solution)/shard_map/ppermute | solution.py:532
  80.5 1.0 copy-start.1
  84.6 0.8 copy-start.4

commit v4 on v3

--- a/solution.py
+++ b/solution.py
@@ -21,7 +21,7 @@
 HIGH = 2.0 ** 100
 NEG = -1e30
 MB = 1024 * 1024
-LIMIT = 5424
+LIMIT = 5360
 PIECES = 2
 
 
@@ -143,44 +143,29 @@
     )(*blocks)
 
 
-def group_body(*refs):
-    wk_ref, wv_ref, kt_ref, vo_ref = refs[-4:]
-    g = jnp.concatenate([ref[...] for ref in refs[:-4]], axis=0)
+def lay_out_group(blocks, wk_ref, wv_ref, kt_ref, vo_ref):
+    g = jnp.concatenate([ref[...] for ref in blocks], axis=0)
     count = g.shape[0]
     kt = lax.dot_general(wk_ref[...], g, (((0,), (1,)), ((), ())), preferred_element_type=F32)
     v = dot(g, wv_ref[...])
     feat = lax.broadcasted_iota(jnp.int32, (128, count), 0) // DIM
     lane = lax.broadcasted_iota(jnp.int32, (count, 128), 1) // DIM
     for h in range(HEADS):
-        lo = (h // HALF) * 128
-        kt_ref[h] = jnp.where(feat == h % HALF, kt[lo:lo + 128], 0.0).astype(BF)
-        mine = lane == h % HALF
-        vo_ref[h // HALF, h % HALF * count:h % HALF * count + count, 0:128] = jnp.where(mine, v[:, lo:lo + 128], 0.0).astype(BF)
-        vo_ref[h // HALF, h % HALF * count:h % HALF * count + count, 128:256] = jnp.where(mine, 1.0, 0.0).astype(BF)
-
-
-def group(blocks, w_qkv):
+        half, k = h // HALF, h % HALF
+        kt_ref[h] = jnp.where(feat == k, kt[half * 128:half * 128 + 128], 0.0).astype(BF)
+        vo_ref[half, k * count:k * count + count, 0:128] = jnp.where(
+            lane == k, v[:, half * 128:half * 128 + 128], 0.0
+        ).astype(BF)
+        vo_ref[half, k * count:k * count + count, 128:256] = jnp.where(lane == k, 1.0, 0.0).astype(BF)
+
+
+def group_scratch(blocks):
     count = sum(b.shape[0] for b in blocks)
-    return pl.pallas_call(
-        group_body,
-        grid=(1,),
-        in_specs=[pl.BlockSpec(b.shape, lambda i: (0, 0)) for b in blocks]
-        + [pl.BlockSpec((C, C), lambda i: (0, 1)), pl.BlockSpec((C, C), lambda i: (0, 2))],
-        out_specs=[
-            pl.BlockSpec((HEADS, 128, count), lambda i: (0, 0, 0)),
-            pl.BlockSpec((2, HALF * count, C), lambda i: (0, 0, 0)),
-        ],
-        out_shape=[
-            jax.ShapeDtypeStruct((HEADS, 128, count), BF),
-            jax.ShapeDtypeStruct((2, HALF * count, C), BF),
-        ],
-        compiler_params=params(32),
-        name="group_keys_values",
-    )(*blocks, w_qkv, w_qkv)
-
-
-def coarse_body(x_ref, next_ref, gain_ref, wq_ref, kt_ref, vo_ref, *refs):
-    q_ref, acc_ref, held = refs[-3:]
+    return [pltpu.VMEM((HEADS, 128, count), BF), pltpu.VMEM((2, HALF * count, C), BF)]
+
+
+def coarse_body(blocks, x_ref, next_ref, gain_ref, wq_ref, wk_ref, wv_ref, *refs):
+    q_ref, acc_ref, held, kt_ref, vo_ref = refs[-5:]
     step = pl.program_id(0)
 
     def queries(ref):
@@ -188,6 +173,7 @@
 
     @pl.when(step == 0)
     def _():
+        lay_out_group(refs[:blocks], wk_ref, wv_ref, kt_ref, vo_ref)
         held[...] = queries(x_ref)
 
     q = held[...]
@@ -202,22 +188,24 @@
     held[...] = queries(next_ref)
 
 
-def coarse(first, run, x, gain, w_qkv, kt, vo, after, given=(), rows=1024):
+def coarse(first, run, x, gain, w_qkv, blocks, after, given=(), rows=1024):
     pixels = x.shape[0]
     steps = run // rows
     base = first // rows
-    count = kt.shape[2]
+    count = sum(b.shape[0] for b in blocks)
+    fixed = 6 + len(blocks) + 1
     return pl.pallas_call(
-        coarse_body,
+        functools.partial(coarse_body, len(blocks)),
         grid=(steps,),
         in_specs=[
             pl.BlockSpec((rows, C), lambda i: (base, 0)),
             pl.BlockSpec((rows, C), lambda i: (base + jnp.minimum(i + 1, steps - 1), 0)),
             pl.BlockSpec((1, C), lambda i: (0, 0)),
             pl.BlockSpec((C, C), lambda i: (0, 0)),
-            pl.BlockSpec(kt.shape, lambda i: (0, 0, 0)),
-            pl.BlockSpec(vo.shape, lambda i: (0, 0, 0)),
+            pl.BlockSpec((C, C), lambda i: (0, 1)),
+            pl.BlockSpec((C, C), lambda i: (0, 2)),
         ]
+        + [pl.BlockSpec(b.shape, lambda i: (0, 0)) for b in blocks]
         + [pl.BlockSpec(memory_space=pl.ANY)] * (1 + len(given)),
         out_specs=[
             pl.BlockSpec((rows, C), lambda i: (base + i, 0)),
@@ -227,14 +215,14 @@
             jax.ShapeDtypeStruct((pixels, C), BF),
             jax.ShapeDtypeStruct((pixels, 2 * C), F32),
         ],
-        scratch_shapes=[pltpu.VMEM((rows, C), BF)],
-        input_output_aliases={7: 0, 8: 1} if given else {},
+        scratch_shapes=[pltpu.VMEM((rows, C), BF)] + group_scratch(blocks),
+        input_output_aliases={fixed: 0, fixed + 1: 1} if given else {},
         compiler_params=params(60),
         cost_estimate=pl.CostEstimate(
             flops=4 * run * HEADS * count * C, bytes_accessed=10 * run * C, transcendentals=run * HEADS * count
         ),
         name="group_attention",
-    )(x, x, gain, w_qkv, kt, vo, after, *given)
+    )(x, x, gain, w_qkv, w_qkv, w_qkv, *blocks, after, *given)
 
 
 def seam_body(index_ref, *refs):
@@ -266,9 +254,10 @@
 
 
 def window_body(
-    offset_ref, x_ref, main_ref, rest_hbm, q_ref, acc_ref, seam_ref, gain_ref, wk_ref, wv_ref, wo_ref,
-    kt_hbm, vo_hbm, out_ref, kbd, vbd, vsm, ksm, sums, packed, rest_ref, wkt_ref, kt_ref, vo_ref, at_row, done,
+    offset_ref, x_ref, main_ref, rest_hbm, q_ref, acc_ref, seam_ref, gain_ref, wk_ref, wv_ref, wo_ref, *refs,
 ):
+    out_ref, kbd, vbd, vsm, ksm, mixed, packed, rest_ref, wkt_ref, kt_ref, vo_ref, at_row, done = refs[-13:]
+    blocks = refs[:-13]
     rows = x_ref.shape[0]
     count = rows // WIN
     pairs = count // 2
@@ -292,7 +281,7 @@
 
         @pl.when(lax.fori_loop(0, pl.num_programs(0) * count, add, 0) > LIMIT)
         def _():
-            copy = pltpu.make_async_copy(rest_hbm, rest_ref, done.at[0])
+            copy = pltpu.make_async_copy(rest_hbm, rest_ref, done)
             copy.start()
             copy.wait()
             packed[LIMIT:, :] = rest_ref[...].astype(F32)
@@ -386,27 +375,23 @@
 
     def add_up(piece, weights):
         weights_s, weights_w = weights
+        check = jnp.zeros((8, 128), F32)
         for p in range(some_pairs):
-            at = slice((piece * some_pairs + p) * 128, (piece * some_pairs + p) * 128 + 128)
-            sums[at, :] = acc_ref[at, :] + dot(weights_s[p], vsm[piece * some_pairs + p])
-        for w in range(some):
-            at = slice((piece * some + w) * WIN, (piece * some + w) * WIN + WIN)
+            lo = (piece * some_pairs + p) * 128
+            base = acc_ref[lo:lo + 128, :] + dot(weights_s[p], vsm[piece * some_pairs + p])
             for half in range(2):
-                sums[at, half * C:half * C + C] += dot(weights_w[w][half], vbd[piece * some + w, half])
+                total = base[:, half * C:half * C + C] + jnp.concatenate(
+                    [dot(weights_w[2 * p + w][half], vbd[piece * some + 2 * p + w, half]) for w in range(2)], axis=0
+                )
+                den = total[:, 128:256]
+                inverse = 1.0 / den
+                check = check + jnp.sum((den + inverse).reshape(16, 8, 128), axis=0)
+                mixed[lo:lo + 128, half * 128:half * 128 + 128] = (total[:, 0:128] * inverse).astype(BF)
+        return check
 
     def finish(piece):
-        size = some * WIN
-        at = slice(piece * size, piece * size + size)
-        check = jnp.zeros((8, 128), F32)
-        parts = []
-        for half in range(2):
-            den = sums[at, half * C + 128:half * C + C]
-            inverse = 1.0 / den
-            check = check + jnp.sum((den + inverse).reshape(size // 8, 8, 128), axis=0)
-            parts.append(sums[at, half * C:half * C + 128] * inverse)
-        attended = jnp.concatenate(parts, axis=1).astype(BF)
-        out_ref[at, :] = (x_ref[at, :].astype(F32) + dot(attended, wo_ref[...])).astype(BF)
-        return check
+        at = slice(piece * some * WIN, piece * some * WIN + some * WIN)
+        out_ref[at, :] = (x_ref[at, :].astype(F32) + dot(mixed[at, :], wo_ref[...])).astype(BF)
 
     build(0)
     check = jnp.zeros((8, 128), F32)
@@ -414,19 +399,15 @@
         weights = weigh(piece)
         if piece + 1 < PIECES:
             build(piece + 1)
-        add_up(piece, weights)
+        check = check + add_up(piece, weights)
         if piece > 0:
-            check = check + finish(piece - 1)
-    check = check + finish(PIECES - 1)
+            finish(piece - 1)
+    finish(PIECES - 1)
     fine = jnp.sum(check) <= HIGH
 
     @pl.when(jnp.logical_not(fine))
     def _():
-        copies = [pltpu.make_async_copy(kt_hbm, kt_ref, done.at[0]), pltpu.make_async_copy(vo_hbm, vo_ref, done.at[1])]
-        for copy in copies:
-            copy.start()
-        for copy in copies:
-            copy.wait()
+        lay_out_group(blocks, wk_ref, wv_ref, kt_ref, vo_ref)
         keys_g = kt_ref.shape[2]
         head_s = lax.broadcasted_iota(jnp.int32, (128, 128), 1) // near
         head_w = lax.broadcasted_iota(jnp.int32, (128, C), 1) // WIN
@@ -467,7 +448,7 @@
         lax.fori_loop(0, pairs, exact, 0)
 
 
-def window(offsets, x, main, rest, q, acc, seam_rows, gain, w_qkv, wo, kt, vo, rows=1024):
+def window(offsets, x, main, rest, q, acc, seam_rows, gain, w_qkv, wo, blocks, rows=1024):
     pixels = x.shape[0]
     count = rows // WIN
     row = lambda i, s: (i, 0)
@@ -488,23 +469,21 @@
                 pl.BlockSpec((C, C), lambda i, s: (0, 1)),
                 pl.BlockSpec((C, C), lambda i, s: (0, 2)),
                 pl.BlockSpec((C, C), fixed),
-                pl.BlockSpec(memory_space=pl.ANY),
-                pl.BlockSpec(memory_space=pl.ANY),
-            ],
+            ]
+            + [pl.BlockSpec(b.shape, fixed) for b in blocks],
             out_specs=pl.BlockSpec((rows, C), row),
             scratch_shapes=[
                 pltpu.VMEM((count, 2, 128, C), BF),
                 pltpu.VMEM((count, 2, HALF * WIN, C), BF),
                 pltpu.VMEM((count // 2, 128, 2 * C), BF),
                 pltpu.VMEM((count // 2, C, 128), BF),
-                pltpu.VMEM((rows, 2 * C), F32),
+                pltpu.VMEM((rows, C), BF),
                 pltpu.VMEM((pixels, C), F32),
                 pltpu.VMEM(rest.shape, BF),
                 pltpu.VMEM((C, C), BF),
-                pltpu.VMEM(kt.shape, BF),
-                pltpu.VMEM(vo.shape, BF),
+                *group_scratch(blocks),
                 pltpu.SMEM((1,), jnp.int32),
-                pltpu.SemaphoreType.DMA((2,)),
+                pltpu.SemaphoreType.DMA,
             ],
         ),
         out_shape=jax.ShapeDtypeStruct((pixels, C), BF),
@@ -513,7 +492,7 @@
             flops=40 * pixels * C * C, bytes_accessed=20 * pixels * C, transcendentals=0
         ),
         name="window_attention",
-    )(offsets, x, main, rest, q, acc, seam_rows, gain, w_qkv, w_qkv, wo, kt, vo)
+    )(offsets, x, main, rest, q, acc, seam_rows, gain, w_qkv, w_qkv, wo, *blocks)
 
 
 def rotation(dx, dz, dy):
@@ -557,14 +536,13 @@
     planes = turned(join(*columns), [(0, 1, 0)])
     cube = join(*planes)
     pools = turned(cube, [(1, 0, 0), (2, 0, 0), (3, 0, 0)])
-    kt, vo = group(groups, w_qkv)
     split = pixels // 4
-    sums = coarse(0, split, pixel_state, gain, w_qkv, kt, vo, gain, rows=512)
-    q, acc = coarse(split, pixels - split, pixel_state, gain, w_qkv, kt, vo, cube, sums)
+    sums = coarse(0, split, pixel_state, gain, w_qkv, groups, gain, rows=512)
+    q, acc = coarse(split, pixels - split, pixel_state, gain, w_qkv, groups, cube, sums)
     index = place_in_pool(seam_table, pooled.shape[0]).reshape(-1, 1)
     seam_rows = seam(index, pools)
     _, rest = lax.while_loop(lambda c: c[0] > 0, lambda c: (c[0] - 1, partner(c[1])), (more[0], rest))
-    return window(shift_offsets, pixel_state, main, rest, q, acc, seam_rows, gain, w_qkv, w_out, kt, vo)
+    return window(shift_offsets, pixel_state, main, rest, q, acc, seam_rows, gain, w_qkv, w_out, groups)
 
 
 def solution(mesh):

time: 229 us -> 217 us (0.948)
  Pallas kernels: 204 us -> 192 us
    pallas_call x1, Pallas kernels: 141 us -> 131 us  [window(): pl.pallas_call(window_body, grid_spec=pltpu.PrefetchScalarGridSpec(num_sc...]
    pallas_call x3 -> x2, Pallas kernels: 45.9 us -> 44.4 us  [coarse(): pl.pallas_call(functools.partial(coarse_body, len(blocks)), grid=(steps,)...]
  transfers between devices with their start and end apart: 12 -> 12, of which waited for: 0 -> 1; matrix products, arithmetic and copies ran while one was open for 0% -> 0% of each run, Pallas kernels for 27% -> 28%
where the time goes in v4:
time: 217 us
  Pallas kernels  192 us (88%)
  starting transfers between devices  19.1 us (9%)
  local copies, waits for them, and re-layouts  3.46 us (2%)
    pallas_call x1, Pallas kernels, window(): pl.pallas_call(window_body, grid_spec=pltpu.PrefetchScalarGridSpec(num_sc...  131 us
    pallas_call x2, Pallas kernels, coarse(): pl.pallas_call(functools.partial(coarse_body, len(blocks)), grid=(steps,)...  44.4 us
    ppermute x7, starting transfers between devices, turned(): return [block] + [lax.ppermute(block, 'face', rotation(*s)) for s in steps]  13 us
    pallas_call x1, Pallas kernels, pack(): pl.pallas_call(pack_body, grid_spec=pltpu.PrefetchScalarGridSpec(num_scal...  7.51 us
    pallas_call x1, Pallas kernels, pool_rows(): pl.pallas_call(pool_body, grid=(pixels // rows,), in_specs=[pl.BlockSpec(...  5.85 us
  transfers between devices with their start and end apart: 12, of which 1 were waited for; matrix products, arithmetic and copies ran while one was open for 0% of the time, Pallas kernels for 28%

profile of v4, /device:TPU:1, one launch (start us, length us, event | category | flops | bytes accessed | tf_op | source)
XLA Modules:
  0.0 216.8 jit_solution(16429824838684227452)
XLA Ops:
  0.0 0.0 copy-start.4
  0.0 2.1 collective-permute-start.1
  2.1 5.8 %norm_pool.1.refs_0_ = bf16[128,256]{1,0:T(8,128)(2,1)} custom-call(bf16[8192,256]{1,0:T(8,128)(2,1)} %x_ref.9, f32[1,256]{1,0:T(1,128)} %bitcast.2), custom_call_target="tpu_custom_call" | custom-call | flops 1073741824 | bytes 8388608 | tf_op jit(solution)/shard_map/norm_pool/pallas_call | solution.py:66
  8.0 0.0 copy-start.3
  8.0 0.0 collective-permute-done.1.offset_ref
  8.0 0.0 copy-start.5
  8.0 0.1 collective-permute-start.6
  8.1 3.0 %collective-permute-start.7 = (bf16[128,256]{1,0:T(8,128)(2,1)}, bf16[128,256]{1,0:T(8,128)(2,1)S(1)}, u32[]{:S(2)}, u32[]{:S(2)}) collective-permute-start(bf16[128,256]{1,0:T(8,128)(2,1)} %norm_pool.1.refs_0_), channel_id=1, source_target_pairs={{0,8},{4,12},{8,0},{12,4},{16,24},{20,28},{24,16},{28,20},{32,40},... | collective-permute-start | bytes 196616 | tf_op jit(solution)/shard_map/ppermute | solution.py:511
  11.1 1.6 collective-permute-start.8
  12.7 1.8 collective-permute-start.3
  14.5 1.6 collective-permute-start.4
  16.2 0.0 collective-permute-done.6.refs_1_
  16.2 0.4 collective-permute-start.5
  16.6 0.0 copy-done.4
  16.7 0.1 copy.10
  16.8 0.2 reshape.8.index_ref
  16.9 0.0 copy-done.5
  17.0 7.5 %pack_rows.1 = (bf16[5360,256]{1,0:T(8,128)(2,1)}, bf16[2832,256]{1,0:T(8,128)(2,1)}, s32[1]{0:T(128)}) custom-call(s32[128]{0:T(128)} %copy-done.5, s32[128]{0:T(128)} %offset_ref.1, bf16[8192,256]{1,0:T(8,128)(2,1)} %x_ref.9), custom_call_target="tpu_custom_call" | custom-call | bytes 20971520 | tf_op jit(solution)/shard_map/pack_rows/pallas_call | solution.py:108
  24.5 0.0 collective-permute-done.7.refs_2_
  24.5 0.1 collective-permute-start.2
  24.6 0.0 collective-permute-done.8.refs_3_
  24.6 0.0 copy-done.3
  24.6 3.4 %collective-permute-start.9 = (bf16[512,256]{1,0:T(8,128)(2,1)S(1)}, bf16[512,256]{1,0:T(8,128)(2,1)S(1)}, u32[]{:S(2)}, u32[]{:S(2)}) collective-permute-start(bf16[512,256]{1,0:T(8,128)(2,1)S(1)} %join_blocks.2.refs_0_), channel_id=1, source_target_pairs={{0,16},{4,20},{8,24},{12,28},{16,0},{20,4},{24,8},{28,12},{32,48},... | collective-permute-start | bytes 786440 | tf_op jit(solution)/shard_map/ppermute | solution.py:511
  28.0 0.0 collective-permute-done.3.refs_1_
  28.0 0.0 copy-start.6
  28.0 0.0 collective-permute-done.4.refs_2_
  28.0 0.0 copy-start.7
  28.0 0.0 collective-permute-done.5.refs_3_
  28.0 0.6 copy-done.6
  28.6 0.0 copy-done.7
  28.7 0.0 copy-start.8
  28.7 0.6 copy-done.8
  29.3 12.7 %group_attention.2 = (bf16[8192,256]{1,0:T(8,128)(2,1)}, f32[8192,512]{1,0:T(8,128)}) custom-call(bf16[8192,256]{1,0:T(8,128)(2,1)} %x_ref.9, bf16[8192,256]{1,0:T(8,128)(2,1)} %x_ref.9, f32[1,256]{1,0:T(1,128)} %bitcast.3, bf16[256,768]{1,0:T(8,128)(2,1)} %wv_ref.5, bf16[256,768]{1,0:T(8,128)(2,1)} %wv_ref.5, bf16[256,768]{1,0:T(8,128)(2,1)} %wv_ref.5, ...), custom_call_target="tpu_custom_call" | custom-call | flops 8589934592 | bytes 5242880 | tf_op jit(solution)/shard_map/group_attention/pallas_call | solution.py:197
  42.0 0.0 collective-permute-done.9.refs_1_
  42.1 0.0 copy-start
  42.1 1.3 collective-permute-start.10
  43.4 2.4 %collective-permute-start.11 = (bf16[1024,256]{1,0:T(8,128)(2,1)S(1)}, bf16[1024,256]{1,0:T(8,128)(2,1)S(1)}, u32[]{:S(2)}, u32[]{:S(2)}) collective-permute-start(bf16[1024,256]{1,0:T(8,128)(2,1)S(1)} %join_blocks.3.refs_4_.refs_0_), channel_id=1, source_target_pairs={{0,64},{4,68},{8,72},{12,76},{16,80},{20,84},{24,88},{28,92},{32,9... | collective-permute-start | bytes 1572872 | tf_op jit(solution)/shard_map/ppermute | solution.py:511
  45.8 1.2 collective-permute-start.12
  47.0 0.0 copy-done
  47.0 31.7 %group_attention.3 = (bf16[8192,256]{1,0:T(8,128)(2,1)}, f32[8192,512]{1,0:T(8,128)}) custom-call(bf16[8192,256]{1,0:T(8,128)(2,1)} %x_ref.9, bf16[8192,256]{1,0:T(8,128)(2,1)} %x_ref.9, f32[1,256]{1,0:T(1,128)} %bitcast.5, bf16[256,768]{1,0:T(8,128)(2,1)} %wv_ref.5, bf16[256,768]{1,0:T(8,128)(2,1)} %wv_ref.5, ...), custom_call_target="tpu_custom_call", output_to_operand_aliasing={{0}: (11, {}), {1}: (12, {})} | custom-call | flops 25769803776 | bytes 15728640 | tf_op jit(solution)/shard_map/group_attention/pallas_call | solution.py:197
  78.7 0.0 collective-permute-done.10.refs_1_
  78.7 0.0 collective-permute-done.11.refs_2_
  78.7 0.0 collective-permute-done.12.refs_3_
  78.7 0.0 copy-start.1
  78.7 1.0 copy-done.1
  79.8 3.0 %seam_rows.1.seam_ref = bf16[1024,256]{1,0:T(8,128)(2,1)S(1)} custom-call(s32[1024,1]{1,0:T(8,128)S(1)} %reshape.8.index_ref, bf16[1024,256]{1,0:T(8,128)(2,1)S(1)} %copy-done.1, bf16[1024,256]{1,0:T(8,128)(2,1)S(1)} %collective-permute-done.10.refs_1_, bf16[1024,256]{1,0:T(8,128)(2,1)S(1)} %collective-permute-done.11.refs_2_, ...), custom_call_target="tpu_custom_call" | custom-call | tf_op jit(solution)/shard_map/seam_rows/pallas_call | solution.py:244
  82.8 0.0 copy-start.2
  82.8 0.8 copy-done.2
  83.7 0.6 while.10
  84.3 1.7 collective-permute-done.2.main_ref
  86.0 130.6 %window_attention.1 = bf16[8192,256]{1,0:T(8,128)(2,1)} custom-call(s32[128]{0:T(128)} %offset_ref.1, bf16[8192,256]{1,0:T(8,128)(2,1)} %x_ref.9, bf16[5360,256]{1,0:T(8,128)(2,1)} %collective-permute-done.2.main_ref, bf16[2832,256]{1,0:T(8,128)(2,1)} %get-tuple-element.30.rest_hbm, bf16[8192,256]{1,0:T(8,128)(2,1)} %get-tuple-element.34.q_ref, ...), custom_call_target="tpu_custom_call" | custom-call | flops 21474836480 | bytes 41943040 | tf_op jit(solution)/shard_map/window_attention/pallas_call | solution.py:456
  (3 shorter events, 0.1 us)
Async XLA Ops:
  0.0 16.6 %copy-start.4 = (s32[128,8]{0,1:T(8,128)S(1)}, s32[128,8]{0,1:T(8,128)}, u32[]{:S(2)}) copy-start(s32[128,8]{0,1:T(8,128)} %param.13) | copy-start | bytes 12292
  0.0 8.0 %collective-permute-start.1 = (s32[128]{0:T(128)}, s32[128]{0:T(128)S(1)}, u32[]{:S(2)}, u32[]{:S(2)}) collective-permute-start(s32[128]{0:T(128)} %offset_ref.1), channel_id=1, source_target_pairs={{0,4},{4,0},{8,12},{12,8},{16,20},{20,16},{24,28},{28,24},{32,36},... | collective-permute-start | bytes 1544 | tf_op jit(solution)/shard_map/ppermute | solution.py:507
  8.0 16.6 %copy-start.3 = (bf16[128,256]{1,0:T(8,128)(2,1)S(1)}, bf16[128,256]{1,0:T(8,128)(2,1)}, u32[]{:S(2)}) copy-start(bf16[128,256]{1,0:T(8,128)(2,1)} %norm_pool.1.refs_0_) | copy-start | bytes 196612
  8.0 9.0 %copy-start.5 = (s32[128]{0:T(128)}, s32[128]{0:T(128)S(1)}, u32[]{:S(2)}) copy-start(s32[128]{0:T(128)S(1)} %collective-permute-done.1.offset_ref) | copy-start | bytes 1540
  8.0 8.2 %collective-permute-start.6 = (bf16[128,256]{1,0:T(8,128)(2,1)}, bf16[128,256]{1,0:T(8,128)(2,1)S(1)}, u32[]{:S(2)}, u32[]{:S(2)}) collective-permute-start(bf16[128,256]{1,0:T(8,128)(2,1)} %norm_pool.1.refs_0_), channel_id=1, source_target_pairs={{0,4},{4,8},{8,12},{12,0},{16,20},{20,24},{24,28},{28,16},{32,36},... | collective-permute-start | bytes 196616 | tf_op jit(solution)/shard_map/ppermute | solution.py:511
  8.1 16.4 %collective-permute-start.7 = (bf16[128,256]{1,0:T(8,128)(2,1)}, bf16[128,256]{1,0:T(8,128)(2,1)S(1)}, u32[]{:S(2)}, u32[]{:S(2)}) collective-permute-start(bf16[128,256]{1,0:T(8,128)(2,1)} %norm_pool.1.refs_0_), channel_id=1, source_target_pairs={{0,8},{4,12},{8,0},{12,4},{16,24},{20,28},{24,16},{28,20},{32,40},... | collective-permute-start | bytes 196616 | tf_op jit(solution)/shard_map/ppermute | solution.py:511
  11.1 13.4 %collective-permute-start.8 = (bf16[128,256]{1,0:T(8,128)(2,1)}, bf16[128,256]{1,0:T(8,128)(2,1)S(1)}, u32[]{:S(2)}, u32[]{:S(2)}) collective-permute-start(bf16[128,256]{1,0:T(8,128)(2,1)} %norm_pool.1.refs_0_), channel_id=1, source_target_pairs={{0,12},{4,0},{8,4},{12,8},{16,28},{20,16},{24,20},{28,24},{32,44},... | collective-permute-start | bytes 196616 | tf_op jit(solution)/shard_map/ppermute | solution.py:511
  12.7 15.3 %collective-permute-start.3 = (bf16[128,256]{1,0:T(8,128)(2,1)}, bf16[128,256]{1,0:T(8,128)(2,1)S(1)}, u32[]{:S(2)}, u32[]{:S(2)}) collective-permute-start(bf16[128,256]{1,0:T(8,128)(2,1)} %norm_pool.1.refs_0_), channel_id=1, source_target_pairs={{0,1},{1,0},{2,3},{3,2},{4,5},{5,4},{6,7},{7,6},{8,9},{9,8},{10,11... | collective-permute-start | bytes 196616 | tf_op jit(solution)/shard_map/ppermute | solution.py:524
  14.5 13.5 %collective-permute-start.4 = (bf16[128,256]{1,0:T(8,128)(2,1)}, bf16[128,256]{1,0:T(8,128)(2,1)S(1)}, u32[]{:S(2)}, u32[]{:S(2)}) collective-permute-start(bf16[128,256]{1,0:T(8,128)(2,1)} %norm_pool.1.refs_0_), channel_id=1, source_target_pairs={{0,2},{1,3},{2,0},{3,1},{4,6},{5,7},{6,4},{7,5},{8,10},{9,11},{10,... | collective-permute-start | bytes 196616 | tf_op jit(solution)/shard_map/ppermute | solution.py:524
  16.2 11.9 %collective-permute-start.5 = (bf16[128,256]{1,0:T(8,128)(2,1)}, bf16[128,256]{1,0:T(8,128)(2,1)S(1)}, u32[]{:S(2)}, u32[]{:S(2)}) collective-permute-start(bf16[128,256]{1,0:T(8,128)(2,1)} %norm_pool.1.refs_0_), channel_id=1, source_target_pairs={{0,3},{1,2},{2,1},{3,0},{4,7},{5,6},{6,5},{7,4},{8,11},{9,10},{10,... | collective-permute-start | bytes 196616 | tf_op jit(solution)/shard_map/ppermute | solution.py:524
  24.5 61.5 %collective-permute-start.2 = (bf16[5360,256]{1,0:T(8,128)(2,1)}, bf16[5360,256]{1,0:T(8,128)(2,1)}, u32[]{:S(2)}, u32[]{:S(2)}) collective-permute-start(bf16[5360,256]{1,0:T(8,128)(2,1)} %get-tuple-element.27), channel_id=1, source_target_pairs={{0,4},{4,0},{8,12},{12,8},{16,20},{20,16},{24,28},{28,24},{32,36},... | collective-permute-start | bytes 8232968 | tf_op jit(solution)/shard_map/ppermute | solution.py:507
  24.6 17.4 %collective-permute-start.9 = (bf16[512,256]{1,0:T(8,128)(2,1)S(1)}, bf16[512,256]{1,0:T(8,128)(2,1)S(1)}, u32[]{:S(2)}, u32[]{:S(2)}) collective-permute-start(bf16[512,256]{1,0:T(8,128)(2,1)S(1)} %join_blocks.2.refs_0_), channel_id=1, source_target_pairs={{0,16},{4,20},{8,24},{12,28},{16,0},{20,4},{24,8},{28,12},{32,48},... | collective-permute-start | bytes 786440 | tf_op jit(solution)/shard_map/ppermute | solution.py:511
  28.0 0.6 copy-start.6
  28.0 0.6 copy-start.7
  28.7 0.6 copy-start.8
  42.1 4.9 %copy-start = (bf16[1024,256]{1,0:T(8,128)(2,1)}, bf16[1024,256]{1,0:T(8,128)(2,1)S(1)}, u32[]{:S(2)}) copy-start(bf16[1024,256]{1,0:T(8,128)(2,1)S(1)} %join_blocks.3.refs_4_.refs_0_) | copy-start | bytes 1572868
  42.1 36.6 %collective-permute-start.10 = (bf16[1024,256]{1,0:T(8,128)(2,1)S(1)}, bf16[1024,256]{1,0:T(8,128)(2,1)S(1)}, u32[]{:S(2)}, u32[]{:S(2)}) collective-permute-start(bf16[1024,256]{1,0:T(8,128)(2,1)S(1)} %join_blocks.3.refs_4_.refs_0_), channel_id=1, source_target_pairs={{0,32},{4,36},{8,40},{12,44},{16,48},{20,52},{24,56},{28,60},{32,6... | collective-permute-start | bytes 1572872 | tf_op jit(solution)/shard_map/ppermute | solution.py:511
  43.4 35.3 %collective-permute-start.11 = (bf16[1024,256]{1,0:T(8,128)(2,1)S(1)}, bf16[1024,256]{1,0:T(8,128)(2,1)S(1)}, u32[]{:S(2)}, u32[]{:S(2)}) collective-permute-start(bf16[1024,256]{1,0:T(8,128)(2,1)S(1)} %join_blocks.3.refs_4_.refs_0_), channel_id=1, source_target_pairs={{0,64},{4,68},{8,72},{12,76},{16,80},{20,84},{24,88},{28,92},{32,9... | collective-permute-start | bytes 1572872 | tf_op jit(solution)/shard_map/ppermute | solution.py:511
  45.8 32.9 %collective-permute-start.12 = (bf16[1024,256]{1,0:T(8,128)(2,1)S(1)}, bf16[1024,256]{1,0:T(8,128)(2,1)S(1)}, u32[]{:S(2)}, u32[]{:S(2)}) collective-permute-start(bf16[1024,256]{1,0:T(8,128)(2,1)S(1)} %join_blocks.3.refs_4_.refs_0_), channel_id=1, source_target_pairs={{0,96},{4,100},{8,104},{12,108},{16,112},{20,116},{24,120},{28,124... | collective-permute-start | bytes 1572872 | tf_op jit(solution)/shard_map/ppermute | solution.py:511
  78.7 1.0 copy-start.1
  82.8 0.9 copy-start.2

commit v5 on v4

--- a/solution.py
+++ b/solution.py
@@ -78,7 +78,7 @@
     )(x, gain)
 
 
-def pack_body(offset_ref, mine_ref, x_ref, main_ref, rest_ref, more_ref, packed, at_row):
+def pack_body(offset_ref, mine_ref, x_ref, main_ref, rest_hbm, more_ref, packed, rest_ref, at_row, done):
     step = pl.program_id(0)
     count = x_ref.shape[0] // WIN
     @pl.when(step == 0)
@@ -100,6 +100,9 @@
         @pl.when(start > LIMIT)
         def _():
             rest_ref[...] = packed[LIMIT:, :].astype(BF)
+            copy = pltpu.make_async_copy(rest_ref, rest_hbm, done)
+            copy.start()
+            copy.wait()
 
 
 def pack(offsets, mine, x, rows=4096):
@@ -113,10 +116,15 @@
             in_specs=[pl.BlockSpec((rows, C), lambda i, s, t: (i, 0))],
             out_specs=[
                 pl.BlockSpec((LIMIT, C), whole),
-                pl.BlockSpec((pixels - LIMIT, C), whole),
+                pl.BlockSpec(memory_space=pl.ANY),
                 pl.BlockSpec(memory_space=pltpu.SMEM),
             ],
-            scratch_shapes=[pltpu.VMEM((pixels, C), F32), pltpu.SMEM((1,), jnp.int32)],
+            scratch_shapes=[
+                pltpu.VMEM((pixels, C), F32),
+                pltpu.VMEM((pixels - LIMIT, C), BF),
+                pltpu.SMEM((1,), jnp.int32),
+                pltpu.SemaphoreType.DMA,
+            ],
         ),
         out_shape=[
             jax.ShapeDtypeStruct((LIMIT, C), BF),
@@ -448,7 +456,7 @@
         lax.fori_loop(0, pairs, exact, 0)
 
 
-def window(offsets, x, main, rest, q, acc, seam_rows, gain, w_qkv, wo, blocks, rows=1024):
+def window(offsets, x, main, rest, q, acc, seam_rows, gain, w_qkv, wo, blocks, rows=2048):
     pixels = x.shape[0]
     count = rows // WIN
     row = lambda i, s: (i, 0)

time: 217 us -> 213 us (0.982)
  Pallas kernels: 192 us -> 187 us
    pallas_call x1, Pallas kernels: 131 us -> 127 us  [window(): pl.pallas_call(window_body, grid_spec=pltpu.PrefetchScalarGridSpec(num_sc...]
where the time goes in v5:
time: 213 us; the launch traced here: 212 us
  Pallas kernels  187 us (88%)
  starting transfers between devices  19.1 us (9%)
  local copies, waits for them, and re-layouts  3.46 us (2%)
    pallas_call x1, Pallas kernels, window(): pl.pallas_call(window_body, grid_spec=pltpu.PrefetchScalarGridSpec(num_sc...  127 us
    pallas_call x2, Pallas kernels, coarse(): pl.pallas_call(functools.partial(coarse_body, len(blocks)), grid=(steps,)...  44.4 us
    ppermute x7, starting transfers between devices, turned(): return [block] + [lax.ppermute(block, 'face', rotation(*s)) for s in steps]  13 us
    pallas_call x1, Pallas kernels, pack(): pl.pallas_call(pack_body, grid_spec=pltpu.PrefetchScalarGridSpec(num_scal...  6.94 us
    pallas_call x1, Pallas kernels, pool_rows(): pl.pallas_call(pool_body, grid=(pixels // rows,), in_specs=[pl.BlockSpec(...  5.85 us
  transfers between devices with their start and end apart: 12, of which 1 were waited for; matrix products, arithmetic and copies ran while one was open for 0% of the time, Pallas kernels for 28%

profile of v5, /device:TPU:1, one launch (start us, length us, event | category | flops | bytes accessed | tf_op | source)
XLA Modules:
  0.0 212.2 jit_solution(3506954010397032725)
XLA Ops:
  0.0 0.0 copy-start.4
  0.0 2.1 %collective-permute-start.1 = (s32[128]{0:T(128)}, s32[128]{0:T(128)S(1)}, u32[]{:S(2)}, u32[]{:S(2)}) collective-permute-start(s32[128]{0:T(128)} %offset_ref.1), channel_id=1, source_target_pairs={{0,4},{4,0},{8,12},{12,8},{16,20},{20,16},{24,28},{28,24},{32,36},... | collective-permute-start | bytes 1544 | tf_op jit(solution)/shard_map/ppermute | solution.py:515
  2.1 5.8 %norm_pool.1.refs_0_ = bf16[128,256]{1,0:T(8,128)(2,1)} custom-call(bf16[8192,256]{1,0:T(8,128)(2,1)} %x_ref.9, f32[1,256]{1,0:T(1,128)} %bitcast.2), custom_call_target="tpu_custom_call" | custom-call | flops 1073741824 | bytes 8388608 | tf_op jit(solution)/shard_map/norm_pool/pallas_call | solution.py:66
  8.0 0.0 copy-start.3
  8.0 0.0 collective-permute-done.1.offset_ref
  8.0 0.0 copy-start.5
  8.0 0.1 collective-permute-start.6
  8.1 3.0 %collective-permute-start.7 = (bf16[128,256]{1,0:T(8,128)(2,1)}, bf16[128,256]{1,0:T(8,128)(2,1)S(1)}, u32[]{:S(2)}, u32[]{:S(2)}) collective-permute-start(bf16[128,256]{1,0:T(8,128)(2,1)} %norm_pool.1.refs_0_), channel_id=1, source_target_pairs={{0,8},{4,12},{8,0},{12,4},{16,24},{20,28},{24,16},{28,20},{32,40},... | collective-permute-start | bytes 196616 | tf_op jit(solution)/shard_map/ppermute | solution.py:519
  11.1 1.6 collective-permute-start.8
  12.7 1.8 collective-permute-start.3
  14.5 1.6 collective-permute-start.4
  16.2 0.0 collective-permute-done.6.refs_1_
  16.2 0.4 collective-permute-start.5
  16.6 0.0 copy-done.4
  16.7 0.1 copy.10
  16.8 0.2 reshape.8.index_ref
  16.9 0.0 copy-done.5
  17.0 6.9 %pack_rows.1 = (bf16[5360,256]{1,0:T(8,128)(2,1)}, bf16[2832,256]{1,0:T(8,128)(2,1)}, s32[1]{0:T(128)}) custom-call(s32[128]{0:T(128)} %copy-done.5, s32[128]{0:T(128)} %offset_ref.1, bf16[8192,256]{1,0:T(8,128)(2,1)} %x_ref.9), custom_call_target="tpu_custom_call" | custom-call | bytes 20971520 | tf_op jit(solution)/shard_map/pack_rows/pallas_call | solution.py:111
  23.9 0.0 collective-permute-done.7.refs_2_
  23.9 0.1 collective-permute-start.2
  24.0 0.0 collective-permute-done.8.refs_3_
  24.0 0.0 copy-done.3
  24.1 3.4 %collective-permute-start.9 = (bf16[512,256]{1,0:T(8,128)(2,1)S(1)}, bf16[512,256]{1,0:T(8,128)(2,1)S(1)}, u32[]{:S(2)}, u32[]{:S(2)}) collective-permute-start(bf16[512,256]{1,0:T(8,128)(2,1)S(1)} %join_blocks.2.refs_0_), channel_id=1, source_target_pairs={{0,16},{4,20},{8,24},{12,28},{16,0},{20,4},{24,8},{28,12},{32,48},... | collective-permute-start | bytes 786440 | tf_op jit(solution)/shard_map/ppermute | solution.py:519
  27.4 0.0 collective-permute-done.3.refs_1_
  27.4 0.0 copy-start.6
  27.4 0.0 collective-permute-done.4.refs_2_
  27.5 0.0 copy-start.7
  27.5 0.0 collective-permute-done.5.refs_3_
  27.5 0.6 copy-done.6
  28.1 0.0 copy-done.7
  28.1 0.0 copy-start.8
  28.1 0.6 copy-done.8
  28.7 12.7 %group_attention.2 = (bf16[8192,256]{1,0:T(8,128)(2,1)}, f32[8192,512]{1,0:T(8,128)}) custom-call(bf16[8192,256]{1,0:T(8,128)(2,1)} %x_ref.9, bf16[8192,256]{1,0:T(8,128)(2,1)} %x_ref.9, f32[1,256]{1,0:T(1,128)} %bitcast.3, bf16[256,768]{1,0:T(8,128)(2,1)} %wv_ref.5, bf16[256,768]{1,0:T(8,128)(2,1)} %wv_ref.5, bf16[256,768]{1,0:T(8,128)(2,1)} %wv_ref.5, ...), custom_call_target="tpu_custom_call" | custom-call | flops 8589934592 | bytes 5242880 | tf_op jit(solution)/shard_map/group_attention/pallas_call | solution.py:205
  41.4 0.0 collective-permute-done.9.refs_1_
  41.5 0.0 copy-start
  41.5 1.3 collective-permute-start.10
  42.8 2.4 %collective-permute-start.11 = (bf16[1024,256]{1,0:T(8,128)(2,1)S(1)}, bf16[1024,256]{1,0:T(8,128)(2,1)S(1)}, u32[]{:S(2)}, u32[]{:S(2)}) collective-permute-start(bf16[1024,256]{1,0:T(8,128)(2,1)S(1)} %join_blocks.3.refs_4_.refs_0_), channel_id=1, source_target_pairs={{0,64},{4,68},{8,72},{12,76},{16,80},{20,84},{24,88},{28,92},{32,9... | collective-permute-start | bytes 1572872 | tf_op jit(solution)/shard_map/ppermute | solution.py:519
  45.2 1.2 collective-permute-start.12
  46.4 0.0 copy-done
  46.4 31.7 %group_attention.3 = (bf16[8192,256]{1,0:T(8,128)(2,1)}, f32[8192,512]{1,0:T(8,128)}) custom-call(bf16[8192,256]{1,0:T(8,128)(2,1)} %x_ref.9, bf16[8192,256]{1,0:T(8,128)(2,1)} %x_ref.9, f32[1,256]{1,0:T(1,128)} %bitcast.5, bf16[256,768]{1,0:T(8,128)(2,1)} %wv_ref.5, bf16[256,768]{1,0:T(8,128)(2,1)} %wv_ref.5, ...), custom_call_target="tpu_custom_call", output_to_operand_aliasing={{0}: (11, {}), {1}: (12, {})} | custom-call | flops 25769803776 | bytes 15728640 | tf_op jit(solution)/shard_map/group_attention/pallas_call | solution.py:205
  78.1 0.0 collective-permute-done.10.refs_1_
  78.1 0.0 collective-permute-done.11.refs_2_
  78.1 0.0 collective-permute-done.12.refs_3_
  78.2 0.0 copy-start.1
  78.2 1.0 copy-done.1
  79.2 3.0 %seam_rows.1.seam_ref = bf16[1024,256]{1,0:T(8,128)(2,1)S(1)} custom-call(s32[1024,1]{1,0:T(8,128)S(1)} %reshape.8.index_ref, bf16[1024,256]{1,0:T(8,128)(2,1)S(1)} %copy-done.1, bf16[1024,256]{1,0:T(8,128)(2,1)S(1)} %collective-permute-done.10.refs_1_, bf16[1024,256]{1,0:T(8,128)(2,1)S(1)} %collective-permute-done.11.refs_2_, ...), custom_call_target="tpu_custom_call" | custom-call | tf_op jit(solution)/shard_map/seam_rows/pallas_call | solution.py:252
  82.2 0.0 copy-start.2
  82.2 0.8 copy-done.2
  83.1 0.8 while.10
  83.9 1.5 collective-permute-done.2.main_ref
  85.5 126.6 %window_attention.1 = bf16[8192,256]{1,0:T(8,128)(2,1)} custom-call(s32[128]{0:T(128)} %offset_ref.1, bf16[8192,256]{1,0:T(8,128)(2,1)} %x_ref.9, bf16[5360,256]{1,0:T(8,128)(2,1)} %collective-permute-done.2.main_ref, bf16[2832,256]{1,0:T(8,128)(2,1)} %get-tuple-element.30.rest_hbm, bf16[8192,256]{1,0:T(8,128)(2,1)} %get-tuple-element.34.q_ref, ...), custom_call_target="tpu_custom_call" | custom-call | flops 21474836480 | bytes 41943040 | tf_op jit(solution)/shard_map/window_attention/pallas_call | solution.py:464
  (3 shorter events, 0.1 us)
Async XLA Ops:
  0.0 16.6 %copy-start.4 = (s32[128,8]{0,1:T(8,128)S(1)}, s32[128,8]{0,1:T(8,128)}, u32[]{:S(2)}) copy-start(s32[128,8]{0,1:T(8,128)} %param.13) | copy-start | bytes 12292
  0.0 8.0 %collective-permute-start.1 = (s32[128]{0:T(128)}, s32[128]{0:T(128)S(1)}, u32[]{:S(2)}, u32[]{:S(2)}) collective-permute-start(s32[128]{0:T(128)} %offset_ref.1), channel_id=1, source_target_pairs={{0,4},{4,0},{8,12},{12,8},{16,20},{20,16},{24,28},{28,24},{32,36},... | collective-permute-start | bytes 1544 | tf_op jit(solution)/shard_map/ppermute | solution.py:515
  8.0 16.0 %copy-start.3 = (bf16[128,256]{1,0:T(8,128)(2,1)S(1)}, bf16[128,256]{1,0:T(8,128)(2,1)}, u32[]{:S(2)}) copy-start(bf16[128,256]{1,0:T(8,128)(2,1)} %norm_pool.1.refs_0_) | copy-start | bytes 196612
  8.0 9.0 %copy-start.5 = (s32[128]{0:T(128)}, s32[128]{0:T(128)S(1)}, u32[]{:S(2)}) copy-start(s32[128]{0:T(128)S(1)} %collective-permute-done.1.offset_ref) | copy-start | bytes 1540
  8.0 8.2 %collective-permute-start.6 = (bf16[128,256]{1,0:T(8,128)(2,1)}, bf16[128,256]{1,0:T(8,128)(2,1)S(1)}, u32[]{:S(2)}, u32[]{:S(2)}) collective-permute-start(bf16[128,256]{1,0:T(8,128)(2,1)} %norm_pool.1.refs_0_), channel_id=1, source_target_pairs={{0,4},{4,8},{8,12},{12,0},{16,20},{20,24},{24,28},{28,16},{32,36},... | collective-permute-start | bytes 196616 | tf_op jit(solution)/shard_map/ppermute | solution.py:519
  8.1 15.8 %collective-permute-start.7 = (bf16[128,256]{1,0:T(8,128)(2,1)}, bf16[128,256]{1,0:T(8,128)(2,1)S(1)}, u32[]{:S(2)}, u32[]{:S(2)}) collective-permute-start(bf16[128,256]{1,0:T(8,128)(2,1)} %norm_pool.1.refs_0_), channel_id=1, source_target_pairs={{0,8},{4,12},{8,0},{12,4},{16,24},{20,28},{24,16},{28,20},{32,40},... | collective-permute-start | bytes 196616 | tf_op jit(solution)/shard_map/ppermute | solution.py:519
  11.1 12.9 %collective-permute-start.8 = (bf16[128,256]{1,0:T(8,128)(2,1)}, bf16[128,256]{1,0:T(8,128)(2,1)S(1)}, u32[]{:S(2)}, u32[]{:S(2)}) collective-permute-start(bf16[128,256]{1,0:T(8,128)(2,1)} %norm_pool.1.refs_0_), channel_id=1, source_target_pairs={{0,12},{4,0},{8,4},{12,8},{16,28},{20,16},{24,20},{28,24},{32,44},... | collective-permute-start | bytes 196616 | tf_op jit(solution)/shard_map/ppermute | solution.py:519
  12.7 14.7 %collective-permute-start.3 = (bf16[128,256]{1,0:T(8,128)(2,1)}, bf16[128,256]{1,0:T(8,128)(2,1)S(1)}, u32[]{:S(2)}, u32[]{:S(2)}) collective-permute-start(bf16[128,256]{1,0:T(8,128)(2,1)} %norm_pool.1.refs_0_), channel_id=1, source_target_pairs={{0,1},{1,0},{2,3},{3,2},{4,5},{5,4},{6,7},{7,6},{8,9},{9,8},{10,11... | collective-permute-start | bytes 196616 | tf_op jit(solution)/shard_map/ppermute | solution.py:532
  14.5 12.9 %collective-permute-start.4 = (bf16[128,256]{1,0:T(8,128)(2,1)}, bf16[128,256]{1,0:T(8,128)(2,1)S(1)}, u32[]{:S(2)}, u32[]{:S(2)}) collective-permute-start(bf16[128,256]{1,0:T(8,128)(2,1)} %norm_pool.1.refs_0_), channel_id=1, source_target_pairs={{0,2},{1,3},{2,0},{3,1},{4,6},{5,7},{6,4},{7,5},{8,10},{9,11},{10,... | collective-permute-start | bytes 196616 | tf_op jit(solution)/shard_map/ppermute | solution.py:532
  16.2 11.3 %collective-permute-start.5 = (bf16[128,256]{1,0:T(8,128)(2,1)}, bf16[128,256]{1,0:T(8,128)(2,1)S(1)}, u32[]{:S(2)}, u32[]{:S(2)}) collective-permute-start(bf16[128,256]{1,0:T(8,128)(2,1)} %norm_pool.1.refs_0_), channel_id=1, source_target_pairs={{0,3},{1,2},{2,1},{3,0},{4,7},{5,6},{6,5},{7,4},{8,11},{9,10},{10,... | collective-permute-start | bytes 196616 | tf_op jit(solution)/shard_map/ppermute | solution.py:532
  23.9 61.5 %collective-permute-start.2 = (bf16[5360,256]{1,0:T(8,128)(2,1)}, bf16[5360,256]{1,0:T(8,128)(2,1)}, u32[]{:S(2)}, u32[]{:S(2)}) collective-permute-start(bf16[5360,256]{1,0:T(8,128)(2,1)} %get-tuple-element.27), channel_id=1, source_target_pairs={{0,4},{4,0},{8,12},{12,8},{16,20},{20,16},{24,28},{28,24},{32,36},... | collective-permute-start | bytes 8232968 | tf_op jit(solution)/shard_map/ppermute | solution.py:515
  24.1 17.4 %collective-permute-start.9 = (bf16[512,256]{1,0:T(8,128)(2,1)S(1)}, bf16[512,256]{1,0:T(8,128)(2,1)S(1)}, u32[]{:S(2)}, u32[]{:S(2)}) collective-permute-start(bf16[512,256]{1,0:T(8,128)(2,1)S(1)} %join_blocks.2.refs_0_), channel_id=1, source_target_pairs={{0,16},{4,20},{8,24},{12,28},{16,0},{20,4},{24,8},{28,12},{32,48},... | collective-permute-start | bytes 786440 | tf_op jit(solution)/shard_map/ppermute | solution.py:519
  27.4 0.6 copy-start.6
  27.5 0.6 copy-start.7
  28.1 0.6 copy-start.8
  41.5 4.9 %copy-start = (bf16[1024,256]{1,0:T(8,128)(2,1)}, bf16[1024,256]{1,0:T(8,128)(2,1)S(1)}, u32[]{:S(2)}) copy-start(bf16[1024,256]{1,0:T(8,128)(2,1)S(1)} %join_blocks.3.refs_4_.refs_0_) | copy-start | bytes 1572868
  41.5 36.6 %collective-permute-start.10 = (bf16[1024,256]{1,0:T(8,128)(2,1)S(1)}, bf16[1024,256]{1,0:T(8,128)(2,1)S(1)}, u32[]{:S(2)}, u32[]{:S(2)}) collective-permute-start(bf16[1024,256]{1,0:T(8,128)(2,1)S(1)} %join_blocks.3.refs_4_.refs_0_), channel_id=1, source_target_pairs={{0,32},{4,36},{8,40},{12,44},{16,48},{20,52},{24,56},{28,60},{32,6... | collective-permute-start | bytes 1572872 | tf_op jit(solution)/shard_map/ppermute | solution.py:519
  42.8 35.3 %collective-permute-start.11 = (bf16[1024,256]{1,0:T(8,128)(2,1)S(1)}, bf16[1024,256]{1,0:T(8,128)(2,1)S(1)}, u32[]{:S(2)}, u32[]{:S(2)}) collective-permute-start(bf16[1024,256]{1,0:T(8,128)(2,1)S(1)} %join_blocks.3.refs_4_.refs_0_), channel_id=1, source_target_pairs={{0,64},{4,68},{8,72},{12,76},{16,80},{20,84},{24,88},{28,92},{32,9... | collective-permute-start | bytes 1572872 | tf_op jit(solution)/shard_map/ppermute | solution.py:519
  45.2 32.9 %collective-permute-start.12 = (bf16[1024,256]{1,0:T(8,128)(2,1)S(1)}, bf16[1024,256]{1,0:T(8,128)(2,1)S(1)}, u32[]{:S(2)}, u32[]{:S(2)}) collective-permute-start(bf16[1024,256]{1,0:T(8,128)(2,1)S(1)} %join_blocks.3.refs_4_.refs_0_), channel_id=1, source_target_pairs={{0,96},{4,100},{8,104},{12,108},{16,112},{20,116},{24,120},{28,124... | collective-permute-start | bytes 1572872 | tf_op jit(solution)/shard_map/ppermute | solution.py:519
  78.2 1.0 copy-start.1
  82.2 0.9 copy-start.2

commit v6 on v5

--- a/solution.py
+++ b/solution.py
@@ -264,8 +264,8 @@
 def window_body(
     offset_ref, x_ref, main_ref, rest_hbm, q_ref, acc_ref, seam_ref, gain_ref, wk_ref, wv_ref, wo_ref, *refs,
 ):
-    out_ref, kbd, vbd, vsm, ksm, mixed, packed, rest_ref, wkt_ref, kt_ref, vo_ref, at_row, done = refs[-13:]
-    blocks = refs[:-13]
+    out_ref, kbd, vbd, vsm, ones_w, ones_s, ksm, mixed, packed, rest_ref, wkt_ref, kt_ref, vo_ref, at_row, done = refs[-15:]
+    blocks = refs[:-15]
     rows = x_ref.shape[0]
     count = rows // WIN
     pairs = count // 2
@@ -294,17 +294,9 @@
             copy.wait()
             packed[LIMIT:, :] = rest_ref[...].astype(F32)
 
-        kbd[...] = jnp.zeros(kbd.shape, BF)
-        vsm[...] = jnp.zeros(vsm.shape, BF)
-        for half in range(2):
-            for k in range(HALF):
-                for w in range(count):
-                    vbd[w, half, k * WIN:k * WIN + WIN, 128:256] = jnp.broadcast_to(lanes_of(k), (WIN, 128))
-                h = half * HALF + k
-                for p in range(pairs):
-                    vsm[p, h * near:h * near + near, half * C + 128:half * C + C] = jnp.broadcast_to(
-                        lanes_of(k), (near, 128)
-                    )
+        for k in range(HALF):
+            ones_w[k * WIN:k * WIN + WIN, :] = jnp.broadcast_to(lanes_of(k), (WIN, 128))
+            ones_s[k * near:k * near + near, :] = jnp.broadcast_to(lanes_of(k), (near, 128))
 
     block = (lax.broadcasted_iota(jnp.int32, (64, 128), 0) // DIM) == (
         lax.broadcasted_iota(jnp.int32, (64, 128), 1) // WIN
@@ -336,13 +328,13 @@
                 for p in range(some_pairs):
                     pair = keys[lo:lo + 64, p * 128:p * 128 + 128]
                     turn = pltpu.roll(pair, WIN, 1)
-                    to = (half, slice(b * 64, b * 64 + 64), slice(b * 128, b * 128 + 128))
+                    to = (half, b)
                     w = w0 + 2 * p
                     kbd[(w,) + to] = jnp.where(block, jnp.where(first_lanes, pair, turn), 0.0).astype(BF)
                     kbd[(w + 1,) + to] = jnp.where(block, jnp.where(first_lanes, turn, pair), 0.0).astype(BF)
             for k in range(HALF):
                 for w in range(some):
-                    vbd[w0 + w, half, k * WIN:k * WIN + WIN, 0:128] = (
+                    vbd[w0 + w, half, k * WIN:k * WIN + WIN, :] = (
                         values[w * WIN:w * WIN + WIN, half * 128:half * 128 + 128] * lanes_of(k)
                     )
 
@@ -363,13 +355,26 @@
             ksm[p0 + p] = seam_kt[:, p * 128:p * 128 + 128]
             for h in range(HEADS):
                 half, k = h // HALF, h % HALF
-                vsm[p0 + p, h * near:h * near + near, half * C:half * C + 128] = (
+                vsm[p0 + p, half, k * near:k * near + near, :] = (
                     seam_v[p * near:p * near + near, half * 128:half * 128 + 128] * lanes_of(k)
                 )
 
+    gap = jnp.zeros((64, 128), BF)
+
+    def window_keys(w, half):
+        top = jnp.concatenate([kbd[w, half, 0], gap], axis=1)
+        return jnp.concatenate([top, jnp.concatenate([gap, kbd[w, half, 1]], axis=1)], axis=0)
+
+    def window_values(w, half):
+        return jnp.concatenate([vbd[w, half], ones_w[...]], axis=1)
+
+    def seam_values(p):
+        top = jnp.concatenate([vsm[p, 0], ones_s[...], gap, gap], axis=1)
+        return jnp.concatenate([top, jnp.concatenate([gap, gap, vsm[p, 1], ones_s[...]], axis=1)], axis=0)
+
     def window_scores(w, half):
         at = pl.ds(pl.multiple_of(w * WIN, WIN), WIN)
-        return dot(q_ref[at, half * 128:half * 128 + 128], kbd[w, half])
+        return dot(q_ref[at, half * 128:half * 128 + 128], window_keys(w, half))
 
     def seam_scores(p):
         return dot(q_ref[pl.ds(pl.multiple_of(p * 128, 128), 128), :], ksm[p])
@@ -386,10 +391,10 @@
         check = jnp.zeros((8, 128), F32)
         for p in range(some_pairs):
             lo = (piece * some_pairs + p) * 128
-            base = acc_ref[lo:lo + 128, :] + dot(weights_s[p], vsm[piece * some_pairs + p])
+            base = acc_ref[lo:lo + 128, :] + dot(weights_s[p], seam_values(piece * some_pairs + p))
             for half in range(2):
                 total = base[:, half * C:half * C + C] + jnp.concatenate(
-                    [dot(weights_w[2 * p + w][half], vbd[piece * some + 2 * p + w, half]) for w in range(2)], axis=0
+                    [dot(weights_w[2 * p + w][half], window_values(piece * some + 2 * p + w, half)) for w in range(2)], axis=0
                 )
                 den = total[:, 128:256]
                 inverse = 1.0 / den
@@ -443,10 +448,10 @@
                     )
                 weights = exp2(scores_w - tops_w).astype(BF)
                 totals.append(total + jnp.concatenate(
-                    [dot(weights[w * WIN:w * WIN + WIN], vbd[2 * p + w, half]) for w in range(2)], axis=0
+                    [dot(weights[w * WIN:w * WIN + WIN], window_values(2 * p + w, half)) for w in range(2)], axis=0
                 ))
             weights = jnp.where(own, exp2(jnp.where(own, scores_s - tops_s, NEG)), 0.0).astype(BF)
-            total = jnp.concatenate(totals, axis=1) + dot(weights, vsm[p])
+            total = jnp.concatenate(totals, axis=1) + dot(weights, seam_values(p))
             again = jnp.concatenate(
                 [total[:, half * C:half * C + 128] / total[:, half * C + 128:half * C + C] for half in range(2)], axis=1
             ).astype(BF)
@@ -481,9 +486,11 @@
             + [pl.BlockSpec(b.shape, fixed) for b in blocks],
             out_specs=pl.BlockSpec((rows, C), row),
             scratch_shapes=[
-                pltpu.VMEM((count, 2, 128, C), BF),
-                pltpu.VMEM((count, 2, HALF * WIN, C), BF),
-                pltpu.VMEM((count // 2, 128, 2 * C), BF),
+                pltpu.VMEM((count, 2, 2, 64, 128), BF),
+                pltpu.VMEM((count, 2, HALF * WIN, 128), BF),
+                pltpu.VMEM((count // 2, 2, 64, 128), BF),
+                pltpu.VMEM((HALF * WIN, 128), BF),
+                pltpu.VMEM((64, 128), BF),
                 pltpu.VMEM((count // 2, C, 128), BF),
                 pltpu.VMEM((rows, C), BF),
                 pltpu.VMEM((pixels, C), F32),

time: 213 us -> 212 us (level)
  transfers between devices with their start and end apart: 12 -> 12, of which waited for: 1 -> 1; matrix products, arithmetic and copies ran while one was open for 0% -> 0% of each run, Pallas kernels for 28% -> 29%
where the time goes in v6:
time: 212 us; the launch traced here: 211 us
  Pallas kernels  186 us (88%)
  starting transfers between devices  19.1 us (9%)
  local copies, waits for them, and re-layouts  3.46 us (2%)
    pallas_call x1, Pallas kernels, window(): pl.pallas_call(window_body, grid_spec=pltpu.PrefetchScalarGridSpec(num_sc...  126 us
    pallas_call x2, Pallas kernels, coarse(): pl.pallas_call(functools.partial(coarse_body, len(blocks)), grid=(steps,)...  44.4 us
    ppermute x7, starting transfers between devices, turned(): return [block] + [lax.ppermute(block, 'face', rotation(*s)) for s in steps]  13 us
    pallas_call x1, Pallas kernels, pack(): pl.pallas_call(pack_body, grid_spec=pltpu.PrefetchScalarGridSpec(num_scal...  6.94 us
    pallas_call x1, Pallas kernels, pool_rows(): pl.pallas_call(pool_body, grid=(pixels // rows,), in_specs=[pl.BlockSpec(...  5.85 us
  transfers between devices with their start and end apart: 12, of which 1 were waited for; matrix products, arithmetic and copies ran while one was open for 0% of the time, Pallas kernels for 29%

profile of v6, /device:TPU:1, one launch (start us, length us, event | category | flops | bytes accessed | tf_op | source)
XLA Modules:
  0.0 211.2 jit_solution(18082890254988600308)
XLA Ops:
  0.0 0.0 copy-start.4
  0.0 2.1 %collective-permute-start.1 = (s32[128]{0:T(128)}, s32[128]{0:T(128)S(1)}, u32[]{:S(2)}, u32[]{:S(2)}) collective-permute-start(s32[128]{0:T(128)} %offset_ref.1), channel_id=1, source_target_pairs={{0,4},{4,0},{8,12},{12,8},{16,20},{20,16},{24,28},{28,24},{32,36},... | collective-permute-start | bytes 1544 | tf_op jit(solution)/shard_map/ppermute | solution.py:522
  2.1 5.8 %norm_pool.1.refs_0_ = bf16[128,256]{1,0:T(8,128)(2,1)} custom-call(bf16[8192,256]{1,0:T(8,128)(2,1)} %x_ref.9, f32[1,256]{1,0:T(1,128)} %bitcast.2), custom_call_target="tpu_custom_call" | custom-call | flops 1073741824 | bytes 8388608 | tf_op jit(solution)/shard_map/norm_pool/pallas_call | solution.py:66
  8.0 0.0 copy-start.3
  8.0 0.0 collective-permute-done.1.offset_ref
  8.0 0.0 copy-start.5
  8.0 0.1 collective-permute-start.6
  8.1 3.0 %collective-permute-start.7 = (bf16[128,256]{1,0:T(8,128)(2,1)}, bf16[128,256]{1,0:T(8,128)(2,1)S(1)}, u32[]{:S(2)}, u32[]{:S(2)}) collective-permute-start(bf16[128,256]{1,0:T(8,128)(2,1)} %norm_pool.1.refs_0_), channel_id=1, source_target_pairs={{0,8},{4,12},{8,0},{12,4},{16,24},{20,28},{24,16},{28,20},{32,40},... | collective-permute-start | bytes 196616 | tf_op jit(solution)/shard_map/ppermute | solution.py:526
  11.1 1.6 collective-permute-start.8
  12.7 1.8 collective-permute-start.3
  14.5 1.6 collective-permute-start.4
  16.2 0.0 collective-permute-done.6.refs_1_
  16.2 0.4 collective-permute-start.5
  16.6 0.0 copy-done.4
  16.7 0.1 copy.10
  16.8 0.2 reshape.8.index_ref
  16.9 0.0 copy-done.5
  17.0 6.9 %pack_rows.1 = (bf16[5360,256]{1,0:T(8,128)(2,1)}, bf16[2832,256]{1,0:T(8,128)(2,1)}, s32[1]{0:T(128)}) custom-call(s32[128]{0:T(128)} %copy-done.5, s32[128]{0:T(128)} %offset_ref.1, bf16[8192,256]{1,0:T(8,128)(2,1)} %x_ref.9), custom_call_target="tpu_custom_call" | custom-call | bytes 20971520 | tf_op jit(solution)/shard_map/pack_rows/pallas_call | solution.py:111
  23.9 0.0 collective-permute-done.7.refs_2_
  23.9 0.1 collective-permute-start.2
  24.0 0.0 collective-permute-done.8.refs_3_
  24.0 0.0 copy-done.3
  24.1 3.4 %collective-permute-start.9 = (bf16[512,256]{1,0:T(8,128)(2,1)S(1)}, bf16[512,256]{1,0:T(8,128)(2,1)S(1)}, u32[]{:S(2)}, u32[]{:S(2)}) collective-permute-start(bf16[512,256]{1,0:T(8,128)(2,1)S(1)} %join_blocks.2.refs_0_), channel_id=1, source_target_pairs={{0,16},{4,20},{8,24},{12,28},{16,0},{20,4},{24,8},{28,12},{32,48},... | collective-permute-start | bytes 786440 | tf_op jit(solution)/shard_map/ppermute | solution.py:526
  27.4 0.0 collective-permute-done.3.refs_1_
  27.4 0.0 copy-start.6
  27.4 0.0 collective-permute-done.4.refs_2_
  27.5 0.0 copy-start.7
  27.5 0.0 collective-permute-done.5.refs_3_
  27.5 0.6 copy-done.6
  28.1 0.0 copy-done.7
  28.1 0.0 copy-start.8
  28.1 0.6 copy-done.8
  28.7 12.7 %group_attention.2 = (bf16[8192,256]{1,0:T(8,128)(2,1)}, f32[8192,512]{1,0:T(8,128)}) custom-call(bf16[8192,256]{1,0:T(8,128)(2,1)} %x_ref.9, bf16[8192,256]{1,0:T(8,128)(2,1)} %x_ref.9, f32[1,256]{1,0:T(1,128)} %bitcast.3, bf16[256,768]{1,0:T(8,128)(2,1)} %wv_ref.5, bf16[256,768]{1,0:T(8,128)(2,1)} %wv_ref.5, bf16[256,768]{1,0:T(8,128)(2,1)} %wv_ref.5, ...), custom_call_target="tpu_custom_call" | custom-call | flops 8589934592 | bytes 5242880 | tf_op jit(solution)/shard_map/group_attention/pallas_call | solution.py:205
  41.4 0.0 collective-permute-done.9.refs_1_
  41.5 0.0 copy-start
  41.5 1.3 collective-permute-start.10
  42.8 2.4 %collective-permute-start.11 = (bf16[1024,256]{1,0:T(8,128)(2,1)S(1)}, bf16[1024,256]{1,0:T(8,128)(2,1)S(1)}, u32[]{:S(2)}, u32[]{:S(2)}) collective-permute-start(bf16[1024,256]{1,0:T(8,128)(2,1)S(1)} %join_blocks.3.refs_4_.refs_0_), channel_id=1, source_target_pairs={{0,64},{4,68},{8,72},{12,76},{16,80},{20,84},{24,88},{28,92},{32,9... | collective-permute-start | bytes 1572872 | tf_op jit(solution)/shard_map/ppermute | solution.py:526
  45.2 1.2 collective-permute-start.12
  46.4 0.0 copy-done
  46.4 31.7 %group_attention.3 = (bf16[8192,256]{1,0:T(8,128)(2,1)}, f32[8192,512]{1,0:T(8,128)}) custom-call(bf16[8192,256]{1,0:T(8,128)(2,1)} %x_ref.9, bf16[8192,256]{1,0:T(8,128)(2,1)} %x_ref.9, f32[1,256]{1,0:T(1,128)} %bitcast.5, bf16[256,768]{1,0:T(8,128)(2,1)} %wv_ref.5, bf16[256,768]{1,0:T(8,128)(2,1)} %wv_ref.5, ...), custom_call_target="tpu_custom_call", output_to_operand_aliasing={{0}: (11, {}), {1}: (12, {})} | custom-call | flops 25769803776 | bytes 15728640 | tf_op jit(solution)/shard_map/group_attention/pallas_call | solution.py:205
  78.1 0.0 collective-permute-done.10.refs_1_
  78.1 0.0 collective-permute-done.11.refs_2_
  78.1 0.0 collective-permute-done.12.refs_3_
  78.2 0.0 copy-start.1
  78.2 1.0 copy-done.1
  79.2 3.0 %seam_rows.1.seam_ref = bf16[1024,256]{1,0:T(8,128)(2,1)S(1)} custom-call(s32[1024,1]{1,0:T(8,128)S(1)} %reshape.8.index_ref, bf16[1024,256]{1,0:T(8,128)(2,1)S(1)} %copy-done.1, bf16[1024,256]{1,0:T(8,128)(2,1)S(1)} %collective-permute-done.10.refs_1_, bf16[1024,256]{1,0:T(8,128)(2,1)S(1)} %collective-permute-done.11.refs_2_, ...), custom_call_target="tpu_custom_call" | custom-call | tf_op jit(solution)/shard_map/seam_rows/pallas_call | solution.py:252
  82.2 0.0 copy-start.2
  82.2 0.8 copy-done.2
  83.1 0.8 while.10
  83.9 1.5 collective-permute-done.2.main_ref
  85.5 125.6 %window_attention.1 = bf16[8192,256]{1,0:T(8,128)(2,1)} custom-call(s32[128]{0:T(128)} %offset_ref.1, bf16[8192,256]{1,0:T(8,128)(2,1)} %x_ref.9, bf16[5360,256]{1,0:T(8,128)(2,1)} %collective-permute-done.2.main_ref, bf16[2832,256]{1,0:T(8,128)(2,1)} %get-tuple-element.30.rest_hbm, bf16[8192,256]{1,0:T(8,128)(2,1)} %get-tuple-element.34.q_ref, ...), custom_call_target="tpu_custom_call" | custom-call | flops 21474836480 | bytes 41943040 | tf_op jit(solution)/shard_map/window_attention/pallas_call | solution.py:469
  (3 shorter events, 0.1 us)
Async XLA Ops:
  0.0 16.6 %copy-start.4 = (s32[128,8]{0,1:T(8,128)S(1)}, s32[128,8]{0,1:T(8,128)}, u32[]{:S(2)}) copy-start(s32[128,8]{0,1:T(8,128)} %param.13) | copy-start | bytes 12292
  0.0 8.0 %collective-permute-start.1 = (s32[128]{0:T(128)}, s32[128]{0:T(128)S(1)}, u32[]{:S(2)}, u32[]{:S(2)}) collective-permute-start(s32[128]{0:T(128)} %offset_ref.1), channel_id=1, source_target_pairs={{0,4},{4,0},{8,12},{12,8},{16,20},{20,16},{24,28},{28,24},{32,36},... | collective-permute-start | bytes 1544 | tf_op jit(solution)/shard_map/ppermute | solution.py:522
  8.0 16.0 %copy-start.3 = (bf16[128,256]{1,0:T(8,128)(2,1)S(1)}, bf16[128,256]{1,0:T(8,128)(2,1)}, u32[]{:S(2)}) copy-start(bf16[128,256]{1,0:T(8,128)(2,1)} %norm_pool.1.refs_0_) | copy-start | bytes 196612
  8.0 9.0 %copy-start.5 = (s32[128]{0:T(128)}, s32[128]{0:T(128)S(1)}, u32[]{:S(2)}) copy-start(s32[128]{0:T(128)S(1)} %collective-permute-done.1.offset_ref) | copy-start | bytes 1540
  8.0 8.2 %collective-permute-start.6 = (bf16[128,256]{1,0:T(8,128)(2,1)}, bf16[128,256]{1,0:T(8,128)(2,1)S(1)}, u32[]{:S(2)}, u32[]{:S(2)}) collective-permute-start(bf16[128,256]{1,0:T(8,128)(2,1)} %norm_pool.1.refs_0_), channel_id=1, source_target_pairs={{0,4},{4,8},{8,12},{12,0},{16,20},{20,24},{24,28},{28,16},{32,36},... | collective-permute-start | bytes 196616 | tf_op jit(solution)/shard_map/ppermute | solution.py:526
  8.1 15.8 %collective-permute-start.7 = (bf16[128,256]{1,0:T(8,128)(2,1)}, bf16[128,256]{1,0:T(8,128)(2,1)S(1)}, u32[]{:S(2)}, u32[]{:S(2)}) collective-permute-start(bf16[128,256]{1,0:T(8,128)(2,1)} %norm_pool.1.refs_0_), channel_id=1, source_target_pairs={{0,8},{4,12},{8,0},{12,4},{16,24},{20,28},{24,16},{28,20},{32,40},... | collective-permute-start | bytes 196616 | tf_op jit(solution)/shard_map/ppermute | solution.py:526
  11.1 12.9 %collective-permute-start.8 = (bf16[128,256]{1,0:T(8,128)(2,1)}, bf16[128,256]{1,0:T(8,128)(2,1)S(1)}, u32[]{:S(2)}, u32[]{:S(2)}) collective-permute-start(bf16[128,256]{1,0:T(8,128)(2,1)} %norm_pool.1.refs_0_), channel_id=1, source_target_pairs={{0,12},{4,0},{8,4},{12,8},{16,28},{20,16},{24,20},{28,24},{32,44},... | collective-permute-start | bytes 196616 | tf_op jit(solution)/shard_map/ppermute | solution.py:526
  12.7 14.7 %collective-permute-start.3 = (bf16[128,256]{1,0:T(8,128)(2,1)}, bf16[128,256]{1,0:T(8,128)(2,1)S(1)}, u32[]{:S(2)}, u32[]{:S(2)}) collective-permute-start(bf16[128,256]{1,0:T(8,128)(2,1)} %norm_pool.1.refs_0_), channel_id=1, source_target_pairs={{0,1},{1,0},{2,3},{3,2},{4,5},{5,4},{6,7},{7,6},{8,9},{9,8},{10,11... | collective-permute-start | bytes 196616 | tf_op jit(solution)/shard_map/ppermute | solution.py:539
  14.5 12.9 %collective-permute-start.4 = (bf16[128,256]{1,0:T(8,128)(2,1)}, bf16[128,256]{1,0:T(8,128)(2,1)S(1)}, u32[]{:S(2)}, u32[]{:S(2)}) collective-permute-start(bf16[128,256]{1,0:T(8,128)(2,1)} %norm_pool.1.refs_0_), channel_id=1, source_target_pairs={{0,2},{1,3},{2,0},{3,1},{4,6},{5,7},{6,4},{7,5},{8,10},{9,11},{10,... | collective-permute-start | bytes 196616 | tf_op jit(solution)/shard_map/ppermute | solution.py:539
  16.2 11.3 %collective-permute-start.5 = (bf16[128,256]{1,0:T(8,128)(2,1)}, bf16[128,256]{1,0:T(8,128)(2,1)S(1)}, u32[]{:S(2)}, u32[]{:S(2)}) collective-permute-start(bf16[128,256]{1,0:T(8,128)(2,1)} %norm_pool.1.refs_0_), channel_id=1, source_target_pairs={{0,3},{1,2},{2,1},{3,0},{4,7},{5,6},{6,5},{7,4},{8,11},{9,10},{10,... | collective-permute-start | bytes 196616 | tf_op jit(solution)/shard_map/ppermute | solution.py:539
  23.9 61.5 %collective-permute-start.2 = (bf16[5360,256]{1,0:T(8,128)(2,1)}, bf16[5360,256]{1,0:T(8,128)(2,1)}, u32[]{:S(2)}, u32[]{:S(2)}) collective-permute-start(bf16[5360,256]{1,0:T(8,128)(2,1)} %get-tuple-element.27), channel_id=1, source_target_pairs={{0,4},{4,0},{8,12},{12,8},{16,20},{20,16},{24,28},{28,24},{32,36},... | collective-permute-start | bytes 8232968 | tf_op jit(solution)/shard_map/ppermute | solution.py:522
  24.1 17.4 %collective-permute-start.9 = (bf16[512,256]{1,0:T(8,128)(2,1)S(1)}, bf16[512,256]{1,0:T(8,128)(2,1)S(1)}, u32[]{:S(2)}, u32[]{:S(2)}) collective-permute-start(bf16[512,256]{1,0:T(8,128)(2,1)S(1)} %join_blocks.2.refs_0_), channel_id=1, source_target_pairs={{0,16},{4,20},{8,24},{12,28},{16,0},{20,4},{24,8},{28,12},{32,48},... | collective-permute-start | bytes 786440 | tf_op jit(solution)/shard_map/ppermute | solution.py:526
  27.4 0.6 copy-start.6
  27.5 0.6 copy-start.7
  28.1 0.6 copy-start.8
  41.5 4.9 %copy-start = (bf16[1024,256]{1,0:T(8,128)(2,1)}, bf16[1024,256]{1,0:T(8,128)(2,1)S(1)}, u32[]{:S(2)}) copy-start(bf16[1024,256]{1,0:T(8,128)(2,1)S(1)} %join_blocks.3.refs_4_.refs_0_) | copy-start | bytes 1572868
  41.5 36.6 %collective-permute-start.10 = (bf16[1024,256]{1,0:T(8,128)(2,1)S(1)}, bf16[1024,256]{1,0:T(8,128)(2,1)S(1)}, u32[]{:S(2)}, u32[]{:S(2)}) collective-permute-start(bf16[1024,256]{1,0:T(8,128)(2,1)S(1)} %join_blocks.3.refs_4_.refs_0_), channel_id=1, source_target_pairs={{0,32},{4,36},{8,40},{12,44},{16,48},{20,52},{24,56},{28,60},{32,6... | collective-permute-start | bytes 1572872 | tf_op jit(solution)/shard_map/ppermute | solution.py:526
  42.8 35.3 %collective-permute-start.11 = (bf16[1024,256]{1,0:T(8,128)(2,1)S(1)}, bf16[1024,256]{1,0:T(8,128)(2,1)S(1)}, u32[]{:S(2)}, u32[]{:S(2)}) collective-permute-start(bf16[1024,256]{1,0:T(8,128)(2,1)S(1)} %join_blocks.3.refs_4_.refs_0_), channel_id=1, source_target_pairs={{0,64},{4,68},{8,72},{12,76},{16,80},{20,84},{24,88},{28,92},{32,9... | collective-permute-start | bytes 1572872 | tf_op jit(solution)/shard_map/ppermute | solution.py:526
  45.2 32.9 %collective-permute-start.12 = (bf16[1024,256]{1,0:T(8,128)(2,1)S(1)}, bf16[1024,256]{1,0:T(8,128)(2,1)S(1)}, u32[]{:S(2)}, u32[]{:S(2)}) collective-permute-start(bf16[1024,256]{1,0:T(8,128)(2,1)S(1)} %join_blocks.3.refs_4_.refs_0_), channel_id=1, source_target_pairs={{0,96},{4,100},{8,104},{12,108},{16,112},{20,116},{24,120},{28,124... | collective-permute-start | bytes 1572872 | tf_op jit(solution)/shard_map/ppermute | solution.py:526
  78.2 1.0 copy-start.1
  82.2 0.9 copy-start.2
